TPU v7x, 32 devices: a whole 2x2x4 slice. The times are simulated.
32 devices in a mesh: rep: 8 (over y, x, core), fsdp: 4 (over z).
Axes of the slice: x: 2, y: 2, z: 4, core: 2. Of those that a mesh axis runs over, the one named last changes fastest.
Arguments:
- tokens: bfloat16 [4096, 8192], P(('rep', 'fsdp')), may hold values from -6 to 6
- grad_out: bfloat16 [4096, 128], P(('rep', 'fsdp')), may hold values from -0.25 to 0.25
- moment: float32 [8, 8192, 128], P('rep', 'fsdp'), may hold values from -6 to 6
- weight: bfloat16 [8192, 128], P('fsdp'), may hold values from -0.0625 to 0.0625
- next_tokens: bfloat16 [4096, 8192], P(('rep', 'fsdp')), may hold values from -6 to 6
- index: int32 [8, 128, 2, 32], P('rep', 'fsdp'), may hold values from 0 to 4095, as said below
Outputs:
- update: float32 [8192, 128], P('fsdp')
- new_moment: float32 [8, 8192, 128], P('rep', 'fsdp')
- next_out: bfloat16 [4096, 128], P(('rep', 'fsdp'))
Inputs may be any that keep to these rules, and one draw needn't show every extreme that they name: `index`: for each replica and tile the 32 positions are distinct; position p stands for row p // 64 and column p % 64 of the tile.
All inputs are finite; a program needn't handle non-finite values.
Results may differ from a plain program's by a relative error of at most 0.008.
Values may be sent and summed in bfloat16 or wider, within the bound.
No kernel may reach another device: no remote copies, remote signals or barrier semaphores. Data moves between devices by JAX's collectives and lax.ppermute only.
A program may use at most 64 MiB of HBM per device.

v0:
```python
import jax
import jax.numpy as jnp
from jax import lax
from jax.sharding import PartitionSpec as P

TILE = 64


momentum_decay = 0.999
step_size = 0.005


def cosine_table(order):
    freq = jnp.arange(order, dtype=jnp.float32)[:, None]
    place = jnp.arange(order, dtype=jnp.float32)[None, :]
    table = jnp.sqrt(2.0 / order) * jnp.cos(jnp.pi * (2.0 * place + 1.0) * freq / (2.0 * order))
    return table * jnp.where(freq == 0.0, jnp.sqrt(0.5), 1.0)


def forward_tiles(field, table):
    side = table.shape[0]
    shard_rows, width = field.shape
    tiles = field.reshape(shard_rows // side, side, width)
    along = jnp.einsum("ab,ibc->iac", table, tiles, precision=lax.Precision.HIGHEST)
    block = jnp.kron(jnp.eye(width // side, dtype=jnp.float32), table.T)
    return jnp.matmul(along, block, precision=lax.Precision.HIGHEST)


def inverse_tiles(spectra, table):
    side = table.shape[0]
    width = spectra.shape[2]
    along = jnp.einsum("ab,iac->ibc", table, spectra, precision=lax.Precision.HIGHEST)
    block = jnp.kron(jnp.eye(width // side, dtype=jnp.float32), table)
    result = jnp.matmul(along, block, precision=lax.Precision.HIGHEST)
    return result.reshape(spectra.shape[0] * side, width)


def one_hots(places, side, width):
    row_of = places // side
    col_of = places % side + jnp.arange(width // side, dtype=jnp.int32)[:, None] * side
    row_hot = (row_of[..., None] == jnp.arange(side, dtype=jnp.int32)).astype(jnp.float32)
    col_hot = (col_of[..., None] == jnp.arange(width, dtype=jnp.int32)).astype(jnp.float32)
    return (row_hot, col_hot)


def select_values(spectra, row_hot, col_hot):
    picked = jnp.einsum("ijka,iac->ijkc", row_hot, spectra, precision=lax.Precision.HIGHEST)
    return jnp.sum(picked * col_hot, axis=-1)


def densify(sent_values, row_hot, col_hot):
    return jnp.einsum(
        "ijka,ijkc->iac", row_hot * sent_values[..., None], col_hot, precision=lax.Precision.HIGHEST
    )


def local(tokens, grad_out, moment, weight, next_tokens, index):
    table = cosine_table(TILE)
    width = weight.shape[1]
    columns = tokens
    grad = lax.psum_scatter(
        lax.dot_general(
            columns, grad_out, (((0,), (0,)), ((), ())), preferred_element_type=jnp.float32
        ).astype(jnp.bfloat16),
        "fsdp",
        scatter_dimension=0,
        tiled=True,
    ).astype(jnp.float32)
    moment_now = momentum_decay * moment[0] + grad
    spectra = forward_tiles(moment_now, table)
    row_hot, col_hot = one_hots(index[0], TILE, width)
    sent_values = select_values(spectra, row_hot, col_hot)
    dense = densify(sent_values, row_hot, col_hot)
    new_moment = (moment_now - inverse_tiles(dense, table))[None]
    total = lax.psum(dense.astype(jnp.bfloat16), "rep").astype(jnp.float32)
    update = inverse_tiles(total, table)
    new_weight = (weight.astype(jnp.float32) - step_size * update).astype(jnp.bfloat16)
    columns = next_tokens
    summed = jnp.dot(
        columns,
        lax.all_gather(new_weight, "fsdp", axis=0, tiled=True),
        preferred_element_type=jnp.float32,
    )
    next_out = summed.astype(jnp.bfloat16)
    return (update, new_moment, next_out)


def solution(mesh):
    in_specs = (
        P(("rep", "fsdp"), None),
        P(("rep", "fsdp"), None),
        P("rep", "fsdp", None),
        P("fsdp", None),
        P(("rep", "fsdp"), None),
        P("rep", "fsdp", None, None),
    )
    out_specs = (P("fsdp", None), P("rep", "fsdp", None), P(("rep", "fsdp"), None))
    return jax.shard_map(local, mesh=mesh, in_specs=in_specs, out_specs=out_specs, check_vma=False)
```

profile of v0, /device:TPU:0, one launch (start us, length us, event | category | flops | bytes accessed | tf_op | source)
XLA Modules:
  0.0 186.0 jit_solution(15629691601027459983)
XLA Ops:
  7.2 0.0 copy-start
  7.2 0.0 reduce-scatter.2.cloned.1.call-start
  7.2 1.5 copy-done
  8.8 2.9 %convolution_convert_fusion = bf16[8192,128]{1,0:T(8,128)(2,1)} fusion(bf16[128,8192]{1,0:T(8,128)(2,1)S(1)} %copy-done, bf16[128,128]{1,0:T(8,128)(2,1)} %param.7), kind=kOutput, calls=%fused_computation | convolution fusion | flops 269484032 | bytes 4227072 | tf_op jit(solution)/shard_map/dot_general | solution.py:62
  11.6 0.0 copy-start.1
  11.6 0.0 reduce-scatter.2.cloned.1.call-update
  11.6 0.0 all-reduce.2.cloned.1.call-start
  11.7 0.3 cosine_multiply_fusion.1
  12.0 0.1 copy.10
  12.1 0.1 copy.9
  12.2 0.1 broadcast_multiply_fusion
  12.3 0.1 reshape.186
  12.5 0.0 copy-done.1
  12.5 0.1 and_select_fusion.1
  12.6 45.8 %reduce-scatter.2.cloned.1.call-done = bf16[2048,128]{1,0:T(8,128)(2,1)} async-done(((bf16[8192,128]{1,0:T(8,128)(2,1)}), bf16[2048,128]{1,0:T(8,128)(2,1)}) %reduce-scatter.2.cloned.1.call-update) | async-done | bytes 524304 | tf_op jit(solution)/shard_map/reduce_scatter | solution.py:61
  58.4 1.5 bitcast_add_fusion
  59.9 3.5 %fusion.19 = f32[32,128,64]{2,1,0:T(8,128)S(1)} fusion(f32[32,64,128]{2,1,0:T(8,128)S(1)} %bitcast.65, f32[64]{0:T(128)S(1)} %get-tuple-element.16, f32[64]{0:T(128)S(1)} %get-tuple-element.17), kind=kOutput, calls=%fused_computation.33 | convolution fusion | flops 201338880 | bytes 2097664 | tf_op jit(solution)/shard_map/ab,ibc->iac/dot_general | solution.py:24
  63.3 3.4 %fusion.3 = f32[32,64,128,1]{2,1,3,0:T(8,128)S(1)} fusion(f32[128,128,1]{1,0,2:T(8,128)S(1)} %reshape.186, f32[32,128,64]{2,1,0:T(8,128)S(1)} %fusion.19), kind=kOutput, calls=%fused_computation.6 | convolution fusion | flops 402653184 | bytes 2162688 | tf_op jit(solution)/shard_map/dot_general | solution.py:26
  66.8 1.3 fusion.6
  68.1 3.3 %fusion.35 = (bf16[32,64,128]{2,1,0:T(8,128)(2,1)}, f32[32,64,128]{2,1,0:T(8,128)}) fusion(s32[32,2,32]{2,1,0:T(2,128)S(1)} %get-tuple-element.7, f32[32,2,32]{2,1,0:T(2,128)S(1)} %fusion.6, s32[32,2,32]{2,1,0:T(2,128)S(1)} %get-tuple-element.6), kind=kOutput, calls=%fused_computation.58 | convolution fusion | flops 202113024 | bytes 1597440 | tf_op jit(solution)/shard_map/ijka,ijkc->iac/dot_general | solution.py:52
  71.4 0.0 all-reduce.2.cloned.1.call-update
  71.4 0.2 all-gather.2.cloned.1.call-start
  71.6 0.1 mul.277
  71.8 53.7 %all-reduce.2.cloned.1.call-done = bf16[32,64,128]{2,1,0:T(8,128)(2,1)} async-done(((bf16[32,64,128]{2,1,0:T(8,128)(2,1)}), bf16[32,64,128]{2,1,0:T(8,128)(2,1)}) %all-reduce.2.cloned.1.call-update) | async-done | bytes 524304 | tf_op jit(solution)/shard_map/psum | solution.py:75
  125.4 1.8 fusion.17
  127.2 3.2 %subtract_convert_fusion = (bf16[2048,128]{1,0:T(8,128)(2,1)}, f32[2048,128]{1,0:T(8,128)}) fusion(bf16[2048,128]{1,0:T(8,128)(2,1)} %param.9, f32[2048,128]{1,0:T(8,128)S(1)} %bitcast.66, f32[128,128]{1,0:T(8,128)S(1)} %mul.277), kind=kOutput, calls=%fused_computation.12 | convolution fusion | flops 403701760 | bytes 3211264 | tf_op jit(solution)/shard_map/dot_general | solution.py:34
  130.4 0.0 all-gather.2.cloned.1.call-update
  130.4 2.5 %fusion.15 = f32[32,128,64]{1,2,0:T(8,128)S(1)} fusion(f32[32,64,128]{2,1,0:T(8,128)} %get-tuple-element.13, f32[64]{0:T(128)S(1)} %get-tuple-element.16, f32[64]{0:T(128)S(1)} %get-tuple-element.17), kind=kOutput, calls=%fused_computation.29 | convolution fusion | flops 201338880 | bytes 2097664 | tf_op jit(solution)/shard_map/ab,iac->ibc/dot_general | solution.py:32
  132.9 1.9 %fusion = f32[1,2048,128]{2,1,0:T(8,128)} fusion(f32[2048,128]{1,0:T(8,128)S(1)} %bitcast_add_fusion, f32[2048,128]{1,0:T(8,128)S(1)} %bitcast.67, f32[128,128]{1,0:T(8,128)S(1)} %mul.277), kind=kOutput, calls=%fused_computation.2 | convolution fusion | flops 402915328 | bytes 3211264 | tf_op jit(solution)/shard_map/dot_general | solution.py:34
  134.9 41.0 %all-gather.2.cloned.1.call-done = bf16[8192,128]{1,0:T(8,128)(2,1)} async-done(((bf16[2048,128]{1,0:T(8,128)(2,1)}), bf16[8192,128]{1,0:T(8,128)(2,1)}) %all-gather.2.cloned.1.call-update) | async-done | bytes 2097168 | tf_op jit(solution)/shard_map/all_gather | solution.py:81
  175.8 3.0 %fusion.7 = bf16[128,128]{0,1:T(8,128)(2,1)S(1)} fusion(bf16[8192,128]{1,0:T(8,128)(2,1)} %all-gather.2.cloned.1.call-done, bf16[128,8192]{1,0:T(8,128)(2,1)} %param.10), kind=kOutput, calls=%fused_computation.10 | convolution fusion | flops 268451840 | bytes 4227072 | tf_op jit(solution)/shard_map/dot_general | solution.py:79
  178.8 0.7 copy.11
  (3 shorter events, 0.0 us)
Async XLA Ops:
  7.2 1.6 copy-start
  7.2 51.2 %reduce-scatter.2.cloned.1.call-start = ((), (), s32[]{:S(2)}) async-start(), calls=%async_computation.1 | async-start | bytes 2621440 | tf_op jit(solution)/shard_map/reduce_scatter | solution.py:61
  11.6 0.9 copy-start.1
  11.6 113.8 %all-reduce.2.cloned.1.call-start = ((), (), s32[]{:S(2)}) async-start(), calls=%async_computation.2 | async-start | bytes 1048576 | tf_op jit(solution)/shard_map/psum | solution.py:75
  71.4 104.4 %all-gather.2.cloned.1.call-start = ((), (), s32[]{:S(2)}) async-start(), calls=%async_computation.3 | async-start | bytes 2621440 | tf_op jit(solution)/shard_map/all_gather | solution.py:81
Sparse Core Ops, SparseCore 0:
  11.8 46.5 reduce-scatter.1
  71.5 53.8 all-reduce.1
  130.5 45.2 all-gather.1
where the time goes:
time: 186 us
  waiting for transfers between devices  140 us (75%)
  matrix products  26.7 us (14%)
  between operations  13.8 us (7%)
  local copies, waits for them, and re-layouts  2.68 us (1%)
  other arithmetic  2.08 us (1%)
    psum x1, waiting for transfers between devices, local(): total = lax.psum(dense.astype(jnp.bfloat16), 'rep').astype(jnp.float32)  53.7 us
    reduce_scatter x1, waiting for transfers between devices, local(): lax.psum_scatter(lax.dot_general(columns, grad_out, (((0,), (0,)), ((), (...  45.8 us
    all_gather x1, waiting for transfers between devices, local(): lax.all_gather(new_weight, 'fsdp', axis=0, tiled=True)  41 us
    dot_general x2, matrix products, inverse_tiles(): result = jnp.matmul(along, block, precision=lax.Precision.HIGHEST)  5.11 us
    dot_general x2, matrix products, inverse_tiles(): jnp.einsum('ab,iac->ibc', table, spectra, precision=lax.Precision.HIGHEST)  4.27 us
  transfers between devices with their start and end apart: 3, of which 3 were waited for; matrix products, arithmetic and copies ran while one was open for 3% of the time, Pallas kernels for 0%

commit v1 on v0

v1 whole, which is shorter than its diff:
```python
import functools

import jax
import jax.numpy as jnp
import numpy as np
from jax import lax
from jax.experimental import pallas as pl
from jax.experimental.pallas import tpu as pltpu
from jax.sharding import PartitionSpec as P

TILE = 64
LANES = 128

momentum_decay = 0.999
step_size = 0.005


def cosine_array(order):
    freq = np.arange(order, dtype=np.float64)[:, None]
    place = np.arange(order, dtype=np.float64)[None, :]
    table = np.sqrt(2.0 / order) * np.cos(np.pi * (2.0 * place + 1.0) * freq / (2.0 * order))
    return table * np.where(freq == 0.0, np.sqrt(0.5), 1.0)


def tables():
    block = np.kron(np.eye(2), cosine_array(TILE)).astype(np.float32)
    high = block.astype(jnp.bfloat16)
    low = (block - high.astype(np.float32)).astype(jnp.bfloat16)
    inv = np.concatenate([high.T, low.T], axis=0)
    fwd = np.concatenate([high, low], axis=0)
    return jnp.asarray(inv), jnp.asarray(fwd)


def split(x):
    high = x.astype(jnp.bfloat16)
    return high, (x - high.astype(jnp.float32)).astype(jnp.bfloat16)


def dot(a, b, contract=((1,), (0,))):
    return lax.dot_general(a, b, (contract, ((), ())), preferred_element_type=jnp.float32)


def hot(row, fill):
    return jnp.where(lax.broadcasted_iota(jnp.int32, (LANES, LANES), 0) == row, fill, 0.0)


def partial_kernel(slots, tok, grad, *outs):
    for i, out in enumerate(outs):

        @pl.when(pl.program_id(0) == i)
        def _():
            out[...] = dot(tok[...], grad[...], ((0,), (0,))).astype(out.dtype)


def partial_chunks(tokens, grad_out, slots, rows):
    count = slots.shape[0]
    width = grad_out.shape[1]
    toks = tokens.shape[0]
    return pl.pallas_call(
        partial_kernel,
        grid_spec=pltpu.PrefetchScalarGridSpec(
            num_scalar_prefetch=1,
            grid=(count,),
            in_specs=[
                pl.BlockSpec((toks, rows), lambda s, slots: (0, slots[s])),
                pl.BlockSpec((toks, width), lambda s, slots: (0, 0)),
            ],
            out_specs=[pl.BlockSpec((rows, width), lambda s, slots: (0, 0)) for _ in range(count)],
        ),
        out_shape=[jax.ShapeDtypeStruct((rows, width), jnp.bfloat16) for _ in range(count)],
        cost_estimate=pl.CostEstimate(
            flops=2 * count * rows * width * toks, bytes_accessed=count * rows * (width + toks) * 2, transcendentals=0
        ),
        compiler_params=pltpu.CompilerParams(vmem_limit_bytes=32 * 2**20),
    )(slots, tokens, grad_out)


def entry_rows(inv, row, col):
    hots = jnp.concatenate([hot(row, 1.0), hot(col, 1.0)], axis=1).astype(jnp.bfloat16)
    both = dot(inv, hots)
    return both[:LANES, :LANES], both[LANES:, :LANES], both[:LANES, LANES:], both[LANES:, LANES:]


def select_kernel(groups, me, inv_ref, idx_ref, tok_ref, grad_ref, moment_ref, out_ref):
    inv = inv_ref[...]
    grad = grad_ref[...]

    def group(g, own):
        row = idx_ref[0, 0, pl.ds(g, 1), :]
        col = idx_ref[0, 1, pl.ds(g, 1), :]
        a_hi, a_lo, b_hi, b_lo = entry_rows(inv, row, col)
        a2 = jnp.concatenate([a_hi, a_lo], axis=1).astype(jnp.bfloat16)
        b2 = jnp.concatenate([b_hi, b_lo], axis=1).astype(jnp.bfloat16)
        tok = tok_ref[:, pl.ds(pl.multiple_of(g * LANES, LANES), LANES)]
        ta = dot(tok, a2)
        gb = dot(grad, b2)
        value = jnp.sum((ta[:, :LANES] + ta[:, LANES:]) * (gb[:, :LANES] + gb[:, LANES:]), axis=0, keepdims=True)
        if own:
            m_hi, m_lo = split(momentum_decay * moment_ref[pl.ds(pl.multiple_of(g * LANES, LANES), LANES), :])
            mb = dot(m_hi, b2)
            mb = mb[:, :LANES] + mb[:, LANES:] + dot(m_lo, b2[:, :LANES])
            value = value + jnp.sum(mb * (a_hi + a_lo), axis=0, keepdims=True)
        out_ref[0, pl.ds(g, 1), :] = value

    @pl.when(pl.program_id(0) == 0)
    def _():
        for g in range(groups):
            group(g, True)

    @pl.when(pl.program_id(0) != 0)
    def _():
        for g in range(groups):
            group(g, False)


def select_values(me, inv, idx, tokens, grad_out, moment):
    n_f, _, groups, _ = idx.shape
    rows = groups * LANES
    toks = tokens.shape[0]
    width = grad_out.shape[1]
    return pl.pallas_call(
        functools.partial(select_kernel, groups),
        grid_spec=pltpu.PrefetchScalarGridSpec(
            num_scalar_prefetch=1,
            grid=(n_f,),
            in_specs=[
                pl.BlockSpec(inv.shape, lambda s, me: (0, 0)),
                pl.BlockSpec((1, 2, groups, LANES), lambda s, me: (s, 0, 0, 0)),
                pl.BlockSpec((toks, rows), lambda s, me: (0, me[0] ^ s)),
                pl.BlockSpec((toks, width), lambda s, me: (0, 0)),
                pl.BlockSpec((rows, width), lambda s, me: (0, 0)),
            ],
            out_specs=pl.BlockSpec((1, groups, LANES), lambda s, me: (me[0] ^ s, 0, 0)),
        ),
        out_shape=jax.ShapeDtypeStruct((n_f, groups, LANES), jnp.float32),
        cost_estimate=pl.CostEstimate(
            flops=2 * n_f * groups * LANES**3 * 6, bytes_accessed=4 * 2**20, transcendentals=0
        ),
        compiler_params=pltpu.CompilerParams(vmem_limit_bytes=32 * 2**20),
    )(me, inv, idx, tokens, grad_out, moment)


def base_kernel(groups, inv_ref, idx_ref, val_ref, moment_ref, out_ref):
    inv = inv_ref[...]
    for g in range(groups):
        a_hi, a_lo, b_hi, b_lo = entry_rows(inv, idx_ref[0, 0, g : g + 1, :], idx_ref[0, 1, g : g + 1, :])
        av_hi, av_lo = split((a_hi + a_lo) * val_ref[g : g + 1, :])
        left = jnp.concatenate([av_hi, av_hi, av_lo], axis=1)
        right = jnp.concatenate([b_hi, b_lo, b_hi], axis=1).astype(jnp.bfloat16)
        part = slice(g * LANES, (g + 1) * LANES)
        out_ref[part, :] = momentum_decay * moment_ref[part, :] - dot(left, right, ((1,), (1,)))


def moment_base(inv, idx, values, moment):
    groups = values.shape[0]
    rows, width = moment.shape
    return pl.pallas_call(
        functools.partial(base_kernel, groups),
        grid=(1,),
        in_specs=[
            pl.BlockSpec(inv.shape, lambda i: (0, 0)),
            pl.BlockSpec((1, 2, groups, LANES), lambda i: (0, 0, 0, 0)),
            pl.BlockSpec((groups, LANES), lambda i: (0, 0)),
            pl.BlockSpec((rows, width), lambda i: (0, 0)),
        ],
        out_specs=pl.BlockSpec((rows, width), lambda i: (0, 0)),
        out_shape=jax.ShapeDtypeStruct((rows, width), jnp.float32),
        cost_estimate=pl.CostEstimate(
            flops=2 * groups * LANES**3 * 7, bytes_accessed=2 * rows * width * 4, transcendentals=0
        ),
        compiler_params=pltpu.CompilerParams(vmem_limit_bytes=32 * 2**20),
    )(inv, idx, values, moment)


def project_kernel(pieces, extra, place, inv_ref, nt_ref, here_ref, there_ref, out_ref, coef_ref):
    width = nt_ref.shape[1]
    total = jnp.zeros(out_ref.shape, jnp.float32)
    half = here_ref.shape[0]
    size = width // pieces
    for p in range(pieces):
        source = here_ref if p < half else there_ref
        cols = pl.ds(pl.multiple_of(place[p] * size, size), size)
        total += dot(nt_ref[:, cols], source[p % half, extra:, :])
    out_ref[...] = total
    inv = inv_ref[...]
    table = jnp.concatenate([inv[:LANES], inv[LANES:]], axis=1)
    for g in range(width // LANES):
        part = slice(g * LANES, (g + 1) * LANES)
        both = dot(nt_ref[:, part], table)
        coef_ref[:, part] = (both[:, :LANES] + both[:, LANES:]).astype(jnp.bfloat16)


def project(place, inv, next_tokens, here, there, extra):
    pieces = place.shape[0]
    toks, width = next_tokens.shape
    out = here.shape[2]
    full = lambda *shape: pl.BlockSpec(shape, lambda i, place: (0,) * len(shape))
    return pl.pallas_call(
        functools.partial(project_kernel, pieces, extra),
        grid_spec=pltpu.PrefetchScalarGridSpec(
            num_scalar_prefetch=1,
            grid=(1,),
            in_specs=[full(*inv.shape), full(toks, width), full(*here.shape), full(*there.shape)],
            out_specs=[full(toks, out), full(toks, width)],
        ),
        out_shape=[jax.ShapeDtypeStruct((toks, out), jnp.float32), jax.ShapeDtypeStruct((toks, width), jnp.bfloat16)],
        cost_estimate=pl.CostEstimate(
            flops=2 * toks * width * out * 3, bytes_accessed=6 * toks * width * 2, transcendentals=0
        ),
        compiler_params=pltpu.CompilerParams(vmem_limit_bytes=48 * 2**20),
    )(place, inv, next_tokens, here, there)


def total_kernel(groups, n_r, me, inv_ref, fwd_ref, idx_ref, val_ref, coef_ref, base_ref, up_ref, out_ref, acc_ref):
    step = pl.program_id(0)
    inv = inv_ref[...]
    fwd = fwd_ref[...]

    @pl.when(step == 0)
    def _():
        acc_ref[...] = jnp.zeros_like(acc_ref)

    def group(g, own):
        left, right = [], []
        for r in range(n_r):
            left.append(hot(idx_ref[r, 0, 0, pl.ds(g, 1), :], 1.0).astype(jnp.bfloat16))
            right.append(hot(idx_ref[r, 0, 1, pl.ds(g, 1), :], val_ref[r, 0, pl.ds(g, 1), :]).astype(jnp.bfloat16))
        dense = dot(jnp.concatenate(left, axis=1), jnp.concatenate(right, axis=1), ((1,), (1,)))
        q_hi, q_lo = split(dense)
        cols = pl.ds(pl.multiple_of(g * LANES, LANES), LANES)
        both = dot(coef_ref[:, cols], jnp.concatenate([q_hi, q_lo], axis=1))
        acc_ref[...] += both[:, :LANES] + both[:, LANES:]
        if own:
            c_hi, c_lo = inv[:LANES], inv[LANES:]
            along = dot(
                jnp.concatenate([c_hi, c_hi, c_lo], axis=1), jnp.concatenate([q_hi, q_lo, q_hi], axis=0)
            )
            s_hi, s_lo = split(along)
            f_hi, f_lo = fwd[:LANES], fwd[LANES:]
            up_ref[cols, :] = dot(
                jnp.concatenate([s_hi, s_hi, s_lo], axis=1), jnp.concatenate([f_hi, f_lo, f_hi], axis=0)
            )

    @pl.when(step == 0)
    def _():
        @pl.loop(0, groups)
        def _(g):
            group(g, True)

    @pl.when(step != 0)
    def _():
        @pl.loop(0, groups)
        def _(g):
            group(g, False)

    @pl.when(step == pl.num_programs(0) - 1)
    def _():
        s_hi, s_lo = split(acc_ref[...])
        f_hi, f_lo = fwd[:LANES], fwd[LANES:]
        moved = dot(jnp.concatenate([s_hi, s_hi, s_lo], axis=1), jnp.concatenate([f_hi, f_lo, f_hi], axis=0))
        out_ref[...] = (base_ref[...] - step_size * moved).astype(out_ref.dtype)


def totals(me, inv, fwd, idx, values, coef, base):
    n_r, n_f, _, groups, _ = idx.shape
    rows = groups * LANES
    toks, width = base.shape
    return pl.pallas_call(
        functools.partial(total_kernel, groups, n_r),
        grid_spec=pltpu.PrefetchScalarGridSpec(
            num_scalar_prefetch=1,
            grid=(n_f,),
            in_specs=[
                pl.BlockSpec(inv.shape, lambda s, me: (0, 0)),
                pl.BlockSpec(fwd.shape, lambda s, me: (0, 0)),
                pl.BlockSpec((n_r, 1, 2, groups, LANES), lambda s, me: (0, s, 0, 0, 0)),
                pl.BlockSpec((n_r, 1, groups, LANES), lambda s, me: (0, me[0] ^ s, 0, 0)),
                pl.BlockSpec((toks, rows), lambda s, me: (0, me[0] ^ s)),
                pl.BlockSpec((toks, width), lambda s, me: (0, 0)),
            ],
            out_specs=[
                pl.BlockSpec((rows, width), lambda s, me: (0, 0)),
                pl.BlockSpec((toks, width), lambda s, me: (0, 0)),
            ],
            scratch_shapes=[pltpu.VMEM((toks, width), jnp.float32)],
        ),
        out_shape=[
            jax.ShapeDtypeStruct((rows, width), jnp.float32),
            jax.ShapeDtypeStruct((toks, width), jnp.bfloat16),
        ],
        cost_estimate=pl.CostEstimate(
            flops=2 * n_f * groups * LANES**3 * (n_r + 2), bytes_accessed=4 * 2**20, transcendentals=0
        ),
        compiler_params=pltpu.CompilerParams(vmem_limit_bytes=32 * 2**20),
    )(me, inv, fwd, idx, values, coef, base)


def swap(x, axis, size, mask):
    return lax.ppermute(x, axis, [(i, i ^ mask) for i in range(size)])


SLOTS = np.array([[3, 1, 2, 0], [2, 0, 3, 1], [3, 1, 0, 2], [2, 0, 1, 3]], np.int32)


def line_fast(n_r, n_f, tokens, grad_out, moment, weight, next_tokens, index):
    bf16 = jnp.bfloat16
    r, f = lax.axis_index("rep"), lax.axis_index("fsdp")
    me = jnp.stack([f]).astype(jnp.int32)
    inv, fwd = tables()
    moment = moment[0]
    rows = moment.shape[0]
    groups = rows // LANES
    slice_rows = rows // n_r

    flat = index[0].reshape(groups, LANES)
    lane = jnp.arange(LANES, dtype=jnp.int32)
    row_pos = flat // TILE + (lane // TILE) * TILE
    col_pos = flat % TILE + (lane // (TILE // 2)) % 2 * TILE
    own_idx = jnp.concatenate([row_pos, col_pos], axis=0).astype(bf16)
    extra = own_idx.shape[0]
    share = lax.dynamic_slice_in_dim(weight, r * slice_rows, slice_rows, axis=0)
    held = jnp.concatenate([own_idx, share], axis=0)[None]

    slots = jnp.asarray(SLOTS)[f]
    first, second = partial_chunks(tokens, grad_out, slots[:2], rows)
    third, kept = partial_chunks(tokens, grad_out, slots[2:], rows)
    right = lax.ppermute(first, "fsdp", [(0, 1), (1, 2), (2, 3)])
    left = lax.ppermute(second, "fsdp", [(3, 2), (2, 1), (1, 0)])
    far_r = lax.ppermute(second, "fsdp", [(0, 1)])
    far_l = lax.ppermute(first, "fsdp", [(3, 2)])
    merged = (
        third.astype(jnp.float32)
        + jnp.where(f == 1, right.astype(jnp.float32), 0.0)
        + jnp.where(f == 2, left.astype(jnp.float32), 0.0)
    ).astype(bf16)
    two = lax.ppermute(merged, "fsdp", [(0, 2), (1, 3), (2, 0), (3, 1)])

    order = [(0, 0)]
    mask = 1
    while mask < n_f:
        held = jnp.concatenate([held, swap(held, "fsdp", n_f, mask)], axis=0)
        order = order + [(a, b ^ mask) for a, b in order]
        mask *= 2
    idx_near = held[:, :extra].astype(jnp.int32).reshape(n_f, 2, groups, LANES)
    mask = n_r // 2
    while mask >= 1:
        there = swap(held, "rep", n_r, mask)
        order = order + [(a ^ mask, b) for a, b in order]
        if mask > 1:
            held = jnp.concatenate([held, there], axis=0)
        mask //= 2
    idx_all = (
        jnp.concatenate([held[:, :extra], there[:, :extra]], axis=0)
        .astype(jnp.int32)
        .reshape(n_r, n_f, 2, groups, LANES)
    )
    order = np.array(order, np.int32)
    place = (jnp.asarray(order[:, 1]) ^ f) * n_r + (jnp.asarray(order[:, 0]) ^ r)

    values = select_values(me, inv, idx_near, tokens, grad_out, moment)
    mask = 1
    while mask < n_f:
        values = values + swap(values, "fsdp", n_f, mask)
        mask *= 2
    own_values = lax.dynamic_index_in_dim(values, f, 0, keepdims=False)
    sent = values.astype(bf16)[None]
    mask = n_r // 2
    while mask >= 1:
        sent = jnp.concatenate([sent, swap(sent, "rep", n_r, mask)], axis=0)
        mask //= 2

    base = moment_base(inv, idx_near, own_values, moment)
    old_out, coef = project(place.astype(jnp.int32), inv, next_tokens, held, there, extra)
    update, next_out = totals(me, inv, fwd, idx_all, sent.astype(jnp.float32), coef, old_out)

    near = jnp.where(f <= 1, left, right).astype(jnp.float32)
    grad = kept.astype(jnp.float32) + near + two.astype(jnp.float32) + far_r.astype(jnp.float32) + far_l.astype(jnp.float32)
    return update, (base + grad)[None], next_out


def cosine_table(order):
    return jnp.asarray(cosine_array(order), jnp.float32)


def forward_tiles(field, table):
    side = table.shape[0]
    shard_rows, width = field.shape
    tiles = field.reshape(shard_rows // side, side, width)
    along = jnp.einsum("ab,ibc->iac", table, tiles, precision=lax.Precision.HIGHEST)
    block = jnp.kron(jnp.eye(width // side, dtype=jnp.float32), table.T)
    return jnp.matmul(along, block, precision=lax.Precision.HIGHEST)


def inverse_tiles(spectra, table):
    side = table.shape[0]
    width = spectra.shape[2]
    along = jnp.einsum("ab,iac->ibc", table, spectra, precision=lax.Precision.HIGHEST)
    block = jnp.kron(jnp.eye(width // side, dtype=jnp.float32), table)
    result = jnp.matmul(along, block, precision=lax.Precision.HIGHEST)
    return result.reshape(spectra.shape[0] * side, width)


def one_hots(places, side, width):
    row_of = places // side
    col_of = places % side + jnp.arange(width // side, dtype=jnp.int32)[:, None] * side
    row_hot = (row_of[..., None] == jnp.arange(side, dtype=jnp.int32)).astype(jnp.float32)
    col_hot = (col_of[..., None] == jnp.arange(width, dtype=jnp.int32)).astype(jnp.float32)
    return (row_hot, col_hot)


def any_mesh(tokens, grad_out, moment, weight, next_tokens, index):
    table = cosine_table(TILE)
    width = weight.shape[1]
    partial = lax.dot_general(tokens, grad_out, (((0,), (0,)), ((), ())), preferred_element_type=jnp.float32)
    grad = lax.psum_scatter(partial.astype(jnp.bfloat16), "fsdp", scatter_dimension=0, tiled=True)
    moment_now = momentum_decay * moment[0] + grad.astype(jnp.float32)
    spectra = forward_tiles(moment_now, table)
    row_hot, col_hot = one_hots(index[0], TILE, width)
    picked = jnp.einsum("ijka,iac->ijkc", row_hot, spectra, precision=lax.Precision.HIGHEST)
    values = jnp.sum(picked * col_hot, axis=-1)
    dense = jnp.einsum("ijka,ijkc->iac", row_hot * values[..., None], col_hot, precision=lax.Precision.HIGHEST)
    new_moment = (moment_now - inverse_tiles(dense, table))[None]
    total = lax.psum(dense.astype(jnp.bfloat16), "rep").astype(jnp.float32)
    update = inverse_tiles(total, table)
    new_weight = (weight.astype(jnp.float32) - step_size * update).astype(jnp.bfloat16)
    full = lax.all_gather(new_weight, "fsdp", axis=0, tiled=True)
    next_out = jnp.dot(next_tokens, full, preferred_element_type=jnp.float32).astype(jnp.bfloat16)
    return (update, new_moment, next_out)


def solution(mesh):
    n_r, n_f = mesh.shape["rep"], mesh.shape["fsdp"]
    local = functools.partial(line_fast, n_r, n_f) if (n_r, n_f) == (8, 4) else any_mesh
    in_specs = (
        P(("rep", "fsdp"), None),
        P(("rep", "fsdp"), None),
        P("rep", "fsdp", None),
        P("fsdp", None),
        P(("rep", "fsdp"), None),
        P("rep", "fsdp", None, None),
    )
    out_specs = (P("fsdp", None), P("rep", "fsdp", None), P(("rep", "fsdp"), None))
    return jax.shard_map(local, mesh=mesh, in_specs=in_specs, out_specs=out_specs, check_vma=False)
```

time: 186 us -> 120 us (0.65)
  waiting for transfers between devices: 140 us -> 22.7 us
  Pallas kernels: 0 us -> 52.2 us
  starting transfers between devices: 0.3 us -> 27.5 us
  matrix products: 26.7 us -> 0 us
  between operations: 13.8 us -> 0.98 us
  local copies, waits for them, and re-layouts: 2.68 us -> 10.2 us
  other arithmetic: 2.08 us -> 6.12 us
    psum x1 -> x0, waiting for transfers between devices: 53.7 us -> none  [local(): total = lax.psum(dense.astype(jnp.bfloat16), 'rep').astype(jnp.float32)]
    pallas_call x0 -> x6, Pallas kernels: none -> 52.2 us  [the longest x1 33.7 us: totals(): pl.pallas_call(functools.partial(total_kernel, groups, n_r), grid_spec=pl...]
    reduce_scatter x1 -> x0, waiting for transfers between devices: 45.8 us -> none  [local(): lax.psum_scatter(lax.dot_general(columns, grad_out, (((0,), (0,)), ((), (...]
    all_gather x1 -> x0, waiting for transfers between devices: 41 us -> none  [local(): lax.all_gather(new_weight, 'fsdp', axis=0, tiled=True)]
    ppermute x0 -> x15, starting transfers between devices: none -> 27.5 us  [the longest x10 18.2 us: swap(): return lax.ppermute(x, axis, [(i, i ^ mask) for i in range(size)])]
    dot_general x10 -> x0, matrix products: 26.7 us -> none  [the longest x2 5.11 us: inverse_tiles(): result = jnp.matmul(along, block, precision=lax.Precision.HIGHEST)]
    ppermute x0 -> x15, waiting for transfers between devices: none -> 22.7 us  [the longest x10 12.7 us: swap(): return lax.ppermute(x, axis, [(i, i ^ mask) for i in range(size)])]
    unnamed x5 -> x37, local copies, waits for them, and re-layouts: 2.27 us -> 6.73 us
  transfers between devices with their start and end apart: 3 -> 15, of which waited for: 3 -> 5; matrix products, arithmetic and copies ran while one was open for 3% -> 10% of each run, Pallas kernels for 0% -> 12%
where the time goes in v1:
time: 120 us
  Pallas kernels  52.2 us (44%)
  starting transfers between devices  27.5 us (23%)
  waiting for transfers between devices  22.7 us (19%)
  local copies, waits for them, and re-layouts  10.2 us (8%)
  other arithmetic  6.12 us (5%)
    pallas_call x1, Pallas kernels, totals(): pl.pallas_call(functools.partial(total_kernel, groups, n_r), grid_spec=pl...  33.7 us
    ppermute x10, starting transfers between devices, swap(): return lax.ppermute(x, axis, [(i, i ^ mask) for i in range(size)])  18.2 us
    ppermute x10, waiting for transfers between devices, swap(): return lax.ppermute(x, axis, [(i, i ^ mask) for i in range(size)])  12.7 us
    ppermute x1, waiting for transfers between devices, line_fast(): two = lax.ppermute(merged, 'fsdp', [(0, 2), (1, 3), (2, 0), (3, 1)])  9.94 us
    pallas_call x1, Pallas kernels, select_values(): pl.pallas_call(functools.partial(select_kernel, groups), grid_spec=pltpu....  9.18 us
    unnamed x37, local copies, waits for them, and re-layouts  6.73 us
    ppermute x1, starting transfers between devices, line_fast(): right = lax.ppermute(first, 'fsdp', [(0, 1), (1, 2), (2, 3)])  4.3 us
    pallas_call x1, Pallas kernels, project(): pl.pallas_call(functools.partial(project_kernel, pieces, extra), grid_spe...  4.24 us
  transfers between devices with their start and end apart: 15, of which 5 were waited for; matrix products, arithmetic and copies ran while one was open for 10% of the time, Pallas kernels for 12%

profile of v1, /device:TPU:0, one launch (start us, length us, event | category | flops | bytes accessed | tf_op | source)
XLA Modules:
  0.0 119.6 jit_solution(561233414739260194)
XLA Ops:
  0.6 0.0 copy-start
  0.7 0.9 reshape_squeeze.3
  1.6 0.1 copy-done
  1.7 3.1 %collective-permute-start = (bf16[1,288,128]{2,1,0:T(8,128)(2,1)S(1)}, bf16[1,288,128]{2,1,0:T(8,128)(2,1)S(1)}, u32[]{:S(2)}, u32[]{:S(2)}) collective-permute-start(bf16[1,288,128]{2,1,0:T(8,128)(2,1)S(1)} %maximum_bitcast_fusion), channel_id=1, source_target_pairs={{0,1},{1,0},{2,3},{3,2},{4,5},{5,4},{6,7},{7,6},{8,9},{9,8},{10,11... | collective-permute-start | bytes 221192 | tf_op jit(solution)/shard_map/ppermute | solution.py:299
  4.8 0.7 constant_dynamic-slice_fusion
  5.5 1.6 %collective-permute-done = bf16[1,288,128]{2,1,0:T(8,128)(2,1)S(1)} collective-permute-done((bf16[1,288,128]{2,1,0:T(8,128)(2,1)S(1)}, bf16[1,288,128]{2,1,0:T(8,128)(2,1)S(1)}, u32[]{:S(2)}, u32[]{:S(2)}) %collective-permute-start) | collective-permute-done | bytes 73760 | tf_op jit(solution)/shard_map/ppermute | solution.py:299
  7.2 3.1 %collective-permute-start.1 = (bf16[2,288,128]{2,1,0:T(8,128)(2,1)S(1)}, bf16[2,288,128]{2,1,0:T(8,128)(2,1)S(1)}, u32[]{:S(2)}, u32[]{:S(2)}) collective-permute-start(bf16[2,288,128]{2,1,0:T(8,128)(2,1)S(1)} %pad_maximum_fusion.3), channel_id=1, source_target_pairs={{0,2},{1,3},{2,0},{3,1},{4,6},{5,7},{6,4},{7,5},{8,10},{9,11},{10,... | collective-permute-start | bytes 442376 | tf_op jit(solution)/shard_map/ppermute | solution.py:299
  10.3 0.1 slice_bitcast_fusion.1
  10.4 1.6 %copy-done.1 = bf16[128,8192]{1,0:T(8,128)(2,1)S(1)} copy-done((bf16[128,8192]{1,0:T(8,128)(2,1)S(1)}, bf16[128,8192]{1,0:T(8,128)(2,1)}, u32[]{:S(2)}) %copy-start.1) | copy-done | bytes 2097176
  12.0 0.8 copy-done.6
  12.7 2.3 %shard_map.135 = (bf16[2048,128]{1,0:T(8,128)(2,1)}, bf16[2048,128]{1,0:T(8,128)(2,1)}) custom-call(s32[2]{0:T(128)S(1)} %get-tuple-element.24.slots, bf16[128,8192]{1,0:T(8,128)(2,1)S(1)} %copy-done.1, bf16[128,128]{1,0:T(8,128)(2,1)S(1)} %copy-done.6), custom_call_target="tpu_custom_call" | custom-call | flops 134217728 | bytes 2097152 | tf_op jit(solution)/shard_map/pallas_call | solution.py:59
  15.0 1.5 %collective-permute-start.14 = (bf16[2048,128]{1,0:T(8,128)(2,1)}, bf16[2048,128]{1,0:T(8,128)(2,1)}, u32[]{:S(2)}, u32[]{:S(2)}) collective-permute-start(bf16[2048,128]{1,0:T(8,128)(2,1)} %get-tuple-element.16), channel_id=1, source_target_pairs={{3,2},{7,6},{11,10},{15,14},{19,18},{23,22},{27,26},{31,30}} | collective-permute-start | bytes 1572872 | tf_op jit(solution)/shard_map/ppermute | solution.py:330
  16.5 4.3 %collective-permute-start.11 = (bf16[2048,128]{1,0:T(8,128)(2,1)}, bf16[2048,128]{1,0:T(8,128)(2,1)}, u32[]{:S(2)}, u32[]{:S(2)}) collective-permute-start(bf16[2048,128]{1,0:T(8,128)(2,1)} %get-tuple-element.16), channel_id=1, source_target_pairs={{0,1},{1,2},{2,3},{4,5},{5,6},{6,7},{8,9},{9,10},{10,11},{12,13},{... | collective-permute-start | bytes 1572872 | tf_op jit(solution)/shard_map/ppermute | solution.py:327
  20.8 1.3 %collective-permute-start.10 = (bf16[2048,128]{1,0:T(8,128)(2,1)}, bf16[2048,128]{1,0:T(8,128)(2,1)}, u32[]{:S(2)}, u32[]{:S(2)}) collective-permute-start(bf16[2048,128]{1,0:T(8,128)(2,1)} %get-tuple-element.15), channel_id=1, source_target_pairs={{3,2},{2,1},{1,0},{7,6},{6,5},{5,4},{11,10},{10,9},{9,8},{15,14},{... | collective-permute-start | bytes 1572872 | tf_op jit(solution)/shard_map/ppermute | solution.py:328
  22.2 0.0 copy-start.3
  22.2 1.3 %copy-done.3 = f32[1,2048,128]{2,1,0:T(8,128)S(1)} copy-done((f32[1,2048,128]{2,1,0:T(8,128)S(1)}, f32[1,2048,128]{2,1,0:T(8,128)}, u32[]{:S(2)}) %copy-start.3) | copy-done | bytes 1048600
  23.5 9.2 %shard_map.130 = f32[4,16,128]{2,1,0:T(8,128)S(1)} custom-call(s32[1]{0:T(128)} %bitcast.me, bf16[256,128]{1,0:T(8,128)(2,1)S(1)} %copy-done.5, s32[4,2,16,128]{3,2,1,0:T(8,128)S(1)} %convert.10.idx_ref, bf16[128,8192]{1,0:T(8,128)(2,1)S(1)} %copy-done.2, bf16[128,128]{1,0:T(8,128)(2,1)S(1)} %copy-done.6, f32[2048,128]{1,0:T(8,128)S(1)} %bitcast.20), custom_call_target="tpu_custom_call" | custom-call | flops 1610612736 | bytes 4194304 | tf_op jit(solution)/shard_map/pallas_call | solution.py:121
  32.7 2.7 %collective-permute-start.5 = (f32[4,16,128]{2,1,0:T(8,128)S(1)}, f32[4,16,128]{2,1,0:T(8,128)S(1)}, u32[]{:S(2)}, u32[]{:S(2)}) collective-permute-start(f32[4,16,128]{2,1,0:T(8,128)S(1)} %shard_map.130), channel_id=1, source_target_pairs={{0,1},{1,0},{2,3},{3,2},{4,5},{5,4},{6,7},{7,6},{8,9},{9,8},{10,11... | collective-permute-start | bytes 98312 | tf_op jit(solution)/shard_map/ppermute | solution.py:299
  35.4 0.6 constant_dynamic-update-slice_fusion.4
  36.0 1.4 %shard_map.134 = (bf16[2048,128]{1,0:T(8,128)(2,1)S(1)}, bf16[2048,128]{1,0:T(8,128)(2,1)S(1)}) custom-call(s32[2]{0:T(128)S(1)} %get-tuple-element.23.slots, bf16[128,8192]{1,0:T(8,128)(2,1)S(1)} %copy-done.2, bf16[128,128]{1,0:T(8,128)(2,1)S(1)} %copy-done.7), custom_call_target="tpu_custom_call" | custom-call | flops 134217728 | bytes 2097152 | tf_op jit(solution)/shard_map/pallas_call | solution.py:59
  37.4 0.0 collective-permute-done.5
  37.4 4.5 %collective-permute-start.6 = (f32[4,16,128]{2,1,0:T(8,128)S(1)}, f32[4,16,128]{2,1,0:T(8,128)S(1)}, u32[]{:S(2)}, u32[]{:S(2)}) collective-permute-start(f32[4,16,128]{2,1,0:T(8,128)S(1)} %add.88), channel_id=1, source_target_pairs={{0,2},{1,3},{2,0},{3,1},{4,6},{5,7},{6,4},{7,5},{8,10},{9,11},{10,... | collective-permute-start | bytes 98312 | tf_op jit(solution)/shard_map/ppermute | solution.py:299
  41.9 1.5 %constant_dynamic-update-slice_fusion.3 = bf16[16,288,128]{2,1,0:T(8,128)(2,1)} fusion(bf16[16,288,128]{2,1,0:T(8,128)(2,1)} %constant_dynamic-update-slice_fusion.4, bf16[1,288,128]{2,1,0:T(8,128)(2,1)} %copy-done.11), kind=kLoop, calls=%fused_computation.19 | loop fusion | bytes 147456
  43.4 1.6 %collective-permute-start.2 = (bf16[4,288,128]{2,1,0:T(8,128)(2,1)S(1)}, bf16[4,288,128]{2,1,0:T(8,128)(2,1)S(1)}, u32[]{:S(2)}, u32[]{:S(2)}) collective-permute-start(bf16[4,288,128]{2,1,0:T(8,128)(2,1)S(1)} %copy-done.14), channel_id=1, source_target_pairs={{0,16},{4,20},{8,24},{12,28},{16,0},{20,4},{24,8},{28,12},{1,17},{... | collective-permute-start | bytes 884744 | tf_op jit(solution)/shard_map/ppermute | solution.py:299
  45.0 0.0 collective-permute-done.6
  45.0 0.5 collective-permute-start.7
  45.5 0.7 constant_dynamic-update-slice_fusion.2
  46.2 4.1 %collective-permute-done.7 = bf16[1,4,16,128]{3,2,1,0:T(8,128)(2,1)S(1)} collective-permute-done((bf16[1,4,16,128]{3,2,1,0:T(8,128)(2,1)S(1)}, bf16[1,4,16,128]{3,2,1,0:T(8,128)(2,1)S(1)}, u32[]{:S(2)}, u32[]{:S(2)}) %collective-permute-start.7) | collective-permute-done | bytes 16416 | tf_op jit(solution)/shard_map/ppermute | solution.py:299
  50.3 2.2 %collective-permute-start.13 = (bf16[2048,128]{1,0:T(8,128)(2,1)}, bf16[2048,128]{1,0:T(8,128)(2,1)}, u32[]{:S(2)}, u32[]{:S(2)}) collective-permute-start(bf16[2048,128]{1,0:T(8,128)(2,1)} %get-tuple-element.15), channel_id=1, source_target_pairs={{0,1},{4,5},{8,9},{12,13},{16,17},{20,21},{24,25},{28,29}} | collective-permute-start | bytes 1572872 | tf_op jit(solution)/shard_map/ppermute | solution.py:329
  52.6 0.0 collective-permute-done.2
  52.6 0.1 pad_maximum_fusion
  52.7 1.6 %collective-permute-start.3 = (bf16[8,288,128]{2,1,0:T(8,128)(2,1)S(1)}, bf16[8,288,128]{2,1,0:T(8,128)(2,1)S(1)}, u32[]{:S(2)}, u32[]{:S(2)}) collective-permute-start(bf16[8,288,128]{2,1,0:T(8,128)(2,1)S(1)} %pad_maximum_fusion), channel_id=1, source_target_pairs={{0,8},{4,12},{8,0},{12,4},{16,24},{20,28},{24,16},{28,20},{1,9},{5... | collective-permute-start | bytes 1769480 | tf_op jit(solution)/shard_map/ppermute | solution.py:299
  54.3 0.7 constant_dynamic-update-slice_fusion.1
  55.0 0.5 collective-permute-start.8
  55.5 0.0 collective-permute-done.11
  55.5 2.3 %add_convert_fusion = bf16[2048,128]{1,0:T(8,128)(2,1)} fusion(bf16[2048,128]{1,0:T(8,128)(2,1)} %collective-permute-done.10, bf16[2048,128]{1,0:T(8,128)(2,1)} %collective-permute-done.11, bf16[2048,128]{1,0:T(8,128)(2,1)S(1)} %get-tuple-element.17, pred[]{:T(512)S(6)} %eq.11, pred[]{:T(512)S(6)} %eq.10), kind=kLoop, calls=%fused_computation.1 | loop fusion | flops 2097152 | bytes 2097154 | tf_op jit(solution)/shard_map/convert_element_type | solution.py:335
  57.8 6.4 %collective-permute-done.3 = bf16[8,288,128]{2,1,0:T(8,128)(2,1)S(1)} collective-permute-done((bf16[8,288,128]{2,1,0:T(8,128)(2,1)S(1)}, bf16[8,288,128]{2,1,0:T(8,128)(2,1)S(1)}, u32[]{:S(2)}, u32[]{:S(2)}) %collective-permute-start.3) | collective-permute-done | bytes 589856 | tf_op jit(solution)/shard_map/ppermute | solution.py:299
  64.3 0.9 constant_dynamic-update-slice_fusion.here_ref
  65.2 0.6 collective-permute-start.9
  65.8 1.4 %shard_map.133 = f32[2048,128]{1,0:T(8,128)S(1)} custom-call(bf16[256,128]{1,0:T(8,128)(2,1)S(1)} %copy-done.5, s32[4,2,16,128]{3,2,1,0:T(8,128)S(1)} %convert.10.idx_ref, f32[16,128]{1,0:T(8,128)S(1)} %dynamic-slice_bitcast_fusion.val_ref, f32[2048,128]{1,0:T(8,128)S(1)} %bitcast.21), custom_call_target="tpu_custom_call" | custom-call | flops 469762048 | bytes 2097152 | tf_op jit(solution)/shard_map/pallas_call | solution.py:157
  67.2 0.5 collective-permute-done.9
  67.8 9.9 %collective-permute-done.12 = bf16[2048,128]{1,0:T(8,128)(2,1)} collective-permute-done((bf16[2048,128]{1,0:T(8,128)(2,1)}, bf16[2048,128]{1,0:T(8,128)(2,1)}, u32[]{:S(2)}, u32[]{:S(2)}) %collective-permute-start.12) | collective-permute-done | bytes 524320 | tf_op jit(solution)/shard_map/ppermute | solution.py:336
  77.7 2.9 %add_bitcast_fusion = f32[1,2048,128]{2,1,0:T(8,128)} fusion(f32[2048,128]{1,0:T(8,128)S(1)} %shard_map.133, bf16[2048,128]{1,0:T(8,128)(2,1)} %collective-permute-done.14, bf16[2048,128]{1,0:T(8,128)(2,1)} %collective-permute-done.13, bf16[2048,128]{1,0:T(8,128)(2,1)} %collective-permute-done.12, bf16[2048,128]{1,0:T(8,128)(2,1)S(1)} %get-tuple-element.14, ...), kind=kLoop, calls=%fused_computation | loop fusion | flops 2883584 | bytes 5242881 | tf_op jit(solution)/shard_map/broadcast_in_dim | solution.py:378
  80.6 0.9 slice.28
  81.6 0.1 convert.11.idx_ref
  81.7 0.0 copy-start.8
  81.7 4.2 %shard_map.131 = (f32[128,128]{1,0:T(8,128)S(1)}, bf16[128,8192]{1,0:T(8,128)(2,1)S(1)}) custom-call(s32[32]{0:T(128)S(1)} %xor_add_fusion.place, bf16[256,128]{1,0:T(8,128)(2,1)S(1)} %copy-done.5, bf16[128,8192]{1,0:T(8,128)(2,1)} %nt_ref.1, bf16[16,288,128]{2,1,0:T(8,128)(2,1)} %constant_dynamic-update-slice_fusion.here_ref, ...), custom_call_target="tpu_custom_call" | custom-call | flops 805306368 | bytes 12582912 | tf_op jit(solution)/shard_map/pallas_call | solution.py:198
  86.0 33.7 %shard_map.132 = (f32[2048,128]{1,0:T(8,128)}, bf16[128,128]{1,0:T(8,128)(2,1)}) custom-call(s32[1]{0:T(128)} %bitcast.me, bf16[256,128]{1,0:T(8,128)(2,1)S(1)} %copy-done.5, bf16[256,128]{1,0:T(8,128)(2,1)S(1)} %copy-done.8, s32[8,4,2,16,128]{4,3,2,1,0:T(8,128)S(1)} %convert.11.idx_ref, f32[8,4,16,128]{3,2,1,0:T(8,128)S(1)} %maximum_convert_fusion.val_ref, ...), custom_call_target="tpu_custom_call" | custom-call | flops 2684354560 | bytes 4194304 | tf_op jit(solution)/shard_map/pallas_call | solution.py:268
  (52 shorter events, 0.3 us)
Async XLA Ops:
  0.6 1.1 copy-start
  1.7 20.3 %copy-start.9 = (bf16[1,288,128]{2,1,0:T(8,128)(2,1)}, bf16[1,288,128]{2,1,0:T(8,128)(2,1)S(1)}, u32[]{:S(2)}) copy-start(bf16[1,288,128]{2,1,0:T(8,128)(2,1)S(1)} %maximum_bitcast_fusion) | copy-start | bytes 221188
  1.7 5.4 %collective-permute-start = (bf16[1,288,128]{2,1,0:T(8,128)(2,1)S(1)}, bf16[1,288,128]{2,1,0:T(8,128)(2,1)S(1)}, u32[]{:S(2)}, u32[]{:S(2)}) collective-permute-start(bf16[1,288,128]{2,1,0:T(8,128)(2,1)S(1)} %maximum_bitcast_fusion), channel_id=1, source_target_pairs={{0,1},{1,0},{2,3},{3,2},{4,5},{5,4},{6,7},{7,6},{8,9},{9,8},{10,11... | collective-permute-start | bytes 221192 | tf_op jit(solution)/shard_map/ppermute | solution.py:299
  7.2 14.9 %copy-start.11 = (bf16[1,288,128]{2,1,0:T(8,128)(2,1)}, bf16[1,288,128]{2,1,0:T(8,128)(2,1)S(1)}, u32[]{:S(2)}) copy-start(bf16[1,288,128]{2,1,0:T(8,128)(2,1)S(1)} %collective-permute-done) | copy-start | bytes 221188
  7.2 14.9 %collective-permute-start.1 = (bf16[2,288,128]{2,1,0:T(8,128)(2,1)S(1)}, bf16[2,288,128]{2,1,0:T(8,128)(2,1)S(1)}, u32[]{:S(2)}, u32[]{:S(2)}) collective-permute-start(bf16[2,288,128]{2,1,0:T(8,128)(2,1)S(1)} %pad_maximum_fusion.3), channel_id=1, source_target_pairs={{0,2},{1,3},{2,0},{3,1},{4,6},{5,7},{6,4},{7,5},{8,10},{9,11},{10,... | collective-permute-start | bytes 442376 | tf_op jit(solution)/shard_map/ppermute | solution.py:299
  10.4 1.6 %copy-start.1 = (bf16[128,8192]{1,0:T(8,128)(2,1)S(1)}, bf16[128,8192]{1,0:T(8,128)(2,1)}, u32[]{:S(2)}) copy-start(bf16[128,8192]{1,0:T(8,128)(2,1)} %tok.3) | copy-start | bytes 6291460
  11.9 0.8 copy-start.6
  12.7 9.5 %copy-start.2 = (bf16[128,8192]{1,0:T(8,128)(2,1)S(1)}, bf16[128,8192]{1,0:T(8,128)(2,1)}, u32[]{:S(2)}) copy-start(bf16[128,8192]{1,0:T(8,128)(2,1)} %tok.3) | copy-start | bytes 6291460
  12.7 9.5 %copy-start.5 = (bf16[256,128]{1,0:T(8,128)(2,1)S(1)}, bf16[256,128]{1,0:T(8,128)(2,1)}, u32[]{:S(2)}) copy-start(bf16[256,128]{1,0:T(8,128)(2,1)} %constant.101.clone.inv_ref) | copy-start | bytes 196612
  15.0 52.8 %collective-permute-start.14 = (bf16[2048,128]{1,0:T(8,128)(2,1)}, bf16[2048,128]{1,0:T(8,128)(2,1)}, u32[]{:S(2)}, u32[]{:S(2)}) collective-permute-start(bf16[2048,128]{1,0:T(8,128)(2,1)} %get-tuple-element.16), channel_id=1, source_target_pairs={{3,2},{7,6},{11,10},{15,14},{19,18},{23,22},{27,26},{31,30}} | collective-permute-start | bytes 1572872 | tf_op jit(solution)/shard_map/ppermute | solution.py:330
  16.5 39.0 %collective-permute-start.11 = (bf16[2048,128]{1,0:T(8,128)(2,1)}, bf16[2048,128]{1,0:T(8,128)(2,1)}, u32[]{:S(2)}, u32[]{:S(2)}) collective-permute-start(bf16[2048,128]{1,0:T(8,128)(2,1)} %get-tuple-element.16), channel_id=1, source_target_pairs={{0,1},{1,2},{2,3},{4,5},{5,6},{6,7},{8,9},{9,10},{10,11},{12,13},{... | collective-permute-start | bytes 1572872 | tf_op jit(solution)/shard_map/ppermute | solution.py:327
  20.8 34.3 %collective-permute-start.10 = (bf16[2048,128]{1,0:T(8,128)(2,1)}, bf16[2048,128]{1,0:T(8,128)(2,1)}, u32[]{:S(2)}, u32[]{:S(2)}) collective-permute-start(bf16[2048,128]{1,0:T(8,128)(2,1)} %get-tuple-element.15), channel_id=1, source_target_pairs={{3,2},{2,1},{1,0},{7,6},{6,5},{5,4},{11,10},{10,9},{9,8},{15,14},{... | collective-permute-start | bytes 1572872 | tf_op jit(solution)/shard_map/ppermute | solution.py:328
  22.1 10.5 %copy-start.13 = (bf16[4,288,128]{2,1,0:T(8,128)(2,1)}, bf16[4,288,128]{2,1,0:T(8,128)(2,1)S(1)}, u32[]{:S(2)}) copy-start(bf16[4,288,128]{2,1,0:T(8,128)(2,1)S(1)} %pad_maximum_fusion.1) | copy-start | bytes 884740
  22.2 1.3 %copy-start.3 = (f32[1,2048,128]{2,1,0:T(8,128)S(1)}, f32[1,2048,128]{2,1,0:T(8,128)}, u32[]{:S(2)}) copy-start(f32[1,2048,128]{2,1,0:T(8,128)} %param.13) | copy-start | bytes 3145732
  23.5 12.5 %copy-start.7 = (bf16[128,128]{1,0:T(8,128)(2,1)S(1)}, bf16[128,128]{1,0:T(8,128)(2,1)}, u32[]{:S(2)}) copy-start(bf16[128,128]{1,0:T(8,128)(2,1)} %grad.3) | copy-start | bytes 98308
  32.7 4.7 %collective-permute-start.5 = (f32[4,16,128]{2,1,0:T(8,128)S(1)}, f32[4,16,128]{2,1,0:T(8,128)S(1)}, u32[]{:S(2)}, u32[]{:S(2)}) collective-permute-start(f32[4,16,128]{2,1,0:T(8,128)S(1)} %shard_map.130), channel_id=1, source_target_pairs={{0,1},{1,0},{2,3},{3,2},{4,5},{5,4},{6,7},{7,6},{8,9},{9,8},{10,11... | collective-permute-start | bytes 98312 | tf_op jit(solution)/shard_map/ppermute | solution.py:299
  36.0 7.4 %copy-start.14 = (bf16[4,288,128]{2,1,0:T(8,128)(2,1)S(1)}, bf16[4,288,128]{2,1,0:T(8,128)(2,1)}, u32[]{:S(2)}) copy-start(bf16[4,288,128]{2,1,0:T(8,128)(2,1)} %copy-done.13) | copy-start | bytes 884740
  36.0 16.6 %copy-start.10 = (bf16[1,288,128]{2,1,0:T(8,128)(2,1)S(1)}, bf16[1,288,128]{2,1,0:T(8,128)(2,1)}, u32[]{:S(2)}) copy-start(bf16[1,288,128]{2,1,0:T(8,128)(2,1)} %copy-done.9) | copy-start | bytes 221188
  36.0 16.6 %copy-start.12 = (bf16[1,288,128]{2,1,0:T(8,128)(2,1)S(1)}, bf16[1,288,128]{2,1,0:T(8,128)(2,1)}, u32[]{:S(2)}) copy-start(bf16[1,288,128]{2,1,0:T(8,128)(2,1)} %copy-done.11) | copy-start | bytes 221188
  37.4 7.6 %collective-permute-start.6 = (f32[4,16,128]{2,1,0:T(8,128)S(1)}, f32[4,16,128]{2,1,0:T(8,128)S(1)}, u32[]{:S(2)}, u32[]{:S(2)}) collective-permute-start(f32[4,16,128]{2,1,0:T(8,128)S(1)} %add.88), channel_id=1, source_target_pairs={{0,2},{1,3},{2,0},{3,1},{4,6},{5,7},{6,4},{7,5},{8,10},{9,11},{10,... | collective-permute-start | bytes 98312 | tf_op jit(solution)/shard_map/ppermute | solution.py:299
  43.4 9.2 %collective-permute-start.2 = (bf16[4,288,128]{2,1,0:T(8,128)(2,1)S(1)}, bf16[4,288,128]{2,1,0:T(8,128)(2,1)S(1)}, u32[]{:S(2)}, u32[]{:S(2)}) collective-permute-start(bf16[4,288,128]{2,1,0:T(8,128)(2,1)S(1)} %copy-done.14), channel_id=1, source_target_pairs={{0,16},{4,20},{8,24},{12,28},{16,0},{20,4},{24,8},{28,12},{1,17},{... | collective-permute-start | bytes 884744 | tf_op jit(solution)/shard_map/ppermute | solution.py:299
  45.0 5.3 %collective-permute-start.7 = (bf16[1,4,16,128]{3,2,1,0:T(8,128)(2,1)S(1)}, bf16[1,4,16,128]{3,2,1,0:T(8,128)(2,1)S(1)}, u32[]{:S(2)}, u32[]{:S(2)}) collective-permute-start(bf16[1,4,16,128]{3,2,1,0:T(8,128)(2,1)S(1)} %get-tuple-element.19), channel_id=1, source_target_pairs={{0,16},{4,20},{8,24},{12,28},{16,0},{20,4},{24,8},{28,12},{1,17},{... | collective-permute-start | bytes 49160 | tf_op jit(solution)/shard_map/ppermute | solution.py:299
  50.3 17.5 %collective-permute-start.13 = (bf16[2048,128]{1,0:T(8,128)(2,1)}, bf16[2048,128]{1,0:T(8,128)(2,1)}, u32[]{:S(2)}, u32[]{:S(2)}) collective-permute-start(bf16[2048,128]{1,0:T(8,128)(2,1)} %get-tuple-element.15), channel_id=1, source_target_pairs={{0,1},{4,5},{8,9},{12,13},{16,17},{20,21},{24,25},{28,29}} | collective-permute-start | bytes 1572872 | tf_op jit(solution)/shard_map/ppermute | solution.py:329
  52.7 11.6 %collective-permute-start.3 = (bf16[8,288,128]{2,1,0:T(8,128)(2,1)S(1)}, bf16[8,288,128]{2,1,0:T(8,128)(2,1)S(1)}, u32[]{:S(2)}, u32[]{:S(2)}) collective-permute-start(bf16[8,288,128]{2,1,0:T(8,128)(2,1)S(1)} %pad_maximum_fusion), channel_id=1, source_target_pairs={{0,8},{4,12},{8,0},{12,4},{16,24},{20,28},{24,16},{28,20},{1,9},{5... | collective-permute-start | bytes 1769480 | tf_op jit(solution)/shard_map/ppermute | solution.py:299
  55.0 10.2 %collective-permute-start.8 = (bf16[2,4,16,128]{3,2,1,0:T(8,128)(2,1)S(1)}, bf16[2,4,16,128]{3,2,1,0:T(8,128)(2,1)S(1)}, u32[]{:S(2)}, u32[]{:S(2)}) collective-permute-start(bf16[2,4,16,128]{3,2,1,0:T(8,128)(2,1)S(1)} %pad_maximum_fusion.5), channel_id=1, source_target_pairs={{0,8},{4,12},{8,0},{12,4},{16,24},{20,28},{24,16},{28,20},{1,9},{5... | collective-permute-start | bytes 98312 | tf_op jit(solution)/shard_map/ppermute | solution.py:299
  55.5 9.6 %copy-start.15 = (s32[32]{0:T(128)S(1)}, s32[32]{0:T(128)}, u32[]{:S(2)}) copy-start(s32[32]{0:T(128)} %constant.105.clone) | copy-start | bytes 388
  55.5 9.6 %copy-start.16 = (s32[32]{0:T(128)S(1)}, s32[32]{0:T(128)}, u32[]{:S(2)}) copy-start(s32[32]{0:T(128)} %constant.104.clone) | copy-start | bytes 388
  57.8 8.0 %copy-start.4 = (f32[1,2048,128]{2,1,0:T(8,128)S(1)}, f32[1,2048,128]{2,1,0:T(8,128)}, u32[]{:S(2)}) copy-start(f32[1,2048,128]{2,1,0:T(8,128)} %param.13) | copy-start | bytes 3145732
  57.8 19.9 %collective-permute-start.12 = (bf16[2048,128]{1,0:T(8,128)(2,1)}, bf16[2048,128]{1,0:T(8,128)(2,1)}, u32[]{:S(2)}, u32[]{:S(2)}) collective-permute-start(bf16[2048,128]{1,0:T(8,128)(2,1)} %add_convert_fusion), channel_id=1, source_target_pairs={{0,2},{1,3},{2,0},{3,1},{4,6},{5,7},{6,4},{7,5},{8,10},{9,11},{10,... | collective-permute-start | bytes 1572872 | tf_op jit(solution)/shard_map/ppermute | solution.py:336
  65.2 16.4 %collective-permute-start.4 = (bf16[16,288,128]{2,1,0:T(8,128)(2,1)}, bf16[16,288,128]{2,1,0:T(8,128)(2,1)S(1)}, u32[]{:S(2)}, u32[]{:S(2)}) collective-permute-start(bf16[16,288,128]{2,1,0:T(8,128)(2,1)} %constant_dynamic-update-slice_fusion.here_ref), channel_id=1, source_target_pairs={{0,4},{4,0},{8,12},{12,8},{16,20},{20,16},{24,28},{28,24},{1,5},{5... | collective-permute-start | bytes 3538952 | tf_op jit(solution)/shard_map/ppermute | solution.py:299
  65.2 2.5 %collective-permute-start.9 = (bf16[4,4,16,128]{3,2,1,0:T(8,128)(2,1)S(1)}, bf16[4,4,16,128]{3,2,1,0:T(8,128)(2,1)S(1)}, u32[]{:S(2)}, u32[]{:S(2)}) collective-permute-start(bf16[4,4,16,128]{3,2,1,0:T(8,128)(2,1)S(1)} %pad_maximum_fusion.4), channel_id=1, source_target_pairs={{0,4},{4,0},{8,12},{12,8},{16,20},{20,16},{24,28},{28,24},{1,5},{5... | collective-permute-start | bytes 196616 | tf_op jit(solution)/shard_map/ppermute | solution.py:299
  81.7 4.3 %copy-start.8 = (bf16[256,128]{1,0:T(8,128)(2,1)S(1)}, bf16[256,128]{1,0:T(8,128)(2,1)}, u32[]{:S(2)}) copy-start(bf16[256,128]{1,0:T(8,128)(2,1)} %constant.102.clone.fwd_ref) | copy-start | bytes 196612

commit v2 on v1

v2 whole, which is shorter than its diff:
```python
import functools

import jax
import jax.numpy as jnp
import numpy as np
from jax import lax
from jax.experimental import pallas as pl
from jax.experimental.pallas import tpu as pltpu
from jax.sharding import PartitionSpec as P

TILE = 64
LANES = 128

momentum_decay = 0.999
step_size = 0.005


def cosine_array(order):
    freq = np.arange(order, dtype=np.float64)[:, None]
    place = np.arange(order, dtype=np.float64)[None, :]
    table = np.sqrt(2.0 / order) * np.cos(np.pi * (2.0 * place + 1.0) * freq / (2.0 * order))
    return table * np.where(freq == 0.0, np.sqrt(0.5), 1.0)


def tables():
    block = np.kron(np.eye(2), cosine_array(TILE)).astype(np.float32)
    high = block.astype(jnp.bfloat16)
    low = (block - high.astype(np.float32)).astype(jnp.bfloat16)
    inv = np.concatenate([high.T, low.T], axis=0)
    fwd = np.concatenate([high, low], axis=0)
    return jnp.asarray(inv), jnp.asarray(fwd)


def split(x):
    high = x.astype(jnp.bfloat16)
    return high, (x - high.astype(jnp.float32)).astype(jnp.bfloat16)


def dot(a, b, contract=((1,), (0,))):
    return lax.dot_general(a, b, (contract, ((), ())), preferred_element_type=jnp.float32)


def hot(row, size, fill=None):
    spread = lambda x: jnp.broadcast_to(x, (16, LANES)).astype(jnp.bfloat16)
    place = spread(row)
    fill = jnp.ones((16, LANES), jnp.bfloat16) if fill is None else spread(fill)
    none = jnp.zeros((16, LANES), jnp.bfloat16)
    sub = lax.broadcasted_iota(jnp.int32, (16, LANES), 0).astype(jnp.float32)
    parts = [jnp.where((sub + 16.0 * i).astype(jnp.bfloat16) == place, fill, none) for i in range(size // 16)]
    return jnp.concatenate(parts, axis=0)


def partial_kernel(slots, tok, grad, *outs):
    for i, out in enumerate(outs):

        @pl.when(pl.program_id(0) == i)
        def _():
            out[...] = dot(tok[...], grad[...], ((0,), (0,))).astype(out.dtype)


def partial_chunks(tokens, grad_out, slots, rows):
    count = slots.shape[0]
    width = grad_out.shape[1]
    toks = tokens.shape[0]
    return pl.pallas_call(
        partial_kernel,
        grid_spec=pltpu.PrefetchScalarGridSpec(
            num_scalar_prefetch=1,
            grid=(count,),
            in_specs=[
                pl.BlockSpec((toks, rows), lambda s, slots: (0, slots[s])),
                pl.BlockSpec((toks, width), lambda s, slots: (0, 0)),
            ],
            out_specs=[pl.BlockSpec((rows, width), lambda s, slots: (0, 0)) for _ in range(count)],
        ),
        out_shape=[jax.ShapeDtypeStruct((rows, width), jnp.bfloat16) for _ in range(count)],
        cost_estimate=pl.CostEstimate(
            flops=2 * count * rows * width * toks, bytes_accessed=count * rows * (width + toks) * 2, transcendentals=0
        ),
        compiler_params=pltpu.CompilerParams(vmem_limit_bytes=32 * 2**20),
    )(slots, tokens, grad_out)


def entry_rows(inv, row, col):
    hots = jnp.concatenate([hot(row, LANES), hot(col, LANES)], axis=1)
    both = dot(inv, hots)
    return both[:LANES, :LANES], both[LANES:, :LANES], both[:LANES, LANES:], both[LANES:, LANES:]


def select_kernel(groups, me, inv_ref, idx_ref, tok_ref, grad_ref, moment_ref, out_ref):
    inv = inv_ref[...]
    grad = grad_ref[...]

    grad = jnp.concatenate([grad, grad], axis=1)
    places = idx_ref[0].astype(jnp.float32)

    def group(g, own):
        row = places[g : g + 1]
        col = places[groups + g : groups + g + 1]
        part = slice(g * LANES, (g + 1) * LANES)
        both = dot(inv, jnp.concatenate([hot(row, LANES), hot(col, LANES)], axis=1))
        a2 = both[:, :LANES].astype(jnp.bfloat16)
        b2 = both[:, LANES:].astype(jnp.bfloat16)
        tok = tok_ref[:, part]
        value = jnp.sum(dot(jnp.concatenate([tok, tok], axis=1), a2) * dot(grad, b2), axis=0, keepdims=True)
        if own:
            m_hi, m_lo = split(momentum_decay * moment_ref[part, :])
            mb = dot(jnp.concatenate([m_hi, m_hi], axis=1), b2) + dot(m_lo, b2[:LANES])
            value = value + jnp.sum(mb * (both[:LANES, :LANES] + both[LANES:, :LANES]), axis=0, keepdims=True)
        out_ref[0, g : g + 1, :] = value

    @pl.when(pl.program_id(0) == 0)
    def _():
        for g in range(groups):
            group(g, True)

    @pl.when(pl.program_id(0) != 0)
    def _():
        for g in range(groups):
            group(g, False)


def select_values(me, inv, idx, tokens, grad_out, moment):
    n_f = idx.shape[0]
    rows = moment.shape[0]
    groups = rows // LANES
    toks = tokens.shape[0]
    width = grad_out.shape[1]
    return pl.pallas_call(
        functools.partial(select_kernel, groups),
        grid_spec=pltpu.PrefetchScalarGridSpec(
            num_scalar_prefetch=1,
            grid=(n_f,),
            in_specs=[
                pl.BlockSpec(inv.shape, lambda s, me: (0, 0)),
                pl.BlockSpec((1, 2 * groups, LANES), lambda s, me: (s, 0, 0)),
                pl.BlockSpec((toks, rows), lambda s, me: (0, me[0] ^ s)),
                pl.BlockSpec((toks, width), lambda s, me: (0, 0)),
                pl.BlockSpec((rows, width), lambda s, me: (0, 0)),
            ],
            out_specs=pl.BlockSpec((1, groups, LANES), lambda s, me: (me[0] ^ s, 0, 0)),
        ),
        out_shape=jax.ShapeDtypeStruct((n_f, groups, LANES), jnp.float32),
        cost_estimate=pl.CostEstimate(
            flops=2 * n_f * groups * LANES**3 * 6, bytes_accessed=4 * 2**20, transcendentals=0
        ),
        compiler_params=pltpu.CompilerParams(vmem_limit_bytes=32 * 2**20),
    )(me, inv, idx, tokens, grad_out, moment)


def base_kernel(groups, me, inv_ref, idx_ref, val_ref, moment_ref, kept_ref, outer_ref, inner_ref, out_ref):
    inv = inv_ref[...]
    places = idx_ref[0].astype(jnp.float32)
    outer = (me[0] == 0) | (me[0] == me[1] - 1)
    for g in range(groups):
        a_hi, a_lo, b_hi, b_lo = entry_rows(inv, places[g : g + 1], places[groups + g : groups + g + 1])
        av_hi, av_lo = split((a_hi + a_lo) * val_ref[0, g : g + 1, :])
        left = jnp.concatenate([av_hi, av_hi, av_lo], axis=1)
        right = jnp.concatenate([b_hi, b_lo, b_hi], axis=1).astype(jnp.bfloat16)
        part = slice(g * LANES, (g + 1) * LANES)
        near = jnp.where(outer, outer_ref[part, :].astype(jnp.float32), inner_ref[part, :].astype(jnp.float32))
        got = kept_ref[part, :].astype(jnp.float32) + near
        out_ref[part, :] = (momentum_decay * moment_ref[part, :] + got) - dot(left, right, ((1,), (1,)))


def moment_base(me, inv, idx, values, moment, kept, outer, inner):
    groups = values.shape[1]
    rows, width = moment.shape
    slab = pl.BlockSpec((rows, width), lambda i, me: (0, 0))
    return pl.pallas_call(
        functools.partial(base_kernel, groups),
        grid_spec=pltpu.PrefetchScalarGridSpec(
            num_scalar_prefetch=1,
            grid=(1,),
            in_specs=[
                pl.BlockSpec(inv.shape, lambda i, me: (0, 0)),
                pl.BlockSpec((1, 2 * groups, LANES), lambda i, me: (0, 0, 0)),
                pl.BlockSpec((1, groups, LANES), lambda i, me: (me[0], 0, 0)),
                slab,
                slab,
                slab,
                slab,
            ],
            out_specs=slab,
        ),
        out_shape=jax.ShapeDtypeStruct((rows, width), jnp.float32),
        cost_estimate=pl.CostEstimate(
            flops=2 * groups * LANES**3 * 7, bytes_accessed=3 * rows * width * 4, transcendentals=0
        ),
        compiler_params=pltpu.CompilerParams(vmem_limit_bytes=32 * 2**20),
    )(me, inv, idx, values, moment, kept, outer, inner)


AWAY = (0, 4, 2, 6, 1, 5, 3, 7)


def project_kernel(n_r, n_f, extra, me, inv_ref, nt_ref, *refs):
    pieces, (out_ref, coef_ref) = refs[:n_r], refs[n_r:]
    width = nt_ref.shape[1]
    total = jnp.zeros(out_ref.shape, jnp.float32)
    size = width // (n_r * n_f)
    for away, piece in zip(AWAY, pieces):
        for p in range(n_f):
            place = (me[0] ^ p) * n_r + (me[2] ^ away)
            total += dot(nt_ref[:, pl.ds(pl.multiple_of(place * size, size), size)], piece[p, extra:, :])
    out_ref[...] = total
    inv = inv_ref[...]
    table = jnp.concatenate([inv[:LANES], inv[LANES:]], axis=1)
    for g in range(width // LANES):
        part = slice(g * LANES, (g + 1) * LANES)
        both = dot(nt_ref[:, part], table)
        coef_ref[:, part] = (both[:, :LANES] + both[:, LANES:]).astype(jnp.bfloat16)


def project(me, inv, next_tokens, pieces, extra):
    n_r, n_f = len(pieces), pieces[0].shape[0]
    toks, width = next_tokens.shape
    out = pieces[0].shape[2]
    full = lambda *shape: pl.BlockSpec(shape, lambda i, me: (0,) * len(shape))
    return pl.pallas_call(
        functools.partial(project_kernel, n_r, n_f, extra),
        grid_spec=pltpu.PrefetchScalarGridSpec(
            num_scalar_prefetch=1,
            grid=(1,),
            in_specs=[full(*inv.shape), full(toks, width)] + [full(*piece.shape) for piece in pieces],
            out_specs=[full(toks, out), full(toks, width)],
        ),
        out_shape=[jax.ShapeDtypeStruct((toks, out), jnp.float32), jax.ShapeDtypeStruct((toks, width), jnp.bfloat16)],
        cost_estimate=pl.CostEstimate(
            flops=2 * toks * width * out * 3, bytes_accessed=6 * toks * width * 2, transcendentals=0
        ),
        compiler_params=pltpu.CompilerParams(vmem_limit_bytes=48 * 2**20),
    )(me, inv, next_tokens, *pieces)


def total_kernel(groups, n_r, me, inv_ref, fwd_ref, coef_ref, base_ref, *refs):
    idx_refs, val_refs = refs[:n_r], refs[n_r : n_r + n_r // 2]
    up_ref, out_ref, acc_ref, sort_ref, dense_ref = refs[n_r + n_r // 2 :]
    step = pl.program_id(0)
    inv = inv_ref[...]
    fwd = fwd_ref[...]

    @pl.when(step == 0)
    def _():
        acc_ref[...] = jnp.zeros_like(acc_ref)

    lane = lax.broadcasted_iota(jnp.int32, (groups, LANES), 1)
    quarter = LANES // 4

    def regroup(parts):
        out = []
        for t in range(4):
            row = None
            for i, part in enumerate(parts):
                moved = part if i == t else pltpu.roll(part, (quarter * (i - t)) % LANES, 1)
                row = moved if row is None else jnp.where(lane // quarter == i, moved, row)
            out.append(row)
        return out

    for quad in range(n_r // 4):
        of = range(4 * quad, 4 * quad + 4)
        spots = [idx_refs[r][0].astype(jnp.int32) & (TILE - 1) for r in of]
        worth = [val_refs[r % (n_r // 2)][r // (n_r // 2), 0].astype(jnp.float32) for r in of]
        sets = regroup([x[:groups] for x in spots]), regroup([x[groups:] for x in spots]), regroup(worth)
        for kind, four in enumerate(sets):
            for t, rows in enumerate(four):
                sort_ref[kind, quad, t] = rows.astype(jnp.float32)

    def group(g):
        left, right = [], []
        for t in range(4):
            at = lambda kind, quad: sort_ref[kind, quad, t, pl.ds(g, 1), :]
            left.append(jnp.concatenate([hot(at(0, q), TILE) for q in range(n_r // 4)], axis=1))
            right.append(jnp.concatenate([hot(at(1, q), TILE, at(2, q)) for q in range(n_r // 4)], axis=1))
        cross = dot(jnp.concatenate(left, axis=0), jnp.concatenate(right, axis=0), ((1,), (1,)))
        low = lax.broadcasted_iota(jnp.int32, (TILE, LANES), 1) < TILE
        dense = jnp.concatenate(
            [
                jnp.where(low, cross[i : i + TILE, i : i + LANES], cross[i + TILE : i + LANES, i : i + LANES])
                for i in (0, LANES)
            ],
            axis=0,
        )
        q_hi, q_lo = split(dense)
        dense_ref[pl.ds(pl.multiple_of(g * LANES, LANES), LANES), :] = jnp.concatenate([q_hi, q_lo], axis=1)

    @pl.loop(0, groups, unroll=True)
    def _(g):
        group(g)

    both = dot(coef_ref[...], dense_ref[...])
    acc_ref[...] += both[:, :LANES] + both[:, LANES:]

    @pl.when(step == 0)
    def _():
        c_hi, c_lo = inv[:LANES], inv[LANES:]
        f_hi, f_lo = fwd[:LANES], fwd[LANES:]
        for g in range(groups):
            part = slice(g * LANES, (g + 1) * LANES)
            both = dot(jnp.concatenate([c_hi, c_lo], axis=1), jnp.concatenate([dense_ref[part, :], dense_ref[part, :]], axis=0))
            s_hi, s_lo = split(both[:, :LANES] + both[:, LANES:])
            up_ref[part, :] = dot(
                jnp.concatenate([s_hi, s_hi, s_lo], axis=1), jnp.concatenate([f_hi, f_lo, f_hi], axis=0)
            )

    @pl.when(step == pl.num_programs(0) - 1)
    def _():
        s_hi, s_lo = split(acc_ref[...])
        f_hi, f_lo = fwd[:LANES], fwd[LANES:]
        moved = dot(jnp.concatenate([s_hi, s_hi, s_lo], axis=1), jnp.concatenate([f_hi, f_lo, f_hi], axis=0))
        out_ref[...] = (base_ref[...] - step_size * moved).astype(out_ref.dtype)


def totals(me, inv, fwd, coef, base, pieces, sent):
    n_r, n_f = len(pieces), pieces[0].shape[0]
    groups = sent[0].shape[2]
    rows = groups * LANES
    toks, width = base.shape
    return pl.pallas_call(
        functools.partial(total_kernel, groups, n_r),
        grid_spec=pltpu.PrefetchScalarGridSpec(
            num_scalar_prefetch=1,
            grid=(n_f,),
            in_specs=[
                pl.BlockSpec(inv.shape, lambda s, me: (0, 0)),
                pl.BlockSpec(fwd.shape, lambda s, me: (0, 0)),
                pl.BlockSpec((toks, rows), lambda s, me: (0, me[0] ^ s)),
                pl.BlockSpec((toks, width), lambda s, me: (0, 0)),
            ]
            + [pl.BlockSpec((1, 2 * groups, LANES), lambda s, me: (s, 0, 0)) for _ in pieces]
            + [pl.BlockSpec((2, 1, groups, LANES), lambda s, me: (0, me[0] ^ s, 0, 0)) for _ in sent],
            out_specs=[
                pl.BlockSpec((rows, width), lambda s, me: (0, 0)),
                pl.BlockSpec((toks, width), lambda s, me: (0, 0)),
            ],
            scratch_shapes=[
                pltpu.VMEM((toks, width), jnp.float32),
                pltpu.VMEM((3, n_r // 4, 4, groups, LANES), jnp.float32),
                pltpu.VMEM((rows, 2 * LANES), jnp.bfloat16),
            ],
        ),
        out_shape=[
            jax.ShapeDtypeStruct((rows, width), jnp.float32),
            jax.ShapeDtypeStruct((toks, width), jnp.bfloat16),
        ],
        cost_estimate=pl.CostEstimate(
            flops=2 * n_f * groups * LANES**3 * (n_r + 2), bytes_accessed=4 * 2**20, transcendentals=0
        ),
        compiler_params=pltpu.CompilerParams(vmem_limit_bytes=32 * 2**20),
    )(me, inv, fwd, coef, base, *pieces, *sent)


def swap(x, axis, size, mask):
    return lax.ppermute(x, axis, [(i, i ^ mask) for i in range(size)])


def fence(stage, *args):
    shapes = jax.eval_shape(stage, *args)
    other = lambda *args: jax.tree.map(lambda x: jnp.zeros(x.shape, x.dtype), shapes)
    return lax.cond(lax.axis_index("rep") < lax.axis_size("rep"), stage, other, *args)


SLOTS = np.array([[3, 1, 2, 0], [0, 2, 3, 1], [3, 1, 0, 2], [0, 2, 1, 3]], np.int32)


def line_fast(n_r, n_f, tokens, grad_out, moment, weight, next_tokens, index):
    bf16 = jnp.bfloat16
    r, f = lax.axis_index("rep"), lax.axis_index("fsdp")
    me = jnp.stack([f, n_f, r]).astype(jnp.int32)
    inv, fwd = tables()
    moment = moment[0]
    rows = moment.shape[0]
    groups = rows // LANES
    slice_rows = rows // n_r

    flat = index[0].reshape(groups, LANES)
    lane = jnp.arange(LANES, dtype=jnp.int32)
    row_pos = flat // TILE + (lane // TILE) * TILE
    col_pos = flat % TILE + (lane // (TILE // 2)) % 2 * TILE
    own_idx = jnp.concatenate([row_pos, col_pos], axis=0).astype(bf16)
    extra = own_idx.shape[0]
    share = lax.dynamic_slice_in_dim(weight, r * slice_rows, slice_rows, axis=0)
    held = jnp.concatenate([own_idx, share], axis=0)[None]

    held = jnp.concatenate([held] + [swap(held, "fsdp", n_f, p) for p in range(1, n_f)], axis=0)
    slots = jnp.asarray(SLOTS)[f]
    first, second, third, kept = partial_chunks(tokens, grad_out, slots, rows)
    held, first, second = lax.optimization_barrier((held, first, second))
    outer = lax.ppermute(first, "fsdp", [(0, 1), (1, 0), (2, 3), (3, 2)])
    inner = lax.ppermute(second, "fsdp", [(1, 2), (2, 1)])

    def near_stage(held):
        pieces = [swap(held, "rep", n_r, away) for away in AWAY[1 : n_r // 2]]
        return select_values(me, inv, held, tokens, grad_out, moment), pieces

    values, pieces = fence(near_stage, held)
    pieces = [held] + pieces

    outer, inner = lax.optimization_barrier((outer, inner))

    def sum_stage(values, third, outer, pieces):
        parts = [swap(values, "fsdp", n_f, p) for p in range(1, n_f)]
        more = [swap(piece, "rep", n_r, 1) for piece in pieces]
        got = jnp.where((f == 1) | (f == 2), outer.astype(jnp.float32), 0.0)
        merged = (third.astype(jnp.float32) + got).astype(bf16)
        return sum(parts, values), more, merged

    values, more, merged = fence(sum_stage, values, third, outer, pieces)
    values, merged, second = lax.optimization_barrier((values, merged, second))
    two = lax.ppermute(merged, "fsdp", [(0, 2), (1, 3), (2, 0), (3, 1)])
    far = lax.ppermute(second, "fsdp", [(0, 1), (3, 2)])

    def far_stage(values, pieces, kept, outer, inner):
        sent = values.astype(bf16)[None]
        sent = jnp.concatenate([sent, swap(sent, "rep", n_r, 1)], axis=0)
        sents = [sent] + [swap(sent, "rep", n_r, away) for away in AWAY[1 : n_r // 2]]
        base = moment_base(me, inv, held, values, moment, kept, outer, inner)
        old_out, coef = project(me, inv, next_tokens, pieces, extra)
        return sents, base, old_out, coef

    pieces = pieces + more
    sents, base, old_out, coef = fence(far_stage, values, pieces, kept, outer, inner)
    update, next_out = totals(me, inv, fwd, coef, old_out, pieces, sents)
    grad = two.astype(jnp.float32) + far.astype(jnp.float32)
    return update, (base + grad)[None], next_out


def cosine_table(order):
    return jnp.asarray(cosine_array(order), jnp.float32)


def forward_tiles(field, table):
    side = table.shape[0]
    shard_rows, width = field.shape
    tiles = field.reshape(shard_rows // side, side, width)
    along = jnp.einsum("ab,ibc->iac", table, tiles, precision=lax.Precision.HIGHEST)
    block = jnp.kron(jnp.eye(width // side, dtype=jnp.float32), table.T)
    return jnp.matmul(along, block, precision=lax.Precision.HIGHEST)


def inverse_tiles(spectra, table):
    side = table.shape[0]
    width = spectra.shape[2]
    along = jnp.einsum("ab,iac->ibc", table, spectra, precision=lax.Precision.HIGHEST)
    block = jnp.kron(jnp.eye(width // side, dtype=jnp.float32), table)
    result = jnp.matmul(along, block, precision=lax.Precision.HIGHEST)
    return result.reshape(spectra.shape[0] * side, width)


def one_hots(places, side, width):
    row_of = places // side
    col_of = places % side + jnp.arange(width // side, dtype=jnp.int32)[:, None] * side
    row_hot = (row_of[..., None] == jnp.arange(side, dtype=jnp.int32)).astype(jnp.float32)
    col_hot = (col_of[..., None] == jnp.arange(width, dtype=jnp.int32)).astype(jnp.float32)
    return (row_hot, col_hot)


def any_mesh(tokens, grad_out, moment, weight, next_tokens, index):
    table = cosine_table(TILE)
    width = weight.shape[1]
    partial = lax.dot_general(tokens, grad_out, (((0,), (0,)), ((), ())), preferred_element_type=jnp.float32)
    grad = lax.psum_scatter(partial.astype(jnp.bfloat16), "fsdp", scatter_dimension=0, tiled=True)
    moment_now = momentum_decay * moment[0] + grad.astype(jnp.float32)
    spectra = forward_tiles(moment_now, table)
    row_hot, col_hot = one_hots(index[0], TILE, width)
    picked = jnp.einsum("ijka,iac->ijkc", row_hot, spectra, precision=lax.Precision.HIGHEST)
    values = jnp.sum(picked * col_hot, axis=-1)
    dense = jnp.einsum("ijka,ijkc->iac", row_hot * values[..., None], col_hot, precision=lax.Precision.HIGHEST)
    new_moment = (moment_now - inverse_tiles(dense, table))[None]
    total = lax.psum(dense.astype(jnp.bfloat16), "rep").astype(jnp.float32)
    update = inverse_tiles(total, table)
    new_weight = (weight.astype(jnp.float32) - step_size * update).astype(jnp.bfloat16)
    full = lax.all_gather(new_weight, "fsdp", axis=0, tiled=True)
    next_out = jnp.dot(next_tokens, full, preferred_element_type=jnp.float32).astype(jnp.bfloat16)
    return (update, new_moment, next_out)


def solution(mesh):
    n_r, n_f = mesh.shape["rep"], mesh.shape["fsdp"]
    local = functools.partial(line_fast, n_r, n_f) if (n_r, n_f) == (8, 4) else any_mesh
    in_specs = (
        P(("rep", "fsdp"), None),
        P(("rep", "fsdp"), None),
        P("rep", "fsdp", None),
        P("fsdp", None),
        P(("rep", "fsdp"), None),
        P("rep", "fsdp", None, None),
    )
    out_specs = (P("fsdp", None), P("rep", "fsdp", None), P(("rep", "fsdp"), None))
    return jax.shard_map(local, mesh=mesh, in_specs=in_specs, out_specs=out_specs, check_vma=False)
```

time: 120 us -> 71.8 us (0.60)
  waiting for transfers between devices: 22.7 us -> 3.56 us
  Pallas kernels: 52.2 us -> 33.2 us
  local copies, waits for them, and re-layouts: 10.2 us -> 1.72 us
  starting transfers between devices: 27.5 us -> 26.1 us
    pallas_call x1, Pallas kernels: 33.7 us -> 10.3 us  [totals(): pl.pallas_call(functools.partial(total_kernel, groups, n_r), grid_spec=pl...]
    ppermute x1, waiting for transfers between devices: 9.94 us -> 0.01 us  [line_fast(): two = lax.ppermute(merged, 'fsdp', [(0, 2), (1, 3), (2, 0), (3, 1)])]
    ppermute x10 -> x17, waiting for transfers between devices: 12.7 us -> 3.55 us  [swap(): return lax.ppermute(x, axis, [(i, i ^ mask) for i in range(size)])]
    unnamed x37 -> x8, local copies, waits for them, and re-layouts: 6.73 us -> 0.04 us
    ppermute x4 -> x3, starting transfers between devices: 9.29 us -> 5.34 us  [the longest x1 2.6 us: line_fast(): far = lax.ppermute(second, 'fsdp', [(0, 1), (3, 2)])]
    ppermute x1, starting transfers between devices: 0.01 us -> 2.53 us  [line_fast(): two = lax.ppermute(merged, 'fsdp', [(0, 2), (1, 3), (2, 0), (3, 1)])]
    pallas_call x2, Pallas kernels: 5.68 us -> 7.81 us  [the longest x1 4.48 us: project(): pl.pallas_call(functools.partial(project_kernel, n_r, n_f, extra), grid_s...]
    pallas_call x2 -> x1, Pallas kernels: 3.64 us -> 4.7 us  [partial_chunks(): pl.pallas_call(partial_kernel, grid_spec=pltpu.PrefetchScalarGridSpec(num...]
  transfers between devices with their start and end apart: 15 -> 21, of which waited for: 5 -> 4; matrix products, arithmetic and copies ran while one was open for 10% -> 6% of each run, Pallas kernels for 12% -> 47%
where the time goes in v2:
time: 71.8 us; the launch traced here: 71.3 us
  Pallas kernels  33.2 us (46%)
  starting transfers between devices  26.1 us (36%)
  other arithmetic  5.85 us (8%)
  waiting for transfers between devices  3.56 us (5%)
  local copies, waits for them, and re-layouts  1.72 us (2%)
  between operations  0.72 us (1%)
    ppermute x17, starting transfers between devices, swap(): return lax.ppermute(x, axis, [(i, i ^ mask) for i in range(size)])  18.3 us
    pallas_call x1, Pallas kernels, select_values(): pl.pallas_call(functools.partial(select_kernel, groups), grid_spec=pltpu....  10.3 us
    pallas_call x1, Pallas kernels, totals(): pl.pallas_call(functools.partial(total_kernel, groups, n_r), grid_spec=pl...  10.3 us
    pallas_call x1, Pallas kernels, partial_chunks(): pl.pallas_call(partial_kernel, grid_spec=pltpu.PrefetchScalarGridSpec(num...  4.7 us
    pallas_call x1, Pallas kernels, project(): pl.pallas_call(functools.partial(project_kernel, n_r, n_f, extra), grid_s...  4.48 us
    ppermute x17, waiting for transfers between devices, swap(): return lax.ppermute(x, axis, [(i, i ^ mask) for i in range(size)])  3.55 us
    pallas_call x1, Pallas kernels, moment_base(): pl.pallas_call(functools.partial(base_kernel, groups), grid_spec=pltpu.Pr...  3.34 us
    ppermute x1, starting transfers between devices, line_fast(): far = lax.ppermute(second, 'fsdp', [(0, 1), (3, 2)])  2.6 us
  transfers between devices with their start and end apart: 21, of which 4 were waited for; matrix products, arithmetic and copies ran while one was open for 6% of the time, Pallas kernels for 47%

profile of v2, /device:TPU:0, one launch (start us, length us, event | category | flops | bytes accessed | tf_op | source)
XLA Modules:
  0.0 71.3 jit_solution(702728113991392073)
XLA Ops:
  0.6 0.0 copy-start
  0.6 0.0 copy-start.5
  0.7 1.0 %reshape_squeeze.3 = s32[16,128]{1,0:T(8,128)S(1)} reshape(s32[1,32,2,32]{3,2,1,0:T(2,128)} %param.20) | data formatting | bytes 16384 | tf_op jit(solution)/shard_map/reshape;squeeze | solution.py:376
  1.7 0.0 copy-done
  1.7 5.1 %collective-permute-start.16 = (bf16[1,288,128]{2,1,0:T(8,128)(2,1)S(1)}, bf16[1,288,128]{2,1,0:T(8,128)(2,1)S(1)}, u32[]{:S(2)}, u32[]{:S(2)}) collective-permute-start(bf16[1,288,128]{2,1,0:T(8,128)(2,1)S(1)} %maximum_bitcast_fusion), channel_id=1, source_target_pairs={{0,3},{1,2},{2,1},{3,0},{4,7},{5,6},{6,5},{7,4},{8,11},{9,10},{10,... | collective-permute-start | bytes 221192 | tf_op jit(solution)/shard_map/ppermute | solution.py:354
  6.8 0.0 collective-permute-start.15
  6.8 0.6 collective-permute-start.14
  7.5 0.7 dynamic-slice_bitcast_fusion.slots
  8.2 4.7 %shard_map.113 = (bf16[2048,128]{1,0:T(8,128)(2,1)S(1)}, bf16[2048,128]{1,0:T(8,128)(2,1)S(1)}, bf16[2048,128]{1,0:T(8,128)(2,1)}, bf16[2048,128]{1,0:T(8,128)(2,1)}) custom-call(s32[4]{0:T(128)S(1)} %dynamic-slice_bitcast_fusion.slots, bf16[128,8192]{1,0:T(8,128)(2,1)} %tok.1, bf16[128,128]{1,0:T(8,128)(2,1)} %grad.1), custom_call_target="tpu_custom_call" | custom-call | flops 268435456 | bytes 4194304 | tf_op jit(solution)/shard_map/pallas_call | solution.py:65
  12.9 0.2 collective-permute-done.15
  13.1 0.0 collective-permute-done.14
  13.1 1.3 %collective-permute-start.17 = (bf16[2048,128]{1,0:T(8,128)(2,1)S(1)}, bf16[2048,128]{1,0:T(8,128)(2,1)S(1)}, u32[]{:S(2)}, u32[]{:S(2)}) collective-permute-start(bf16[2048,128]{1,0:T(8,128)(2,1)S(1)} %get-tuple-element.134), channel_id=1, source_target_pairs={{0,1},{1,0},{2,3},{3,2},{4,5},{5,4},{6,7},{7,6},{8,9},{9,8},{10,11... | collective-permute-start | bytes 1572872 | tf_op jit(solution)/shard_map/ppermute | solution.py:389
  14.4 1.5 %collective-permute-start.18 = (bf16[2048,128]{1,0:T(8,128)(2,1)S(1)}, bf16[2048,128]{1,0:T(8,128)(2,1)}, u32[]{:S(2)}, u32[]{:S(2)}) collective-permute-start(bf16[2048,128]{1,0:T(8,128)(2,1)S(1)} %get-tuple-element.155), channel_id=1, source_target_pairs={{1,2},{2,1},{5,6},{6,5},{9,10},{10,9},{13,14},{14,13},{17,18},{18,... | collective-permute-start | bytes 1572872 | tf_op jit(solution)/shard_map/ppermute | solution.py:390
  15.8 0.1 pad_add_fusion.me
  15.9 15.4 %conditional.3 = (f32[4,16,128]{2,1,0:T(8,128)S(1)}, bf16[4,288,128]{2,1,0:T(8,128)(2,1)}, bf16[4,288,128]{2,1,0:T(8,128)(2,1)}, bf16[4,288,128]{2,1,0:T(8,128)(2,1)}) conditional(s32[]{:T(128)} %convert_element_type.24, () %tuple.37, (s32[3]{0:T(128)S(1)}, bf16[256,128]{1,0:T(8,128)(2,1)S(1)}, bf16[4,288,128]{2,1,0:T(8,128)(2,1)S(1)}, ...), branch_computations={%region_0.1_spmd, %region_1.2_spmd} | conditional | flops 1610612736 | bytes 7733400 | solution.py:360
  15.9 2.5 %collective-permute-start.2 = (bf16[4,288,128]{2,1,0:T(8,128)(2,1)S(1)}, bf16[4,288,128]{2,1,0:T(8,128)(2,1)}, u32[]{:S(2)}, u32[]{:S(2)}) collective-permute-start(bf16[4,288,128]{2,1,0:T(8,128)(2,1)S(1)} %get-tuple-element.62.idx_ref), channel_id=1, source_target_pairs={{0,24},{4,28},{8,16},{12,20},{16,8},{20,12},{24,0},{28,4},{1,25},{... | collective-permute-start | bytes 884744 | tf_op jit(solution)/shard_map/cond/branch_1_fun/ppermute | solution.py:354
  18.4 0.5 collective-permute-start.1
  19.0 0.5 collective-permute-start
  19.4 10.3 %branch_1_fun.3 = f32[4,16,128]{2,1,0:T(8,128)S(1)} custom-call(s32[3]{0:T(128)S(1)} %get-tuple-element.60.me, bf16[256,128]{1,0:T(8,128)(2,1)S(1)} %get-tuple-element.61.inv_ref, bf16[4,288,128]{2,1,0:T(8,128)(2,1)S(1)} %get-tuple-element.62.idx_ref, bf16[128,8192]{1,0:T(8,128)(2,1)} %get-tuple-element.63.tok_ref, ...), custom_call_target="tpu_custom_call" | custom-call | flops 1610612736 | bytes 4194304 | tf_op jit(solution)/shard_map/cond/branch_1_fun/pallas_call | solution.py:129
  29.8 0.0 collective-permute-done.2
  29.8 1.5 %collective-permute-done.1 = bf16[4,288,128]{2,1,0:T(8,128)(2,1)} collective-permute-done((bf16[4,288,128]{2,1,0:T(8,128)(2,1)S(1)}, bf16[4,288,128]{2,1,0:T(8,128)(2,1)}, u32[]{:S(2)}, u32[]{:S(2)}) %collective-permute-start.1) | collective-permute-done | bytes 294944 | tf_op jit(solution)/shard_map/cond/branch_1_fun/ppermute | solution.py:354
  31.3 0.0 collective-permute-done.17
  31.3 10.1 %conditional.4 = (f32[4,16,128]{2,1,0:T(8,128)S(1)}, bf16[4,288,128]{2,1,0:T(8,128)(2,1)}, bf16[4,288,128]{2,1,0:T(8,128)(2,1)}, bf16[4,288,128]{2,1,0:T(8,128)(...) conditional(s32[]{:T(128)} %convert_element_type.24, () %tuple.36, (f32[4,16,128]{2,1,0:T(8,128)S(1)}, ...), branch_computations={%region_2.3_spmd, %region_3.4_spmd} | conditional | flops 1335299 | bytes 6979962 | solution.py:360
  31.3 0.0 copy-start.6
  31.3 2.4 %collective-permute-start.5 = (f32[4,16,128]{2,1,0:T(8,128)S(1)}, f32[4,16,128]{2,1,0:T(8,128)S(1)}, u32[]{:S(2)}, u32[]{:S(2)}) collective-permute-start(f32[4,16,128]{2,1,0:T(8,128)S(1)} %get-tuple-element.66), channel_id=1, source_target_pairs={{0,3},{1,2},{2,1},{3,0},{4,7},{5,6},{6,5},{7,4},{8,11},{9,10},{10,... | collective-permute-start | bytes 98312 | tf_op jit(solution)/shard_map/cond/branch_1_fun/ppermute | solution.py:354
  33.8 2.5 %collective-permute-start.4 = (f32[4,16,128]{2,1,0:T(8,128)S(1)}, f32[4,16,128]{2,1,0:T(8,128)S(1)}, u32[]{:S(2)}, u32[]{:S(2)}) collective-permute-start(f32[4,16,128]{2,1,0:T(8,128)S(1)} %get-tuple-element.66), channel_id=1, source_target_pairs={{0,2},{1,3},{2,0},{3,1},{4,6},{5,7},{6,4},{7,5},{8,10},{9,11},{10,... | collective-permute-start | bytes 98312 | tf_op jit(solution)/shard_map/cond/branch_1_fun/ppermute | solution.py:354
  36.2 0.0 collective-permute-start.3
  36.2 0.0 collective-permute-start.6
  36.2 0.5 collective-permute-start.7
  36.8 0.4 collective-permute-done.5
  37.1 1.5 %collective-permute-done.4 = f32[4,16,128]{2,1,0:T(8,128)S(1)} collective-permute-done((f32[4,16,128]{2,1,0:T(8,128)S(1)}, f32[4,16,128]{2,1,0:T(8,128)S(1)}, u32[]{:S(2)}, u32[]{:S(2)}) %collective-permute-start.4) | collective-permute-done | bytes 32800 | tf_op jit(solution)/shard_map/cond/branch_1_fun/ppermute | solution.py:354
  38.6 0.0 collective-permute-start.9
  38.6 2.0 %add_convert_fusion = bf16[2048,128]{1,0:T(8,128)(2,1)} fusion(bf16[2048,128]{1,0:T(8,128)(2,1)S(1)} %get-tuple-element.73, bf16[2048,128]{1,0:T(8,128)(2,1)} %get-tuple-element.71, pred[]{:T(512)S(6)} %or.2), kind=kLoop, calls=%fused_computation | loop fusion | flops 1310720 | bytes 1572865 | tf_op jit(solution)/shard_map/cond/branch_1_fun/convert_element_type | solution.py:405
  40.6 0.8 %add_add_fusion = f32[4,16,128]{2,1,0:T(8,128)S(1)} fusion(f32[4,16,128]{2,1,0:T(8,128)S(1)} %collective-permute-done.5, f32[4,16,128]{2,1,0:T(8,128)S(1)} %collective-permute-done.4, f32[4,16,128]{2,1,0:T(8,128)} %copy-done.6, f32[4,16,128]{2,1,0:T(8,128)S(1)} %collective-permute-done.3), kind=kLoop, calls=%fused_computation.1 | loop fusion | flops 24576 | bytes 163840 | tf_op jit(solution)/shard_map/cond/branch_1_fun/add | solution.py:406
  41.4 2.5 %collective-permute-start.19 = (bf16[2048,128]{1,0:T(8,128)(2,1)}, bf16[2048,128]{1,0:T(8,128)(2,1)}, u32[]{:S(2)}, u32[]{:S(2)}) collective-permute-start(bf16[2048,128]{1,0:T(8,128)(2,1)} %get-tuple-element.154), channel_id=1, source_target_pairs={{0,2},{1,3},{2,0},{3,1},{4,6},{5,7},{6,4},{7,5},{8,10},{9,11},{10,... | collective-permute-start | bytes 1572872 | tf_op jit(solution)/shard_map/ppermute | solution.py:410
  44.0 2.6 %collective-permute-start.20 = (bf16[2048,128]{1,0:T(8,128)(2,1)S(1)}, bf16[2048,128]{1,0:T(8,128)(2,1)}, u32[]{:S(2)}, u32[]{:S(2)}) collective-permute-start(bf16[2048,128]{1,0:T(8,128)(2,1)S(1)} %get-tuple-element.155), channel_id=1, source_target_pairs={{0,1},{3,2},{4,5},{7,6},{8,9},{11,10},{12,13},{15,14},{16,17},{19,... | collective-permute-start | bytes 1572872 | tf_op jit(solution)/shard_map/ppermute | solution.py:411
  46.6 12.1 %conditional.5 = (bf16[2,4,16,128]{3,2,1,0:T(8,128)(2,1)}, bf16[2,4,16,128]{3,2,1,0:T(8,128)(2,1)}, bf16[2,4,16,128]{3,2,1,0:T(8,128)(2,1)}, bf16[2,4,16,128]{3,...) conditional(s32[]{:T(128)} %convert_element_type.24, () %tuple.35, ...), branch_computations={%region_4.5_spmd, %region_5.6_spmd} | conditional | flops 1275092992 | bytes 22593808 | solution.py:360
  46.6 0.1 collective-permute-start.10
  46.7 0.0 copy-start.4
  46.7 4.5 %branch_1_fun.5 = (f32[128,128]{1,0:T(8,128)S(1)}, bf16[128,8192]{1,0:T(8,128)(2,1)S(1)}) custom-call(s32[3]{0:T(128)S(1)} %get-tuple-element.75.me, bf16[256,128]{1,0:T(8,128)(2,1)S(1)} %get-tuple-element.76.inv_ref, bf16[128,8192]{1,0:T(8,128)(2,1)} %get-tuple-element.158.nt_ref, bf16[4,288,128]{2,1,0:T(8,128)(2,1)S(1)} %get-tuple-element.77.idx_ref.refs_0_, ...), custom_call_target="tpu_custom_call" | custom-call | flops 805306368 | bytes 12582912 | tf_op jit(solution)/shard_map/cond/branch_1_fun/pallas_call | solution.py:220
  51.2 0.6 pad_maximum_fusion
  51.8 2.1 %collective-permute-start.13 = (bf16[2,4,16,128]{3,2,1,0:T(8,128)(2,1)}, bf16[2,4,16,128]{3,2,1,0:T(8,128)(2,1)}, u32[]{:S(2)}, u32[]{:S(2)}) collective-permute-start(bf16[2,4,16,128]{3,2,1,0:T(8,128)(2,1)} %pad_maximum_fusion), channel_id=1, source_target_pairs={{0,24},{4,28},{8,16},{12,20},{16,8},{20,12},{24,0},{28,4},{1,25},{... | collective-permute-start | bytes 98312 | tf_op jit(solution)/shard_map/cond/branch_1_fun/ppermute | solution.py:354
  53.9 0.5 collective-permute-start.12
  54.4 0.8 %collective-permute-start.11 = (bf16[2,4,16,128]{3,2,1,0:T(8,128)(2,1)}, bf16[2,4,16,128]{3,2,1,0:T(8,128)(2,1)}, u32[]{:S(2)}, u32[]{:S(2)}) collective-permute-start(bf16[2,4,16,128]{3,2,1,0:T(8,128)(2,1)} %pad_maximum_fusion), channel_id=1, source_target_pairs={{0,16},{4,20},{8,24},{12,28},{16,0},{20,4},{24,8},{28,12},{1,17},{... | collective-permute-start | bytes 98312 | tf_op jit(solution)/shard_map/cond/branch_1_fun/ppermute | solution.py:354
  55.3 3.3 %branch_1_fun.4 = f32[2048,128]{1,0:T(8,128)S(1)} custom-call(s32[3]{0:T(128)S(1)} %get-tuple-element.75.me, bf16[256,128]{1,0:T(8,128)(2,1)S(1)} %get-tuple-element.76.inv_ref, bf16[4,288,128]{2,1,0:T(8,128)(2,1)S(1)} %get-tuple-element.77.idx_ref.refs_0_, f32[4,16,128]{2,1,0:T(8,128)S(1)} %get-tuple-element.74.val_ref, f32[2048,128]{1,0:T(8,128)} %copy-done.3, ...), custom_call_target="tpu_custom_call" | custom-call | flops 469762048 | bytes 3145728 | tf_op jit(solution)/shard_map/cond/branch_1_fun/pallas_call | solution.py:170
  58.6 0.0 collective-permute-done.11
  58.6 10.3 %shard_map.114 = (f32[2048,128]{1,0:T(8,128)}, bf16[128,128]{1,0:T(8,128)(2,1)}) custom-call(s32[3]{0:T(128)S(1)} %pad_add_fusion.me, bf16[256,128]{1,0:T(8,128)(2,1)S(1)} %copy-done.5, bf16[256,128]{1,0:T(8,128)(2,1)S(1)} %copy-done.1, bf16[128,8192]{1,0:T(8,128)(2,1)S(1)} %get-tuple-element.146.coef_ref, f32[128,128]{1,0:T(8,128)S(1)} %get-tuple-element.147.base_ref, ...), custom_call_target="tpu_custom_call" | custom-call | flops 2684354560 | bytes 4194304 | tf_op jit(solution)/shard_map/pallas_call | solution.py:319
  69.0 2.3 %add_bitcast_fusion = f32[1,2048,128]{2,1,0:T(8,128)} fusion(f32[2048,128]{1,0:T(8,128)S(1)} %get-tuple-element.153, bf16[2048,128]{1,0:T(8,128)(2,1)} %collective-permute-done.20, bf16[2048,128]{1,0:T(8,128)(2,1)} %collective-permute-done.19), kind=kLoop, calls=%fused_computation.4 | loop fusion | flops 1048576 | bytes 3145728 | tf_op jit(solution)/shard_map/broadcast_in_dim | solution.py:425
  (29 shorter events, 0.1 us)
Async XLA Ops:
  0.6 1.0 %copy-start = (bf16[2048,128]{1,0:T(8,128)(2,1)S(1)}, bf16[2048,128]{1,0:T(8,128)(2,1)}, u32[]{:S(2)}) copy-start(bf16[2048,128]{1,0:T(8,128)(2,1)} %param.18) | copy-start | bytes 1572868
  0.6 15.3 %copy-start.5 = (bf16[256,128]{1,0:T(8,128)(2,1)S(1)}, bf16[256,128]{1,0:T(8,128)(2,1)}, u32[]{:S(2)}) copy-start(bf16[256,128]{1,0:T(8,128)(2,1)} %constant.113.clone.inv_ref) | copy-start | bytes 196612
  0.7 15.3 %copy-start.2 = (f32[1,2048,128]{2,1,0:T(8,128)S(1)}, f32[1,2048,128]{2,1,0:T(8,128)}, u32[]{:S(2)}) copy-start(f32[1,2048,128]{2,1,0:T(8,128)} %param.17) | copy-start | bytes 3145732
  1.7 11.2 %collective-permute-start.16 = (bf16[1,288,128]{2,1,0:T(8,128)(2,1)S(1)}, bf16[1,288,128]{2,1,0:T(8,128)(2,1)S(1)}, u32[]{:S(2)}, u32[]{:S(2)}) collective-permute-start(bf16[1,288,128]{2,1,0:T(8,128)(2,1)S(1)} %maximum_bitcast_fusion), channel_id=1, source_target_pairs={{0,3},{1,2},{2,1},{3,0},{4,7},{5,6},{6,5},{7,4},{8,11},{9,10},{10,... | collective-permute-start | bytes 221192 | tf_op jit(solution)/shard_map/ppermute | solution.py:354
  6.8 6.2 %collective-permute-start.15 = (bf16[1,288,128]{2,1,0:T(8,128)(2,1)S(1)}, bf16[1,288,128]{2,1,0:T(8,128)(2,1)S(1)}, u32[]{:S(2)}, u32[]{:S(2)}) collective-permute-start(bf16[1,288,128]{2,1,0:T(8,128)(2,1)S(1)} %maximum_bitcast_fusion), channel_id=1, source_target_pairs={{0,2},{1,3},{2,0},{3,1},{4,6},{5,7},{6,4},{7,5},{8,10},{9,11},{10,... | collective-permute-start | bytes 221192 | tf_op jit(solution)/shard_map/ppermute | solution.py:354
  6.8 6.2 %collective-permute-start.14 = (bf16[1,288,128]{2,1,0:T(8,128)(2,1)S(1)}, bf16[1,288,128]{2,1,0:T(8,128)(2,1)S(1)}, u32[]{:S(2)}, u32[]{:S(2)}) collective-permute-start(bf16[1,288,128]{2,1,0:T(8,128)(2,1)S(1)} %maximum_bitcast_fusion), channel_id=1, source_target_pairs={{0,1},{1,0},{2,3},{3,2},{4,5},{5,4},{6,7},{7,6},{8,9},{9,8},{10,11... | collective-permute-start | bytes 221192 | tf_op jit(solution)/shard_map/ppermute | solution.py:354
  13.1 18.2 %collective-permute-start.17 = (bf16[2048,128]{1,0:T(8,128)(2,1)S(1)}, bf16[2048,128]{1,0:T(8,128)(2,1)S(1)}, u32[]{:S(2)}, u32[]{:S(2)}) collective-permute-start(bf16[2048,128]{1,0:T(8,128)(2,1)S(1)} %get-tuple-element.134), channel_id=1, source_target_pairs={{0,1},{1,0},{2,3},{3,2},{4,5},{5,4},{6,7},{7,6},{8,9},{9,8},{10,11... | collective-permute-start | bytes 1572872 | tf_op jit(solution)/shard_map/ppermute | solution.py:389
  14.4 16.9 %collective-permute-start.18 = (bf16[2048,128]{1,0:T(8,128)(2,1)S(1)}, bf16[2048,128]{1,0:T(8,128)(2,1)}, u32[]{:S(2)}, u32[]{:S(2)}) collective-permute-start(bf16[2048,128]{1,0:T(8,128)(2,1)S(1)} %get-tuple-element.155), channel_id=1, source_target_pairs={{1,2},{2,1},{5,6},{6,5},{9,10},{10,9},{13,14},{14,13},{17,18},{18,... | collective-permute-start | bytes 1572872 | tf_op jit(solution)/shard_map/ppermute | solution.py:390
  15.9 13.9 %collective-permute-start.2 = (bf16[4,288,128]{2,1,0:T(8,128)(2,1)S(1)}, bf16[4,288,128]{2,1,0:T(8,128)(2,1)}, u32[]{:S(2)}, u32[]{:S(2)}) collective-permute-start(bf16[4,288,128]{2,1,0:T(8,128)(2,1)S(1)} %get-tuple-element.62.idx_ref), channel_id=1, source_target_pairs={{0,24},{4,28},{8,16},{12,20},{16,8},{20,12},{24,0},{28,4},{1,25},{... | collective-permute-start | bytes 884744 | tf_op jit(solution)/shard_map/cond/branch_1_fun/ppermute | solution.py:354
  18.4 12.9 %collective-permute-start.1 = (bf16[4,288,128]{2,1,0:T(8,128)(2,1)S(1)}, bf16[4,288,128]{2,1,0:T(8,128)(2,1)}, u32[]{:S(2)}, u32[]{:S(2)}) collective-permute-start(bf16[4,288,128]{2,1,0:T(8,128)(2,1)S(1)} %get-tuple-element.62.idx_ref), channel_id=1, source_target_pairs={{0,8},{4,12},{8,0},{12,4},{16,24},{20,28},{24,16},{28,20},{1,9},{5... | collective-permute-start | bytes 884744 | tf_op jit(solution)/shard_map/cond/branch_1_fun/ppermute | solution.py:354
  19.0 12.3 %collective-permute-start = (bf16[4,288,128]{2,1,0:T(8,128)(2,1)S(1)}, bf16[4,288,128]{2,1,0:T(8,128)(2,1)}, u32[]{:S(2)}, u32[]{:S(2)}) collective-permute-start(bf16[4,288,128]{2,1,0:T(8,128)(2,1)S(1)} %get-tuple-element.62.idx_ref), channel_id=1, source_target_pairs={{0,16},{4,20},{8,24},{12,28},{16,0},{20,4},{24,8},{28,12},{1,17},{... | collective-permute-start | bytes 884744 | tf_op jit(solution)/shard_map/cond/branch_1_fun/ppermute | solution.py:354
  31.3 9.3 %copy-start.6 = (f32[4,16,128]{2,1,0:T(8,128)}, f32[4,16,128]{2,1,0:T(8,128)S(1)}, u32[]{:S(2)}) copy-start(f32[4,16,128]{2,1,0:T(8,128)S(1)} %get-tuple-element.66) | copy-start | bytes 98308 | tf_op jit(solution)/shard_map/cond
  31.3 5.8 %collective-permute-start.5 = (f32[4,16,128]{2,1,0:T(8,128)S(1)}, f32[4,16,128]{2,1,0:T(8,128)S(1)}, u32[]{:S(2)}, u32[]{:S(2)}) collective-permute-start(f32[4,16,128]{2,1,0:T(8,128)S(1)} %get-tuple-element.66), channel_id=1, source_target_pairs={{0,3},{1,2},{2,1},{3,0},{4,7},{5,6},{6,5},{7,4},{8,11},{9,10},{10,... | collective-permute-start | bytes 98312 | tf_op jit(solution)/shard_map/cond/branch_1_fun/ppermute | solution.py:354
  33.8 4.8 %collective-permute-start.4 = (f32[4,16,128]{2,1,0:T(8,128)S(1)}, f32[4,16,128]{2,1,0:T(8,128)S(1)}, u32[]{:S(2)}, u32[]{:S(2)}) collective-permute-start(f32[4,16,128]{2,1,0:T(8,128)S(1)} %get-tuple-element.66), channel_id=1, source_target_pairs={{0,2},{1,3},{2,0},{3,1},{4,6},{5,7},{6,4},{7,5},{8,10},{9,11},{10,... | collective-permute-start | bytes 98312 | tf_op jit(solution)/shard_map/cond/branch_1_fun/ppermute | solution.py:354
  36.2 4.4 %collective-permute-start.3 = (f32[4,16,128]{2,1,0:T(8,128)S(1)}, f32[4,16,128]{2,1,0:T(8,128)S(1)}, u32[]{:S(2)}, u32[]{:S(2)}) collective-permute-start(f32[4,16,128]{2,1,0:T(8,128)S(1)} %get-tuple-element.66), channel_id=1, source_target_pairs={{0,1},{1,0},{2,3},{3,2},{4,5},{5,4},{6,7},{7,6},{8,9},{9,8},{10,11... | collective-permute-start | bytes 98312 | tf_op jit(solution)/shard_map/cond/branch_1_fun/ppermute | solution.py:354
  36.2 5.2 %collective-permute-start.6 = (bf16[4,288,128]{2,1,0:T(8,128)(2,1)S(1)}, bf16[4,288,128]{2,1,0:T(8,128)(2,1)}, u32[]{:S(2)}, u32[]{:S(2)}) collective-permute-start(bf16[4,288,128]{2,1,0:T(8,128)(2,1)S(1)} %get-tuple-element.67), channel_id=1, source_target_pairs={{0,4},{4,0},{8,12},{12,8},{16,20},{20,16},{24,28},{28,24},{1,5},{5... | collective-permute-start | bytes 884744 | tf_op jit(solution)/shard_map/cond/branch_1_fun/ppermute | solution.py:354
  36.2 5.2 %collective-permute-start.7 = (bf16[4,288,128]{2,1,0:T(8,128)(2,1)}, bf16[4,288,128]{2,1,0:T(8,128)(2,1)}, u32[]{:S(2)}, u32[]{:S(2)}) collective-permute-start(bf16[4,288,128]{2,1,0:T(8,128)(2,1)} %get-tuple-element.68), channel_id=1, source_target_pairs={{0,4},{4,0},{8,12},{12,8},{16,20},{20,16},{24,28},{28,24},{1,5},{5... | collective-permute-start | bytes 884744 | tf_op jit(solution)/shard_map/cond/branch_1_fun/ppermute | solution.py:354
  37.1 4.3 %collective-permute-start.8 = (bf16[4,288,128]{2,1,0:T(8,128)(2,1)}, bf16[4,288,128]{2,1,0:T(8,128)(2,1)}, u32[]{:S(2)}, u32[]{:S(2)}) collective-permute-start(bf16[4,288,128]{2,1,0:T(8,128)(2,1)} %get-tuple-element.69), channel_id=1, source_target_pairs={{0,4},{4,0},{8,12},{12,8},{16,20},{20,16},{24,28},{28,24},{1,5},{5... | collective-permute-start | bytes 884744 | tf_op jit(solution)/shard_map/cond/branch_1_fun/ppermute | solution.py:354
  38.6 2.8 %collective-permute-start.9 = (bf16[4,288,128]{2,1,0:T(8,128)(2,1)}, bf16[4,288,128]{2,1,0:T(8,128)(2,1)}, u32[]{:S(2)}, u32[]{:S(2)}) collective-permute-start(bf16[4,288,128]{2,1,0:T(8,128)(2,1)} %get-tuple-element.70), channel_id=1, source_target_pairs={{0,4},{4,0},{8,12},{12,8},{16,20},{20,16},{24,28},{28,24},{1,5},{5... | collective-permute-start | bytes 884744 | tf_op jit(solution)/shard_map/cond/branch_1_fun/ppermute | solution.py:354
  41.4 27.5 %collective-permute-start.19 = (bf16[2048,128]{1,0:T(8,128)(2,1)}, bf16[2048,128]{1,0:T(8,128)(2,1)}, u32[]{:S(2)}, u32[]{:S(2)}) collective-permute-start(bf16[2048,128]{1,0:T(8,128)(2,1)} %get-tuple-element.154), channel_id=1, source_target_pairs={{0,2},{1,3},{2,0},{3,1},{4,6},{5,7},{6,4},{7,5},{8,10},{9,11},{10,... | collective-permute-start | bytes 1572872 | tf_op jit(solution)/shard_map/ppermute | solution.py:410
  44.0 25.0 %collective-permute-start.20 = (bf16[2048,128]{1,0:T(8,128)(2,1)S(1)}, bf16[2048,128]{1,0:T(8,128)(2,1)}, u32[]{:S(2)}, u32[]{:S(2)}) collective-permute-start(bf16[2048,128]{1,0:T(8,128)(2,1)S(1)} %get-tuple-element.155), channel_id=1, source_target_pairs={{0,1},{3,2},{4,5},{7,6},{8,9},{11,10},{12,13},{15,14},{16,17},{19,... | collective-permute-start | bytes 1572872 | tf_op jit(solution)/shard_map/ppermute | solution.py:411
  46.6 12.1 %copy-start.1 = (bf16[256,128]{1,0:T(8,128)(2,1)S(1)}, bf16[256,128]{1,0:T(8,128)(2,1)}, u32[]{:S(2)}) copy-start(bf16[256,128]{1,0:T(8,128)(2,1)} %constant.114.clone.fwd_ref) | copy-start | bytes 196612
  46.6 8.7 %copy-start.3 = (f32[2048,128]{1,0:T(8,128)}, f32[2048,128]{1,0:T(8,128)S(1)}, u32[]{:S(2)}) copy-start(f32[2048,128]{1,0:T(8,128)S(1)} %get-tuple-element.78.moment_ref) | copy-start | bytes 3145732 | tf_op jit(solution)/shard_map/cond
  46.6 4.6 %collective-permute-start.10 = (bf16[1,4,16,128]{3,2,1,0:T(8,128)(2,1)S(1)}, bf16[1,4,16,128]{3,2,1,0:T(8,128)(2,1)S(1)}, u32[]{:S(2)}, u32[]{:S(2)}) collective-permute-start(bf16[1,4,16,128]{3,2,1,0:T(8,128)(2,1)S(1)} %convert_bitcast_fusion), channel_id=1, source_target_pairs={{0,4},{4,0},{8,12},{12,8},{16,20},{20,16},{24,28},{28,24},{1,5},{5... | collective-permute-start | bytes 49160 | tf_op jit(solution)/shard_map/cond/branch_1_fun/ppermute | solution.py:354
  46.7 8.6 %copy-start.4 = (bf16[2048,128]{1,0:T(8,128)(2,1)S(1)}, bf16[2048,128]{1,0:T(8,128)(2,1)}, u32[]{:S(2)}) copy-start(bf16[2048,128]{1,0:T(8,128)(2,1)} %get-tuple-element.79.kept_ref) | copy-start | bytes 1572868 | tf_op jit(solution)/shard_map/cond
  51.8 6.8 %collective-permute-start.13 = (bf16[2,4,16,128]{3,2,1,0:T(8,128)(2,1)}, bf16[2,4,16,128]{3,2,1,0:T(8,128)(2,1)}, u32[]{:S(2)}, u32[]{:S(2)}) collective-permute-start(bf16[2,4,16,128]{3,2,1,0:T(8,128)(2,1)} %pad_maximum_fusion), channel_id=1, source_target_pairs={{0,24},{4,28},{8,16},{12,20},{16,8},{20,12},{24,0},{28,4},{1,25},{... | collective-permute-start | bytes 98312 | tf_op jit(solution)/shard_map/cond/branch_1_fun/ppermute | solution.py:354
  53.9 4.7 %collective-permute-start.12 = (bf16[2,4,16,128]{3,2,1,0:T(8,128)(2,1)}, bf16[2,4,16,128]{3,2,1,0:T(8,128)(2,1)}, u32[]{:S(2)}, u32[]{:S(2)}) collective-permute-start(bf16[2,4,16,128]{3,2,1,0:T(8,128)(2,1)} %pad_maximum_fusion), channel_id=1, source_target_pairs={{0,8},{4,12},{8,0},{12,4},{16,24},{20,28},{24,16},{28,20},{1,9},{5... | collective-permute-start | bytes 98312 | tf_op jit(solution)/shard_map/cond/branch_1_fun/ppermute | solution.py:354
  54.4 4.2 %collective-permute-start.11 = (bf16[2,4,16,128]{3,2,1,0:T(8,128)(2,1)}, bf16[2,4,16,128]{3,2,1,0:T(8,128)(2,1)}, u32[]{:S(2)}, u32[]{:S(2)}) collective-permute-start(bf16[2,4,16,128]{3,2,1,0:T(8,128)(2,1)} %pad_maximum_fusion), channel_id=1, source_target_pairs={{0,16},{4,20},{8,24},{12,28},{16,0},{20,4},{24,8},{28,12},{1,17},{... | collective-permute-start | bytes 98312 | tf_op jit(solution)/shard_map/cond/branch_1_fun/ppermute | solution.py:354

commit v3 on v2

v3 whole, which is shorter than its diff:
```python
import functools

import jax
import jax.numpy as jnp
import numpy as np
from jax import lax
from jax.experimental import pallas as pl
from jax.experimental.pallas import tpu as pltpu
from jax.sharding import PartitionSpec as P

TILE = 64
LANES = 128

momentum_decay = 0.999
step_size = 0.005


def cosine_array(order):
    freq = np.arange(order, dtype=np.float64)[:, None]
    place = np.arange(order, dtype=np.float64)[None, :]
    table = np.sqrt(2.0 / order) * np.cos(np.pi * (2.0 * place + 1.0) * freq / (2.0 * order))
    return table * np.where(freq == 0.0, np.sqrt(0.5), 1.0)


def tables():
    block = np.kron(np.eye(2), cosine_array(TILE)).astype(np.float32)
    high = block.astype(jnp.bfloat16)
    low = (block - high.astype(np.float32)).astype(jnp.bfloat16)
    inv = np.concatenate([high.T, low.T], axis=0)
    small = [part[i : i + TILE, i : i + TILE].T for i in (0, TILE) for part in (high, low)]
    pair = np.zeros((4 * TILE, LANES), jnp.bfloat16)
    for i, part in enumerate(small):
        pair[i * TILE : (i + 1) * TILE, (i // 2) * TILE : (i // 2 + 1) * TILE] = part
    fwd = np.concatenate([high, low], axis=0)
    return jnp.asarray(inv), jnp.asarray(fwd), jnp.asarray(pair)


def split(x):
    high = x.astype(jnp.bfloat16)
    return high, (x - high.astype(jnp.float32)).astype(jnp.bfloat16)


def dot(a, b, contract=((1,), (0,))):
    return lax.dot_general(a, b, (contract, ((), ())), preferred_element_type=jnp.float32)


def hot(row, size, fill=None):
    spread = lambda x: jnp.broadcast_to(x, (16, LANES)).astype(jnp.bfloat16)
    place = spread(row)
    fill = jnp.ones((16, LANES), jnp.bfloat16) if fill is None else spread(fill)
    none = jnp.zeros((16, LANES), jnp.bfloat16)
    sub = lax.broadcasted_iota(jnp.int32, (16, LANES), 0).astype(jnp.float32)
    parts = [jnp.where((sub + 16.0 * i).astype(jnp.bfloat16) == place, fill, none) for i in range(size // 16)]
    return jnp.concatenate(parts, axis=0)


def chunk_of(slot, f):
    return jnp.where(slot < 2, jnp.where(slot == 0, 3 - 3 * (f & 1), 1 + (f & 1)), jnp.where(slot == 2, f ^ 2, f))


def partial_kernel(me, tok, grad, *outs):
    for i, out in enumerate(outs):

        @pl.when(pl.program_id(0) == i)
        def _():
            out[...] = dot(tok[...], grad[...], ((0,), (0,))).astype(out.dtype)


def partial_chunks(me, tokens, grad_out, rows):
    count = 4
    width = grad_out.shape[1]
    toks = tokens.shape[0]
    return pl.pallas_call(
        partial_kernel,
        grid_spec=pltpu.PrefetchScalarGridSpec(
            num_scalar_prefetch=1,
            grid=(count,),
            in_specs=[
                pl.BlockSpec((toks, rows), lambda s, me: (0, chunk_of(s, me[0]))),
                pl.BlockSpec((toks, width), lambda s, me: (0, 0)),
            ],
            out_specs=[pl.BlockSpec((rows, width), lambda s, me: (0, 0)) for _ in range(count)],
        ),
        out_shape=[jax.ShapeDtypeStruct((rows, width), jnp.bfloat16) for _ in range(count)],
        cost_estimate=pl.CostEstimate(
            flops=2 * count * rows * width * toks, bytes_accessed=count * rows * (width + toks) * 2, transcendentals=0
        ),
        compiler_params=pltpu.CompilerParams(vmem_limit_bytes=32 * 2**20),
    )(me, tokens, grad_out)


def idx_block(s, unit):
    return jnp.where(s == 0, 0, unit * (s - 1) + 1)


def select_kernel(groups, me, pair_ref, idx_ref, tok_ref, grad_ref, moment_ref, out_ref):
    pair = pair_ref[...]
    grad = jnp.concatenate([grad_ref[...]] * 2, axis=1)
    places = (idx_ref[...].astype(jnp.int32) & (TILE - 1)).astype(jnp.float32)
    lane = lax.broadcasted_iota(jnp.int32, (TILE, LANES), 1)
    top = lane < TILE
    even = (lane // (TILE // 2)) % 2 == 0
    none = jnp.zeros((TILE, LANES), jnp.float32)

    def spread(low_half, high, low):
        parts = [jnp.where(low_half, high, none), jnp.where(low_half, none, high)]
        parts += [jnp.where(low_half, low, none), jnp.where(low_half, none, low)]
        return jnp.concatenate(parts, axis=0)

    batch = groups

    def some_groups(g, own):
        of = range(g, g + batch)
        rows = [jnp.concatenate([hot(places[i : i + 1], TILE), hot(places[groups + i : groups + i + 1], TILE)], axis=0) for i in of]
        both = dot(pair, jnp.concatenate(rows, axis=1))
        quarters = [[both[q * TILE : (q + 1) * TILE, i * LANES : (i + 1) * LANES] for q in range(4)] for i in range(batch)]
        a2s = [spread(top, quarter[0], quarter[1]) for quarter in quarters]
        b2s = [spread(even, quarter[2], quarter[3]).astype(jnp.bfloat16) for quarter in quarters]
        gb = dot(grad, jnp.concatenate(b2s, axis=1))
        toks = [tok_ref[:, i * LANES : (i + 1) * LANES] for i in of]
        tas = [dot(jnp.concatenate([tok, tok], axis=1), a2.astype(jnp.bfloat16)) for tok, a2 in zip(toks, a2s)]
        values = [
            jnp.sum(ta * gb[:, i * LANES : (i + 1) * LANES], axis=0, keepdims=True) for i, ta in enumerate(tas)
        ]
        if own:
            parts = [split(momentum_decay * moment_ref[i * LANES : (i + 1) * LANES, :]) for i in of]
            mbs = [
                dot(jnp.concatenate([hi, hi], axis=1), b2) + dot(lo, b2[:LANES]) for (hi, lo), b2 in zip(parts, b2s)
            ]
            values = [
                value + jnp.sum(mb * (a2[:LANES] + a2[LANES:]), axis=0, keepdims=True)
                for value, mb, a2 in zip(values, mbs, a2s)
            ]
        out_ref[0, g : g + batch, :] = jnp.concatenate(values, axis=0)

    @pl.when(pl.program_id(0) == 0)
    def _():
        for g in range(0, groups, batch):
            some_groups(g, True)

    @pl.when(pl.program_id(0) != 0)
    def _():
        for g in range(0, groups, batch):
            some_groups(g, False)


def select_values(me, inv, idx, unit, tokens, grad_out, moment):
    n_f = tokens.shape[1] // moment.shape[0]
    rows = moment.shape[0]
    groups = rows // LANES
    toks = tokens.shape[0]
    width = grad_out.shape[1]
    return pl.pallas_call(
        functools.partial(select_kernel, groups),
        grid_spec=pltpu.PrefetchScalarGridSpec(
            num_scalar_prefetch=1,
            grid=(n_f,),
            in_specs=[
                pl.BlockSpec(inv.shape, lambda s, me: (0, 0)),
                pl.BlockSpec((2 * groups, LANES), lambda s, me: (idx_block(s, unit), 0)),
                pl.BlockSpec((toks, rows), lambda s, me: (0, me[0] ^ s)),
                pl.BlockSpec((toks, width), lambda s, me: (0, 0)),
                pl.BlockSpec((rows, width), lambda s, me: (0, 0)),
            ],
            out_specs=pl.BlockSpec((1, groups, LANES), lambda s, me: (me[0] ^ s, 0, 0)),
        ),
        out_shape=jax.ShapeDtypeStruct((n_f, groups, LANES), jnp.float32),
        cost_estimate=pl.CostEstimate(
            flops=2 * n_f * groups * LANES**3 * 6, bytes_accessed=4 * 2**20, transcendentals=0
        ),
        compiler_params=pltpu.CompilerParams(vmem_limit_bytes=32 * 2**20),
    )(me, inv, idx, tokens, grad_out, moment)


def moment_kernel(groups, me, inv_ref, idx_ref, val_ref, moment_ref, kept_ref, outer_ref, inner_ref, two_ref, far_ref, out_ref):
    inv = inv_ref[...]
    outer = (me[0] == 0) | (me[0] == me[1] - 1)
    step = groups // 2
    first = pl.multiple_of(pl.program_id(0) * step, step)
    row_at = idx_ref[...].astype(jnp.float32)
    upper = pl.program_id(0) > 0
    pick = lambda x: jnp.where(upper, x[step:], x[:step])
    rows, cols, worth = pick(row_at[:groups]), pick(row_at[groups:]), pick(val_ref[0])
    of = range(step)
    hots = [jnp.concatenate([hot(rows[g : g + 1], LANES), hot(cols[g : g + 1], LANES)], axis=1) for g in of]
    both = dot(inv, jnp.concatenate(hots, axis=1))
    block = lambda half, g: both[half * LANES : (half + 1) * LANES, g * LANES : (g + 1) * LANES]
    lefts = [split((block(0, 2 * g) + block(1, 2 * g)) * worth[g : g + 1, :]) for g in of]
    lefts = [jnp.concatenate([hi, hi, lo], axis=1) for hi, lo in lefts]
    rights = [jnp.concatenate([block(0, 2 * g + 1), block(1, 2 * g + 1)], axis=1).astype(jnp.bfloat16) for g in of]
    rights = [jnp.concatenate([right, right[:, :LANES]], axis=1) for right in rights]
    slabs = jnp.concatenate([dot(left, right, ((1,), (1,))) for left, right in zip(lefts, rights)], axis=0)
    wide = lambda ref: ref[...].astype(jnp.float32)
    got = wide(kept_ref) + jnp.where(outer, wide(outer_ref), wide(inner_ref)) + (wide(two_ref) + wide(far_ref))
    out_ref[...] = (momentum_decay * moment_ref[...] + got) - slabs


def new_moment_of(me, inv, idx, values, moment, *parts):
    groups = values.shape[1]
    rows, width = moment.shape
    slab = pl.BlockSpec((rows // 2, width), lambda i, me: (i, 0))
    return pl.pallas_call(
        functools.partial(moment_kernel, groups),
        grid_spec=pltpu.PrefetchScalarGridSpec(
            num_scalar_prefetch=1,
            grid=(2,),
            in_specs=[
                pl.BlockSpec(inv.shape, lambda i, me: (0, 0)),
                pl.BlockSpec((2 * groups, LANES), lambda i, me: (0, 0)),
                pl.BlockSpec((1, groups, LANES), lambda i, me: (me[0], 0, 0)),
                slab,
            ]
            + [slab for _ in parts],
            out_specs=slab,
        ),
        out_shape=jax.ShapeDtypeStruct((rows, width), jnp.float32),
        cost_estimate=pl.CostEstimate(
            flops=2 * groups * LANES**3 * 7, bytes_accessed=5 * rows * width * 4, transcendentals=0
        ),
        compiler_params=pltpu.CompilerParams(vmem_limit_bytes=32 * 2**20),
    )(me, inv, idx, values, moment, *parts)


AWAY = (0, 4, 2, 6, 1, 5, 3, 7)


def project_kernel(n_r, n_f, extra, me, inv_ref, nt_ref, weight_ref, *refs):
    pieces, (out_ref, coef_ref) = refs[:n_r], refs[n_r:]
    width = nt_ref.shape[1]
    size = width // (n_r * n_f)
    near = nt_ref[:, pl.ds(pl.multiple_of(me[0] * size * n_r, size * n_r), size * n_r)]
    total = dot(near, weight_ref[...])
    for p in range(1, n_f):
        lefts, rights = [], []
        for away, piece in zip(AWAY, pieces):
            place = (me[0] ^ p) * n_r + (me[2] ^ away)
            lefts.append(nt_ref[:, pl.ds(pl.multiple_of(place * size, size), size)])
            rights.append(piece[p * (extra + size) - size + extra : p * (extra + size) + extra, :])
        total += dot(jnp.concatenate(lefts, axis=1), jnp.concatenate(rights, axis=0))
    out_ref[...] = total
    inv = inv_ref[...]
    table = jnp.concatenate([inv[:LANES], inv[LANES:]], axis=1)
    toks = nt_ref.shape[0]
    batch = 8
    for g in range(0, width // LANES, batch):
        parts = [slice(i * LANES, (i + 1) * LANES) for i in range(g, g + batch)]
        both = dot(jnp.concatenate([nt_ref[:, part] for part in parts], axis=0), table)
        both = (both[:, :LANES] + both[:, LANES:]).astype(jnp.bfloat16)
        for i, part in enumerate(parts):
            coef_ref[:, part] = both[i * toks : (i + 1) * toks]


def project(me, inv, next_tokens, weight, pieces, extra):
    n_r = len(pieces)
    toks, width = next_tokens.shape
    n_f = width // weight.shape[0]
    out = weight.shape[1]
    full = lambda *shape: pl.BlockSpec(shape, lambda i, me: (0,) * len(shape))
    return pl.pallas_call(
        functools.partial(project_kernel, n_r, n_f, extra),
        grid_spec=pltpu.PrefetchScalarGridSpec(
            num_scalar_prefetch=1,
            grid=(1,),
            in_specs=[full(*inv.shape), full(toks, width), full(*weight.shape)] + [full(*piece.shape) for piece in pieces],
            out_specs=[full(toks, out), full(toks, width)],
        ),
        out_shape=[jax.ShapeDtypeStruct((toks, out), jnp.float32), jax.ShapeDtypeStruct((toks, width), jnp.bfloat16)],
        cost_estimate=pl.CostEstimate(
            flops=2 * toks * width * out * 3, bytes_accessed=6 * toks * width * 2, transcendentals=0
        ),
        compiler_params=pltpu.CompilerParams(vmem_limit_bytes=48 * 2**20),
    )(me, inv, next_tokens, weight, *pieces)


def merge_kernel(me, third_ref, outer_ref, out_ref):
    inner = (me[0] > 0) & (me[0] < me[1] - 1)

    @pl.when(inner)
    def _():
        out_ref[...] = (third_ref[...].astype(jnp.float32) + outer_ref[...].astype(jnp.float32)).astype(out_ref.dtype)

    @pl.when(jnp.logical_not(inner))
    def _():
        out_ref[...] = third_ref[...]


def merge(me, third, outer):
    rows, width = third.shape
    slab = pl.BlockSpec((rows // 4, width), lambda i, me: (i, 0))
    return pl.pallas_call(
        merge_kernel,
        grid_spec=pltpu.PrefetchScalarGridSpec(num_scalar_prefetch=1, grid=(4,), in_specs=[slab, slab], out_specs=slab),
        out_shape=jax.ShapeDtypeStruct((rows, width), third.dtype),
        cost_estimate=pl.CostEstimate(flops=rows * width, bytes_accessed=6 * rows * width, transcendentals=0),
    )(me, third, outer)


def total_kernel(groups, n_r, me, inv_ref, fwd_ref, coef_ref, base_ref, *refs):
    idx_refs, val_refs = refs[:n_r], refs[n_r : n_r + n_r // 2]
    up_ref, out_ref, acc_ref, sort_ref, dense_ref = refs[n_r + n_r // 2 :]
    step = pl.program_id(0)
    inv = inv_ref[...]
    fwd = fwd_ref[...]

    @pl.when(step == 0)
    def _():
        acc_ref[...] = jnp.zeros_like(acc_ref)

    lane = lax.broadcasted_iota(jnp.int32, (groups, LANES), 1)
    quarter = LANES // 4

    def regroup(parts):
        out = []
        for t in range(4):
            row = None
            for i, part in enumerate(parts):
                moved = part if i == t else pltpu.roll(part, (quarter * (i - t)) % LANES, 1)
                row = moved if row is None else jnp.where(lane // quarter == i, moved, row)
            out.append(row)
        return out

    for quad in range(n_r // 4):
        of = range(4 * quad, 4 * quad + 4)
        spots = [idx_refs[r][...].astype(jnp.int32) & (TILE - 1) for r in of]
        worth = [val_refs[r % (n_r // 2)][r // (n_r // 2), 0].astype(jnp.float32) for r in of]
        sets = regroup([x[:groups] for x in spots]), regroup([x[groups:] for x in spots]), regroup(worth)
        for kind, four in enumerate(sets):
            for t, rows in enumerate(four):
                sort_ref[kind, quad, t] = rows.astype(jnp.float32)

    low = lax.broadcasted_iota(jnp.int32, (TILE, LANES), 1) < TILE
    batch = 2

    def some_groups(g):
        of = range(g, g + batch)
        at = lambda kind, quad, t, i: sort_ref[kind, quad, t, i : i + 1, :]
        quads = range(n_r // 4)
        side = lambda tile: jnp.concatenate([jnp.concatenate([tile(t, q) for q in quads], axis=1) for t in range(4)], axis=0)
        lefts = [side(lambda t, q: hot(at(0, q, t, i), TILE)) for i in of]
        rights = [side(lambda t, q: hot(at(1, q, t, i), TILE, at(2, q, t, i))) for i in of]
        crosses = [dot(left, right, ((1,), (1,))) for left, right in zip(lefts, rights)]
        diagonal = lambda cross, i: jnp.where(low, cross[i : i + TILE, i : i + LANES], cross[i + TILE : i + LANES, i : i + LANES])
        denses = [jnp.concatenate([diagonal(cross, 0), diagonal(cross, LANES)], axis=0) for cross in crosses]
        for i, dense in zip(of, denses):
            dense_ref[i * LANES : (i + 1) * LANES, :] = jnp.concatenate(split(dense), axis=1)

    for g in range(0, groups, batch):
        some_groups(g)

    both = dot(coef_ref[...], dense_ref[...])
    acc_ref[...] += both[:, :LANES] + both[:, LANES:]

    @pl.when(step == 0)
    def _():
        c_hi, c_lo = inv[:LANES], inv[LANES:]
        f_hi, f_lo = fwd[:LANES], fwd[LANES:]
        table = jnp.concatenate([c_hi, c_lo], axis=1)
        last = jnp.concatenate([f_hi, f_lo, f_hi], axis=0)
        parts = [dense_ref[g * LANES : (g + 1) * LANES, :] for g in range(groups)]
        boths = [dot(table, jnp.concatenate([part, part], axis=0)) for part in parts]
        halves = [split(both[:, :LANES] + both[:, LANES:]) for both in boths]
        lines = jnp.concatenate([jnp.concatenate([hi, hi, lo], axis=1) for hi, lo in halves], axis=0)
        up_ref[...] = dot(lines, last)

    @pl.when(step == pl.num_programs(0) - 1)
    def _():
        s_hi, s_lo = split(acc_ref[...])
        f_hi, f_lo = fwd[:LANES], fwd[LANES:]
        moved = dot(jnp.concatenate([s_hi, s_hi, s_lo], axis=1), jnp.concatenate([f_hi, f_lo, f_hi], axis=0))
        out_ref[...] = (base_ref[...] - step_size * moved).astype(out_ref.dtype)


def totals(me, inv, fwd, coef, base, pieces, unit, sent):
    n_r, n_f = len(pieces), sent[0].shape[1]
    groups = sent[0].shape[2]
    rows = groups * LANES
    toks, width = base.shape
    return pl.pallas_call(
        functools.partial(total_kernel, groups, n_r),
        grid_spec=pltpu.PrefetchScalarGridSpec(
            num_scalar_prefetch=1,
            grid=(n_f,),
            in_specs=[
                pl.BlockSpec(inv.shape, lambda s, me: (0, 0)),
                pl.BlockSpec(fwd.shape, lambda s, me: (0, 0)),
                pl.BlockSpec((toks, rows), lambda s, me: (0, me[0] ^ s)),
                pl.BlockSpec((toks, width), lambda s, me: (0, 0)),
            ]
            + [pl.BlockSpec((2 * groups, LANES), lambda s, me: (idx_block(s, unit), 0)) for _ in pieces]
            + [pl.BlockSpec((2, 1, groups, LANES), lambda s, me: (0, me[0] ^ s, 0, 0)) for _ in sent],
            out_specs=[
                pl.BlockSpec((rows, width), lambda s, me: (0, 0)),
                pl.BlockSpec((toks, width), lambda s, me: (0, 0)),
            ],
            scratch_shapes=[
                pltpu.VMEM((toks, width), jnp.float32),
                pltpu.VMEM((3, n_r // 4, 4, groups, LANES), jnp.float32),
                pltpu.VMEM((rows, 2 * LANES), jnp.bfloat16),
            ],
        ),
        out_shape=[
            jax.ShapeDtypeStruct((rows, width), jnp.float32),
            jax.ShapeDtypeStruct((toks, width), jnp.bfloat16),
        ],
        cost_estimate=pl.CostEstimate(
            flops=2 * n_f * groups * LANES**3 * (n_r + 2), bytes_accessed=4 * 2**20, transcendentals=0
        ),
        compiler_params=pltpu.CompilerParams(vmem_limit_bytes=32 * 2**20),
    )(me, inv, fwd, coef, base, *pieces, *sent)


def swap(x, axis, size, mask):
    return lax.ppermute(x, axis, [(i, i ^ mask) for i in range(size)])


def fence(stage, *args):
    shapes = jax.eval_shape(stage, *args)
    other = lambda *args: jax.tree.map(lambda x: jnp.zeros(x.shape, x.dtype), shapes)
    return lax.cond(lax.axis_index("rep") < lax.axis_size("rep"), stage, other, *args)


def line_fast(n_r, n_f, tokens, grad_out, moment, weight, next_tokens, index):
    bf16 = jnp.bfloat16
    r, f = lax.axis_index("rep"), lax.axis_index("fsdp")
    me = jnp.stack([f, n_f, r]).astype(jnp.int32)
    inv, fwd, pair = tables()
    moment = moment[0]
    rows = moment.shape[0]
    groups = rows // LANES
    slice_rows = rows // n_r

    flat = index[0].reshape(groups, LANES)
    lane = jnp.arange(LANES, dtype=jnp.int32)
    row_pos = flat // TILE + (lane // TILE) * TILE
    col_pos = flat % TILE + (lane // (TILE // 2)) % 2 * TILE
    own_idx = jnp.concatenate([row_pos, col_pos], axis=0).astype(bf16)
    extra = own_idx.shape[0]
    share = lax.dynamic_slice_in_dim(weight, r * slice_rows, slice_rows, axis=0)
    held = jnp.concatenate([own_idx, share], axis=0)
    unit = held.shape[0] // extra

    held = jnp.concatenate([own_idx] + [swap(held, "fsdp", n_f, p) for p in range(1, n_f)], axis=0)
    first, second, third, kept = partial_chunks(me, tokens, grad_out, rows)
    held, first, second = lax.optimization_barrier((held, first, second))
    outer = lax.ppermute(first, "fsdp", [(0, 1), (1, 0), (2, 3), (3, 2)])
    inner = lax.ppermute(second, "fsdp", [(1, 2), (2, 1)])

    def near_stage(held):
        pieces = [swap(held, "rep", n_r, away) for away in AWAY[1 : n_r // 2]]
        return select_values(me, pair, held, unit, tokens, grad_out, moment), pieces

    values, pieces = fence(near_stage, held)
    pieces = [held] + pieces
    outer, inner = lax.optimization_barrier((outer, inner))

    def sum_stage(values, third, outer, pieces):
        parts = [swap(values, "fsdp", n_f, p) for p in range(1, n_f)]
        more = [swap(piece, "rep", n_r, 1) for piece in pieces]
        return parts, merge(me, third, outer), more

    parts, merged, more = fence(sum_stage, values, third, outer, pieces[:2])
    parts, merged, second = lax.optimization_barrier((parts, merged, second))
    two = lax.ppermute(merged, "fsdp", [(0, 2), (1, 3), (2, 0), (3, 1)])
    far = lax.ppermute(second, "fsdp", [(0, 1), (3, 2)])

    def far_stage(values, parts, pieces, more):
        summed = sum(parts, values)
        sent = summed.astype(bf16)[None]
        last = [swap(piece, "rep", n_r, 1) for piece in pieces[2:]]
        sent = jnp.concatenate([sent, swap(sent, "rep", n_r, 1)], axis=0)
        sent, last = lax.optimization_barrier((sent, last))
        sents = [sent] + [swap(sent, "rep", n_r, away) for away in AWAY[1 : n_r // 2]]
        old_out, coef = project(me, inv, next_tokens, weight, pieces + more + last, extra)
        return summed, sents, old_out, coef, last

    values, sents, old_out, coef, last = fence(far_stage, values, parts, pieces, more)
    pieces = pieces + more + last
    update, next_out = totals(me, inv, fwd, coef, old_out, pieces, unit, sents)
    update, two, far = lax.optimization_barrier((update, two, far))
    new_moment = new_moment_of(me, inv, held, values, moment, kept, outer, inner, two, far)
    return update, new_moment[None], next_out


def cosine_table(order):
    return jnp.asarray(cosine_array(order), jnp.float32)


def forward_tiles(field, table):
    side = table.shape[0]
    shard_rows, width = field.shape
    tiles = field.reshape(shard_rows // side, side, width)
    along = jnp.einsum("ab,ibc->iac", table, tiles, precision=lax.Precision.HIGHEST)
    block = jnp.kron(jnp.eye(width // side, dtype=jnp.float32), table.T)
    return jnp.matmul(along, block, precision=lax.Precision.HIGHEST)


def inverse_tiles(spectra, table):
    side = table.shape[0]
    width = spectra.shape[2]
    along = jnp.einsum("ab,iac->ibc", table, spectra, precision=lax.Precision.HIGHEST)
    block = jnp.kron(jnp.eye(width // side, dtype=jnp.float32), table)
    result = jnp.matmul(along, block, precision=lax.Precision.HIGHEST)
    return result.reshape(spectra.shape[0] * side, width)


def one_hots(places, side, width):
    row_of = places // side
    col_of = places % side + jnp.arange(width // side, dtype=jnp.int32)[:, None] * side
    row_hot = (row_of[..., None] == jnp.arange(side, dtype=jnp.int32)).astype(jnp.float32)
    col_hot = (col_of[..., None] == jnp.arange(width, dtype=jnp.int32)).astype(jnp.float32)
    return (row_hot, col_hot)


def any_mesh(tokens, grad_out, moment, weight, next_tokens, index):
    table = cosine_table(TILE)
    width = weight.shape[1]
    partial = lax.dot_general(tokens, grad_out, (((0,), (0,)), ((), ())), preferred_element_type=jnp.float32)
    grad = lax.psum_scatter(partial.astype(jnp.bfloat16), "fsdp", scatter_dimension=0, tiled=True)
    moment_now = momentum_decay * moment[0] + grad.astype(jnp.float32)
    spectra = forward_tiles(moment_now, table)
    row_hot, col_hot = one_hots(index[0], TILE, width)
    picked = jnp.einsum("ijka,iac->ijkc", row_hot, spectra, precision=lax.Precision.HIGHEST)
    values = jnp.sum(picked * col_hot, axis=-1)
    dense = jnp.einsum("ijka,ijkc->iac", row_hot * values[..., None], col_hot, precision=lax.Precision.HIGHEST)
    new_moment = (moment_now - inverse_tiles(dense, table))[None]
    total = lax.psum(dense.astype(jnp.bfloat16), "rep").astype(jnp.float32)
    update = inverse_tiles(total, table)
    new_weight = (weight.astype(jnp.float32) - step_size * update).astype(jnp.bfloat16)
    full = lax.all_gather(new_weight, "fsdp", axis=0, tiled=True)
    next_out = jnp.dot(next_tokens, full, preferred_element_type=jnp.float32).astype(jnp.bfloat16)
    return (update, new_moment, next_out)


def solution(mesh):
    n_r, n_f = mesh.shape["rep"], mesh.shape["fsdp"]
    local = functools.partial(line_fast, n_r, n_f) if (n_r, n_f) == (8, 4) else any_mesh
    in_specs = (
        P(("rep", "fsdp"), None),
        P(("rep", "fsdp"), None),
        P("rep", "fsdp", None),
        P("fsdp", None),
        P(("rep", "fsdp"), None),
        P("rep", "fsdp", None, None),
    )
    out_specs = (P("fsdp", None), P("rep", "fsdp", None), P(("rep", "fsdp"), None))
    return jax.shard_map(local, mesh=mesh, in_specs=in_specs, out_specs=out_specs, check_vma=False)
```

time: 71.8 us -> 65.6 us (0.914)
  Pallas kernels: 33.2 us -> 28.1 us
  other arithmetic: 5.85 us -> 1.56 us
  waiting for transfers between devices: 3.56 us -> 6.59 us
  local copies, waits for them, and re-layouts: 1.72 us -> 2.64 us
    pallas_call x1, Pallas kernels: 10.3 us -> 6.2 us  [select_values(): pl.pallas_call(functools.partial(select_kernel, groups), grid_spec=pltpu....]
    ppermute x17, waiting for transfers between devices: 3.55 us -> 6.58 us  [swap(): return lax.ppermute(x, axis, [(i, i ^ mask) for i in range(size)])]
    convert_element_type x1 -> x0, other arithmetic: 2.02 us -> none  [sum_stage(): merged = (third.astype(jnp.float32) + got).astype(bf16)]
    broadcast_in_dim x3 -> x1, other arithmetic: 2.32 us -> 0.82 us  [far_stage(): sent = summed.astype(bf16)[None]]
    pallas_call x1, Pallas kernels: 10.3 us -> 8.83 us  [totals(): pl.pallas_call(functools.partial(total_kernel, groups, n_r), grid_spec=pl...]
    pallas_call x1 -> x2, Pallas kernels: 3.34 us -> 4.78 us  [the longest x1 2.84 us: new_moment_of(): pl.pallas_call(functools.partial(moment_kernel, groups), grid_spec=pltpu....]
    ppermute x1, starting transfers between devices: 2.53 us -> 1.11 us  [line_fast(): two = lax.ppermute(merged, 'fsdp', [(0, 2), (1, 3), (2, 0), (3, 1)])]
    ppermute x1, starting transfers between devices: 2.6 us -> 3.59 us  [line_fast(): far = lax.ppermute(second, 'fsdp', [(0, 1), (3, 2)])]
  transfers between devices with their start and end apart: 21 -> 21, of which waited for: 4 -> 6; matrix products, arithmetic and copies ran while one was open for 6% -> 2% of each run, Pallas kernels for 47% -> 39%
where the time goes in v3:
time: 65.6 us; the launch traced here: 65.1 us
  Pallas kernels  28.1 us (43%)
  starting transfers between devices  25.4 us (39%)
  waiting for transfers between devices  6.59 us (10%)
  local copies, waits for them, and re-layouts  2.64 us (4%)
  other arithmetic  1.56 us (2%)
  between operations  0.8 us (1%)
    ppermute x17, starting transfers between devices, swap(): return lax.ppermute(x, axis, [(i, i ^ mask) for i in range(size)])  18.9 us
    pallas_call x1, Pallas kernels, totals(): pl.pallas_call(functools.partial(total_kernel, groups, n_r), grid_spec=pl...  8.83 us
    ppermute x17, waiting for transfers between devices, swap(): return lax.ppermute(x, axis, [(i, i ^ mask) for i in range(size)])  6.58 us
    pallas_call x1, Pallas kernels, select_values(): pl.pallas_call(functools.partial(select_kernel, groups), grid_spec=pltpu....  6.2 us
    pallas_call x1, Pallas kernels, project(): pl.pallas_call(functools.partial(project_kernel, n_r, n_f, extra), grid_s...  4.48 us
    pallas_call x1, Pallas kernels, partial_chunks(): pl.pallas_call(partial_kernel, grid_spec=pltpu.PrefetchScalarGridSpec(num...  3.76 us
    ppermute x1, starting transfers between devices, line_fast(): far = lax.ppermute(second, 'fsdp', [(0, 1), (3, 2)])  3.59 us
    pallas_call x1, Pallas kernels, new_moment_of(): pl.pallas_call(functools.partial(moment_kernel, groups), grid_spec=pltpu....  2.84 us
  transfers between devices with their start and end apart: 21, of which 6 were waited for; matrix products, arithmetic and copies ran while one was open for 2% of the time, Pallas kernels for 39%

profile of v3, /device:TPU:0, one launch (start us, length us, event | category | flops | bytes accessed | tf_op | source)
XLA Modules:
  0.0 65.1 jit_solution(9648465906218022849)
XLA Ops:
  0.6 0.0 copy-start.5
  0.7 0.9 %reshape_squeeze.3 = s32[16,128]{1,0:T(8,128)S(1)} reshape(s32[1,32,2,32]{3,2,1,0:T(2,128)} %param.20) | data formatting | bytes 16384 | tf_op jit(solution)/shard_map/reshape;squeeze | solution.py:432
  1.5 0.8 %constant_dynamic-slice_fusion = bf16[256,128]{1,0:T(8,128)(2,1)S(1)} fusion(bf16[2048,128]{1,0:T(8,128)(2,1)} %param.18, s32[]{:T(128)S(6)} %select_n.46), kind=kLoop, calls=%fused_computation.35 | loop fusion | bytes 131076 | tf_op jit(solution)/shard_map/dynamic_slice | solution.py:438
  2.4 5.1 %collective-permute-start.16 = (bf16[288,128]{1,0:T(8,128)(2,1)S(1)}, bf16[288,128]{1,0:T(8,128)(2,1)S(1)}, u32[]{:S(2)}, u32[]{:S(2)}) collective-permute-start(bf16[288,128]{1,0:T(8,128)(2,1)S(1)} %pad_maximum_fusion.1), channel_id=1, source_target_pairs={{0,3},{1,2},{2,1},{3,0},{4,7},{5,6},{6,5},{7,4},{8,11},{9,10},{10,... | collective-permute-start | bytes 221192 | tf_op jit(solution)/shard_map/ppermute | solution.py:413
  7.5 0.0 collective-permute-start.15
  7.5 0.6 collective-permute-start.14
  8.2 0.1 pad_add_fusion.me
  8.3 3.8 %shard_map.114 = (bf16[2048,128]{1,0:T(8,128)(2,1)S(1)}, bf16[2048,128]{1,0:T(8,128)(2,1)S(1)}, bf16[2048,128]{1,0:T(8,128)(2,1)S(1)}, bf16[2048,128]{1,0:T(8,128)(2,1)S(1)}) custom-call(s32[3]{0:T(128)S(1)} %pad_add_fusion.me, bf16[128,8192]{1,0:T(8,128)(2,1)} %tok.1, bf16[128,128]{1,0:T(8,128)(2,1)} %grad.1), custom_call_target="tpu_custom_call" | custom-call | flops 268435456 | bytes 4194304 | tf_op jit(solution)/shard_map/pallas_call | solution.py:73
  12.0 0.2 collective-permute-done.14
  12.3 1.5 %collective-permute-done.15 = bf16[288,128]{1,0:T(8,128)(2,1)S(1)} collective-permute-done((bf16[288,128]{1,0:T(8,128)(2,1)S(1)}, bf16[288,128]{1,0:T(8,128)(2,1)S(1)}, u32[]{:S(2)}, u32[]{:S(2)}) %collective-permute-start.15) | collective-permute-done | bytes 73760 | tf_op jit(solution)/shard_map/ppermute | solution.py:413
  13.8 0.0 collective-permute-done.16
  13.8 1.1 %collective-permute-start.17 = (bf16[2048,128]{1,0:T(8,128)(2,1)S(1)}, bf16[2048,128]{1,0:T(8,128)(2,1)S(1)}, u32[]{:S(2)}, u32[]{:S(2)}) collective-permute-start(bf16[2048,128]{1,0:T(8,128)(2,1)S(1)} %get-tuple-element.129), channel_id=1, source_target_pairs={{0,1},{1,0},{2,3},{3,2},{4,5},{5,4},{6,7},{7,6},{8,9},{9,8},{10,11... | collective-permute-start | bytes 1572872 | tf_op jit(solution)/shard_map/ppermute | solution.py:445
  14.9 0.7 %collective-permute-start.18 = (bf16[2048,128]{1,0:T(8,128)(2,1)S(1)}, bf16[2048,128]{1,0:T(8,128)(2,1)S(1)}, u32[]{:S(2)}, u32[]{:S(2)}) collective-permute-start(bf16[2048,128]{1,0:T(8,128)(2,1)S(1)} %get-tuple-element.154), channel_id=1, source_target_pairs={{1,2},{2,1},{5,6},{6,5},{9,10},{10,9},{13,14},{14,13},{17,18},{18,... | collective-permute-start | bytes 1572872 | tf_op jit(solution)/shard_map/ppermute | solution.py:446
  15.6 12.3 %conditional.3 = (f32[4,16,128]{2,1,0:T(8,128)S(1)}, bf16[896,128]{1,0:T(8,128)(2,1)}, bf16[896,128]{1,0:T(8,128)(2,1)}, bf16[896,128]{1,0:T(8,128)(2,1)}) conditional(s32[]{:T(128)} %convert_element_type.4, () %tuple.38, (s32[3]{0:T(128)S(1)}, (), bf16[896,128]{1,0:T(8,128)(2,1)S(1)}, bf16[128,8192]{1,0:T(8,128)(2,1)}, ...), branch_computations={%region_0.1_spmd, %region_1.2_spmd} | conditional | flops 1610612736 | bytes 7209140 | solution.py:419
  15.6 2.5 %collective-permute-start.2 = (bf16[896,128]{1,0:T(8,128)(2,1)S(1)}, bf16[896,128]{1,0:T(8,128)(2,1)}, u32[]{:S(2)}, u32[]{:S(2)}) collective-permute-start(bf16[896,128]{1,0:T(8,128)(2,1)S(1)} %get-tuple-element.54.idx_ref), channel_id=1, source_target_pairs={{0,24},{4,28},{8,16},{12,20},{16,8},{20,12},{24,0},{28,4},{1,25},{... | collective-permute-start | bytes 688136 | tf_op jit(solution)/shard_map/cond/branch_1_fun/ppermute | solution.py:413
  18.1 0.5 collective-permute-start.1
  18.6 0.5 collective-permute-start
  19.2 0.8 %copy-done.1 = bf16[256,128]{1,0:T(8,128)(2,1)S(1)} copy-done((bf16[256,128]{1,0:T(8,128)(2,1)S(1)}, bf16[256,128]{1,0:T(8,128)(2,1)}, u32[]{:S(2)}) %copy-start.1) | copy-done | bytes 65560 | tf_op jit(solution)/shard_map/cond
  20.0 6.2 %branch_1_fun.3 = f32[4,16,128]{2,1,0:T(8,128)S(1)} custom-call(s32[3]{0:T(128)S(1)} %get-tuple-element.52.me, bf16[256,128]{1,0:T(8,128)(2,1)S(1)} %copy-done.1, bf16[896,128]{1,0:T(8,128)(2,1)S(1)} %get-tuple-element.54.idx_ref, bf16[128,8192]{1,0:T(8,128)(2,1)} %get-tuple-element.55.tok_ref, bf16[128,128]{1,0:T(8,128)(2,1)S(1)} %get-tuple-element.56.grad_ref, ...), custom_call_target="tpu_custom_call" | custom-call | flops 1610612736 | bytes 4194304 | tf_op jit(solution)/shard_map/cond/branch_1_fun/pallas_call | solution.py:153
  26.2 1.6 %collective-permute-done.1 = bf16[896,128]{1,0:T(8,128)(2,1)} collective-permute-done((bf16[896,128]{1,0:T(8,128)(2,1)S(1)}, bf16[896,128]{1,0:T(8,128)(2,1)}, u32[]{:S(2)}, u32[]{:S(2)}) %collective-permute-start.1) | collective-permute-done | bytes 229408 | tf_op jit(solution)/shard_map/cond/branch_1_fun/ppermute | solution.py:413
  27.9 0.0 collective-permute-done.17.outer_ref
  27.9 9.4 %conditional.4 = (f32[4,16,128]{2,1,0:T(8,128)}, f32[4,16,128]{2,1,0:T(8,128)}, f32[4,16,128]{2,1,0:T(8,128)}, bf16[2048,128]{1,0:T(8,128)(2,1)}, bf16[896,128]{1,0:T(8,128)(2,1)}, /*index=5*/bf16[896,128]{1,0:T(8,128)(2,1)}) conditional(s32[]{:T(128)} %convert_element_type.4, () %tuple.41, (f32[4,16,128]{2,1,0:T(8,128)S(1)}, s32[3]{0:T(128)S(1)}, ...), branch_computations={%region_2.3_spmd, %region_3.4_spmd} | conditional | flops 262144 | bytes 3801336 | solution.py:419
  27.9 0.1 collective-permute-start.6
  28.0 0.5 collective-permute-start.7
  28.5 1.6 %collective-permute-start.5 = (f32[4,16,128]{2,1,0:T(8,128)S(1)}, f32[4,16,128]{2,1,0:T(8,128)}, u32[]{:S(2)}, u32[]{:S(2)}) collective-permute-start(f32[4,16,128]{2,1,0:T(8,128)S(1)} %get-tuple-element.58), channel_id=1, source_target_pairs={{0,3},{1,2},{2,1},{3,0},{4,7},{5,6},{6,5},{7,4},{8,11},{9,10},{10,... | collective-permute-start | bytes 98312 | tf_op jit(solution)/shard_map/cond/branch_1_fun/ppermute | solution.py:413
  30.1 3.2 %collective-permute-start.4 = (f32[4,16,128]{2,1,0:T(8,128)S(1)}, f32[4,16,128]{2,1,0:T(8,128)}, u32[]{:S(2)}, u32[]{:S(2)}) collective-permute-start(f32[4,16,128]{2,1,0:T(8,128)S(1)} %get-tuple-element.58), channel_id=1, source_target_pairs={{0,2},{1,3},{2,0},{3,1},{4,6},{5,7},{6,4},{7,5},{8,10},{9,11},{10,... | collective-permute-start | bytes 98312 | tf_op jit(solution)/shard_map/cond/branch_1_fun/ppermute | solution.py:413
  33.3 1.9 %branch_1_fun.4 = bf16[2048,128]{1,0:T(8,128)(2,1)} custom-call(s32[3]{0:T(128)S(1)} %get-tuple-element.59.me, bf16[2048,128]{1,0:T(8,128)(2,1)S(1)} %get-tuple-element.60.third_ref, bf16[2048,128]{1,0:T(8,128)(2,1)S(1)} %get-tuple-element.61.outer_ref), custom_call_target="tpu_custom_call" | custom-call | flops 262144 | bytes 1572864 | tf_op jit(solution)/shard_map/cond/branch_1_fun/pallas_call | solution.py:290
  35.2 0.5 collective-permute-done.4
  35.7 1.6 %collective-permute-done.3 = f32[4,16,128]{2,1,0:T(8,128)} collective-permute-done((f32[4,16,128]{2,1,0:T(8,128)S(1)}, f32[4,16,128]{2,1,0:T(8,128)}, u32[]{:S(2)}, u32[]{:S(2)}) %collective-permute-start.3) | collective-permute-done | bytes 32800 | tf_op jit(solution)/shard_map/cond/branch_1_fun/ppermute | solution.py:413
  37.3 1.1 %collective-permute-start.19 = (bf16[2048,128]{1,0:T(8,128)(2,1)}, bf16[2048,128]{1,0:T(8,128)(2,1)S(1)}, u32[]{:S(2)}, u32[]{:S(2)}) collective-permute-start(bf16[2048,128]{1,0:T(8,128)(2,1)} %get-tuple-element.153), channel_id=1, source_target_pairs={{0,2},{1,3},{2,0},{3,1},{4,6},{5,7},{6,4},{7,5},{8,10},{9,11},{10,... | collective-permute-start | bytes 1572872 | tf_op jit(solution)/shard_map/ppermute | solution.py:463
  38.4 3.6 %collective-permute-start.20 = (bf16[2048,128]{1,0:T(8,128)(2,1)S(1)}, bf16[2048,128]{1,0:T(8,128)(2,1)S(1)}, u32[]{:S(2)}, u32[]{:S(2)}) collective-permute-start(bf16[2048,128]{1,0:T(8,128)(2,1)S(1)} %get-tuple-element.154), channel_id=1, source_target_pairs={{0,1},{3,2},{4,5},{7,6},{8,9},{11,10},{12,13},{15,14},{16,17},{19,... | collective-permute-start | bytes 1572872 | tf_op jit(solution)/shard_map/ppermute | solution.py:464
  42.0 0.0 copy-start
  42.0 11.3 %conditional.5 = (f32[4,16,128]{2,1,0:T(8,128)S(1)}, bf16[2,4,16,128]{3,2,1,0:T(8,128)(2,1)}, bf16[2,4,16,128]{3,2,1,0:T(8,128)(2,1)}, bf16[2,4,16,128]{3,2,1,0:...) conditional(s32[]{:T(128)} %convert_element_type.4, () %tuple.37, ...), branch_computations={%region_4.5_spmd, %region_5.6_spmd} | conditional | flops 805355520 | bytes 15253844 | solution.py:419
  42.1 0.0 copy-start.4
  42.1 0.1 collective-permute-start.9
  42.1 0.5 collective-permute-start.10
  42.6 0.0 copy-done.4
  42.7 0.8 %convert_bitcast_fusion = (bf16[1,4,16,128]{3,2,1,0:T(8,128)(2,1)S(1)}, f32[4,16,128]{2,1,0:T(8,128)S(1)}) fusion(f32[4,16,128]{2,1,0:T(8,128)} %get-tuple-element.67, f32[4,16,128]{2,1,0:T(8,128)} %get-tuple-element.66, f32[4,16,128]{2,1,0:T(8,128)} %copy-done.4, f32[4,16,128]{2,1,0:T(8,128)} %get-tuple-element.65), kind=kLoop, calls=%fused_computation.2 | loop fusion | flops 32768 | bytes 180224 | tf_op jit(solution)/shard_map/cond/branch_1_fun/broadcast_in_dim | solution.py:468
  43.5 0.1 collective-permute-start.8
  43.6 1.1 %collective-permute-done.8 = bf16[1,4,16,128]{3,2,1,0:T(8,128)(2,1)S(1)} collective-permute-done((bf16[1,4,16,128]{3,2,1,0:T(8,128)(2,1)S(1)}, bf16[1,4,16,128]{3,2,1,0:T(8,128)(2,1)S(1)}, u32[]{:S(2)}, u32[]{:S(2)}) %collective-permute-start.8) | collective-permute-done | bytes 16416 | tf_op jit(solution)/shard_map/cond/branch_1_fun/ppermute | solution.py:413
  44.7 0.6 pad_maximum_fusion
  45.4 2.3 %collective-permute-start.13 = (bf16[2,4,16,128]{3,2,1,0:T(8,128)(2,1)}, bf16[2,4,16,128]{3,2,1,0:T(8,128)(2,1)}, u32[]{:S(2)}, u32[]{:S(2)}) collective-permute-start(bf16[2,4,16,128]{3,2,1,0:T(8,128)(2,1)} %pad_maximum_fusion), channel_id=1, source_target_pairs={{0,24},{4,28},{8,16},{12,20},{16,8},{20,12},{24,0},{28,4},{1,25},{... | collective-permute-start | bytes 98312 | tf_op jit(solution)/shard_map/cond/branch_1_fun/ppermute | solution.py:413
  47.7 0.5 collective-permute-start.12
  48.2 0.6 collective-permute-start.11
  48.9 4.5 %branch_1_fun.5 = (f32[128,128]{1,0:T(8,128)}, bf16[128,8192]{1,0:T(8,128)(2,1)S(1)}) custom-call(s32[3]{0:T(128)S(1)} %get-tuple-element.71.me, bf16[256,128]{1,0:T(8,128)(2,1)S(1)} %get-tuple-element.72.inv_ref, bf16[128,8192]{1,0:T(8,128)(2,1)} %get-tuple-element.165.nt_ref, bf16[2048,128]{1,0:T(8,128)(2,1)} %get-tuple-element.74.weight_ref, ...), custom_call_target="tpu_custom_call" | custom-call | flops 805306368 | bytes 12582912 | tf_op jit(solution)/shard_map/cond/branch_1_fun/pallas_call | solution.py:259
  53.4 0.0 copy-start.2
  53.4 8.8 %shard_map.115 = (f32[2048,128]{1,0:T(8,128)}, bf16[128,128]{1,0:T(8,128)(2,1)}) custom-call(s32[3]{0:T(128)S(1)} %pad_add_fusion.me, bf16[256,128]{1,0:T(8,128)(2,1)S(1)} %copy-done.3, bf16[256,128]{1,0:T(8,128)(2,1)S(1)} %copy-done, bf16[128,8192]{1,0:T(8,128)(2,1)S(1)} %get-tuple-element.144.coef_ref, f32[128,128]{1,0:T(8,128)} %get-tuple-element.145.base_ref, ...), custom_call_target="tpu_custom_call" | custom-call | flops 2684354560 | bytes 4194304 | tf_op jit(solution)/shard_map/pallas_call | solution.py:378
  62.3 2.8 %shard_map.116 = f32[2048,128]{1,0:T(8,128)} custom-call(s32[3]{0:T(128)S(1)} %pad_add_fusion.me, bf16[256,128]{1,0:T(8,128)(2,1)S(1)} %copy-done.3, bf16[896,128]{1,0:T(8,128)(2,1)S(1)} %constant_dynamic-update-slice_fusion.refs_0_.idx_ref, f32[4,16,128]{2,1,0:T(8,128)S(1)} %get-tuple-element.156.val_ref, f32[2048,128]{1,0:T(8,128)S(1)} %bitcast.7, ...), custom_call_target="tpu_custom_call" | custom-call | flops 469762048 | bytes 5242880 | tf_op jit(solution)/shard_map/pallas_call | solution.py:202
  (28 shorter events, 0.1 us)
Async XLA Ops:
  0.6 15.0 %copy-start.5 = (bf16[128,128]{1,0:T(8,128)(2,1)S(1)}, bf16[128,128]{1,0:T(8,128)(2,1)}, u32[]{:S(2)}) copy-start(bf16[128,128]{1,0:T(8,128)(2,1)} %grad.1) | copy-start | bytes 98308
  2.4 11.3 %collective-permute-start.16 = (bf16[288,128]{1,0:T(8,128)(2,1)S(1)}, bf16[288,128]{1,0:T(8,128)(2,1)S(1)}, u32[]{:S(2)}, u32[]{:S(2)}) collective-permute-start(bf16[288,128]{1,0:T(8,128)(2,1)S(1)} %pad_maximum_fusion.1), channel_id=1, source_target_pairs={{0,3},{1,2},{2,1},{3,0},{4,7},{5,6},{6,5},{7,4},{8,11},{9,10},{10,... | collective-permute-start | bytes 221192 | tf_op jit(solution)/shard_map/ppermute | solution.py:413
  7.5 6.2 %collective-permute-start.15 = (bf16[288,128]{1,0:T(8,128)(2,1)S(1)}, bf16[288,128]{1,0:T(8,128)(2,1)S(1)}, u32[]{:S(2)}, u32[]{:S(2)}) collective-permute-start(bf16[288,128]{1,0:T(8,128)(2,1)S(1)} %pad_maximum_fusion.1), channel_id=1, source_target_pairs={{0,2},{1,3},{2,0},{3,1},{4,6},{5,7},{6,4},{7,5},{8,10},{9,11},{10,... | collective-permute-start | bytes 221192 | tf_op jit(solution)/shard_map/ppermute | solution.py:413
  7.5 4.7 %collective-permute-start.14 = (bf16[288,128]{1,0:T(8,128)(2,1)S(1)}, bf16[288,128]{1,0:T(8,128)(2,1)S(1)}, u32[]{:S(2)}, u32[]{:S(2)}) collective-permute-start(bf16[288,128]{1,0:T(8,128)(2,1)S(1)} %pad_maximum_fusion.1), channel_id=1, source_target_pairs={{0,1},{1,0},{2,3},{3,2},{4,5},{5,4},{6,7},{7,6},{8,9},{9,8},{10,11... | collective-permute-start | bytes 221192 | tf_op jit(solution)/shard_map/ppermute | solution.py:413
  13.8 14.1 %collective-permute-start.17 = (bf16[2048,128]{1,0:T(8,128)(2,1)S(1)}, bf16[2048,128]{1,0:T(8,128)(2,1)S(1)}, u32[]{:S(2)}, u32[]{:S(2)}) collective-permute-start(bf16[2048,128]{1,0:T(8,128)(2,1)S(1)} %get-tuple-element.129), channel_id=1, source_target_pairs={{0,1},{1,0},{2,3},{3,2},{4,5},{5,4},{6,7},{7,6},{8,9},{9,8},{10,11... | collective-permute-start | bytes 1572872 | tf_op jit(solution)/shard_map/ppermute | solution.py:445
  14.9 13.0 %collective-permute-start.18 = (bf16[2048,128]{1,0:T(8,128)(2,1)S(1)}, bf16[2048,128]{1,0:T(8,128)(2,1)S(1)}, u32[]{:S(2)}, u32[]{:S(2)}) collective-permute-start(bf16[2048,128]{1,0:T(8,128)(2,1)S(1)} %get-tuple-element.154), channel_id=1, source_target_pairs={{1,2},{2,1},{5,6},{6,5},{9,10},{10,9},{13,14},{14,13},{17,18},{18,... | collective-permute-start | bytes 1572872 | tf_op jit(solution)/shard_map/ppermute | solution.py:446
  15.6 10.6 %collective-permute-start.2 = (bf16[896,128]{1,0:T(8,128)(2,1)S(1)}, bf16[896,128]{1,0:T(8,128)(2,1)}, u32[]{:S(2)}, u32[]{:S(2)}) collective-permute-start(bf16[896,128]{1,0:T(8,128)(2,1)S(1)} %get-tuple-element.54.idx_ref), channel_id=1, source_target_pairs={{0,24},{4,28},{8,16},{12,20},{16,8},{20,12},{24,0},{28,4},{1,25},{... | collective-permute-start | bytes 688136 | tf_op jit(solution)/shard_map/cond/branch_1_fun/ppermute | solution.py:413
  18.1 9.7 %collective-permute-start.1 = (bf16[896,128]{1,0:T(8,128)(2,1)S(1)}, bf16[896,128]{1,0:T(8,128)(2,1)}, u32[]{:S(2)}, u32[]{:S(2)}) collective-permute-start(bf16[896,128]{1,0:T(8,128)(2,1)S(1)} %get-tuple-element.54.idx_ref), channel_id=1, source_target_pairs={{0,8},{4,12},{8,0},{12,4},{16,24},{20,28},{24,16},{28,20},{1,9},{5... | collective-permute-start | bytes 688136 | tf_op jit(solution)/shard_map/cond/branch_1_fun/ppermute | solution.py:413
  18.6 9.2 %collective-permute-start = (bf16[896,128]{1,0:T(8,128)(2,1)S(1)}, bf16[896,128]{1,0:T(8,128)(2,1)}, u32[]{:S(2)}, u32[]{:S(2)}) collective-permute-start(bf16[896,128]{1,0:T(8,128)(2,1)S(1)} %get-tuple-element.54.idx_ref), channel_id=1, source_target_pairs={{0,16},{4,20},{8,24},{12,28},{16,0},{20,4},{24,8},{28,12},{1,17},{... | collective-permute-start | bytes 688136 | tf_op jit(solution)/shard_map/cond/branch_1_fun/ppermute | solution.py:413
  19.2 0.8 %copy-start.1 = (bf16[256,128]{1,0:T(8,128)(2,1)S(1)}, bf16[256,128]{1,0:T(8,128)(2,1)}, u32[]{:S(2)}) copy-start(bf16[256,128]{1,0:T(8,128)(2,1)} %constant.108.clone.1.pair_ref) | copy-start | bytes 196612 | tf_op jit(solution)/shard_map/cond
  27.9 14.2 %copy-start.3 = (bf16[256,128]{1,0:T(8,128)(2,1)S(1)}, bf16[256,128]{1,0:T(8,128)(2,1)}, u32[]{:S(2)}) copy-start(bf16[256,128]{1,0:T(8,128)(2,1)} %constant.106.clone.inv_ref) | copy-start | bytes 196612
  27.9 9.4 %collective-permute-start.6 = (bf16[896,128]{1,0:T(8,128)(2,1)S(1)}, bf16[896,128]{1,0:T(8,128)(2,1)}, u32[]{:S(2)}, u32[]{:S(2)}) collective-permute-start(bf16[896,128]{1,0:T(8,128)(2,1)S(1)} %get-tuple-element.62), channel_id=1, source_target_pairs={{0,4},{4,0},{8,12},{12,8},{16,20},{20,16},{24,28},{28,24},{1,5},{5... | collective-permute-start | bytes 688136 | tf_op jit(solution)/shard_map/cond/branch_1_fun/ppermute | solution.py:413
  28.0 9.4 %collective-permute-start.7 = (bf16[896,128]{1,0:T(8,128)(2,1)}, bf16[896,128]{1,0:T(8,128)(2,1)}, u32[]{:S(2)}, u32[]{:S(2)}) collective-permute-start(bf16[896,128]{1,0:T(8,128)(2,1)} %get-tuple-element.63), channel_id=1, source_target_pairs={{0,4},{4,0},{8,12},{12,8},{16,20},{20,16},{24,28},{28,24},{1,5},{5... | collective-permute-start | bytes 688136 | tf_op jit(solution)/shard_map/cond/branch_1_fun/ppermute | solution.py:413
  28.5 6.8 %collective-permute-start.5 = (f32[4,16,128]{2,1,0:T(8,128)S(1)}, f32[4,16,128]{2,1,0:T(8,128)}, u32[]{:S(2)}, u32[]{:S(2)}) collective-permute-start(f32[4,16,128]{2,1,0:T(8,128)S(1)} %get-tuple-element.58), channel_id=1, source_target_pairs={{0,3},{1,2},{2,1},{3,0},{4,7},{5,6},{6,5},{7,4},{8,11},{9,10},{10,... | collective-permute-start | bytes 98312 | tf_op jit(solution)/shard_map/cond/branch_1_fun/ppermute | solution.py:413
  30.1 5.6 %collective-permute-start.4 = (f32[4,16,128]{2,1,0:T(8,128)S(1)}, f32[4,16,128]{2,1,0:T(8,128)}, u32[]{:S(2)}, u32[]{:S(2)}) collective-permute-start(f32[4,16,128]{2,1,0:T(8,128)S(1)} %get-tuple-element.58), channel_id=1, source_target_pairs={{0,2},{1,3},{2,0},{3,1},{4,6},{5,7},{6,4},{7,5},{8,10},{9,11},{10,... | collective-permute-start | bytes 98312 | tf_op jit(solution)/shard_map/cond/branch_1_fun/ppermute | solution.py:413
  33.3 4.0 %collective-permute-start.3 = (f32[4,16,128]{2,1,0:T(8,128)S(1)}, f32[4,16,128]{2,1,0:T(8,128)}, u32[]{:S(2)}, u32[]{:S(2)}) collective-permute-start(f32[4,16,128]{2,1,0:T(8,128)S(1)} %get-tuple-element.58), channel_id=1, source_target_pairs={{0,1},{1,0},{2,3},{3,2},{4,5},{5,4},{6,7},{7,6},{8,9},{9,8},{10,11... | collective-permute-start | bytes 98312 | tf_op jit(solution)/shard_map/cond/branch_1_fun/ppermute | solution.py:413
  37.3 24.9 %collective-permute-start.19 = (bf16[2048,128]{1,0:T(8,128)(2,1)}, bf16[2048,128]{1,0:T(8,128)(2,1)S(1)}, u32[]{:S(2)}, u32[]{:S(2)}) collective-permute-start(bf16[2048,128]{1,0:T(8,128)(2,1)} %get-tuple-element.153), channel_id=1, source_target_pairs={{0,2},{1,3},{2,0},{3,1},{4,6},{5,7},{6,4},{7,5},{8,10},{9,11},{10,... | collective-permute-start | bytes 1572872 | tf_op jit(solution)/shard_map/ppermute | solution.py:463
  38.4 23.8 %collective-permute-start.20 = (bf16[2048,128]{1,0:T(8,128)(2,1)S(1)}, bf16[2048,128]{1,0:T(8,128)(2,1)S(1)}, u32[]{:S(2)}, u32[]{:S(2)}) collective-permute-start(bf16[2048,128]{1,0:T(8,128)(2,1)S(1)} %get-tuple-element.154), channel_id=1, source_target_pairs={{0,1},{3,2},{4,5},{7,6},{8,9},{11,10},{12,13},{15,14},{16,17},{19,... | collective-permute-start | bytes 1572872 | tf_op jit(solution)/shard_map/ppermute | solution.py:464
  42.0 11.3 %copy-start = (bf16[256,128]{1,0:T(8,128)(2,1)S(1)}, bf16[256,128]{1,0:T(8,128)(2,1)}, u32[]{:S(2)}) copy-start(bf16[256,128]{1,0:T(8,128)(2,1)} %constant.107.clone.fwd_ref) | copy-start | bytes 196612
  42.1 0.6 copy-start.4
  42.1 3.3 %collective-permute-start.9 = (bf16[896,128]{1,0:T(8,128)(2,1)}, bf16[896,128]{1,0:T(8,128)(2,1)}, u32[]{:S(2)}, u32[]{:S(2)}) collective-permute-start(bf16[896,128]{1,0:T(8,128)(2,1)} %get-tuple-element.68.refs_2_), channel_id=1, source_target_pairs={{0,4},{4,0},{8,12},{12,8},{16,20},{20,16},{24,28},{28,24},{1,5},{5... | collective-permute-start | bytes 688136 | tf_op jit(solution)/shard_map/cond/branch_1_fun/ppermute | solution.py:413
  42.1 3.2 %collective-permute-start.10 = (bf16[896,128]{1,0:T(8,128)(2,1)}, bf16[896,128]{1,0:T(8,128)(2,1)}, u32[]{:S(2)}, u32[]{:S(2)}) collective-permute-start(bf16[896,128]{1,0:T(8,128)(2,1)} %get-tuple-element.69.refs_3_), channel_id=1, source_target_pairs={{0,4},{4,0},{8,12},{12,8},{16,20},{20,16},{24,28},{28,24},{1,5},{5... | collective-permute-start | bytes 688136 | tf_op jit(solution)/shard_map/cond/branch_1_fun/ppermute | solution.py:413
  43.5 1.2 %collective-permute-start.8 = (bf16[1,4,16,128]{3,2,1,0:T(8,128)(2,1)S(1)}, bf16[1,4,16,128]{3,2,1,0:T(8,128)(2,1)S(1)}, u32[]{:S(2)}, u32[]{:S(2)}) collective-permute-start(bf16[1,4,16,128]{3,2,1,0:T(8,128)(2,1)S(1)} %get-tuple-element.166), channel_id=1, source_target_pairs={{0,4},{4,0},{8,12},{12,8},{16,20},{20,16},{24,28},{28,24},{1,5},{5... | collective-permute-start | bytes 49160 | tf_op jit(solution)/shard_map/cond/branch_1_fun/ppermute | solution.py:413
  45.4 8.0 %collective-permute-start.13 = (bf16[2,4,16,128]{3,2,1,0:T(8,128)(2,1)}, bf16[2,4,16,128]{3,2,1,0:T(8,128)(2,1)}, u32[]{:S(2)}, u32[]{:S(2)}) collective-permute-start(bf16[2,4,16,128]{3,2,1,0:T(8,128)(2,1)} %pad_maximum_fusion), channel_id=1, source_target_pairs={{0,24},{4,28},{8,16},{12,20},{16,8},{20,12},{24,0},{28,4},{1,25},{... | collective-permute-start | bytes 98312 | tf_op jit(solution)/shard_map/cond/branch_1_fun/ppermute | solution.py:413
  47.7 5.7 %collective-permute-start.12 = (bf16[2,4,16,128]{3,2,1,0:T(8,128)(2,1)}, bf16[2,4,16,128]{3,2,1,0:T(8,128)(2,1)}, u32[]{:S(2)}, u32[]{:S(2)}) collective-permute-start(bf16[2,4,16,128]{3,2,1,0:T(8,128)(2,1)} %pad_maximum_fusion), channel_id=1, source_target_pairs={{0,8},{4,12},{8,0},{12,4},{16,24},{20,28},{24,16},{28,20},{1,9},{5... | collective-permute-start | bytes 98312 | tf_op jit(solution)/shard_map/cond/branch_1_fun/ppermute | solution.py:413
  48.2 5.1 %collective-permute-start.11 = (bf16[2,4,16,128]{3,2,1,0:T(8,128)(2,1)}, bf16[2,4,16,128]{3,2,1,0:T(8,128)(2,1)}, u32[]{:S(2)}, u32[]{:S(2)}) collective-permute-start(bf16[2,4,16,128]{3,2,1,0:T(8,128)(2,1)} %pad_maximum_fusion), channel_id=1, source_target_pairs={{0,16},{4,20},{8,24},{12,28},{16,0},{20,4},{24,8},{28,12},{1,17},{... | collective-permute-start | bytes 98312 | tf_op jit(solution)/shard_map/cond/branch_1_fun/ppermute | solution.py:413
  53.4 8.9 %copy-start.2 = (f32[1,2048,128]{2,1,0:T(8,128)S(1)}, f32[1,2048,128]{2,1,0:T(8,128)}, u32[]{:S(2)}) copy-start(f32[1,2048,128]{2,1,0:T(8,128)} %param.17) | copy-start | bytes 3145732

commit v4 on v3

--- a/solution.py
+++ b/solution.py
@@ -85,7 +85,7 @@
         cost_estimate=pl.CostEstimate(
             flops=2 * count * rows * width * toks, bytes_accessed=count * rows * (width + toks) * 2, transcendentals=0
         ),
-        compiler_params=pltpu.CompilerParams(vmem_limit_bytes=32 * 2**20),
+        compiler_params=pltpu.CompilerParams(vmem_limit_bytes=16 * 2**20),
     )(me, tokens, grad_out)
 
 
@@ -168,7 +168,7 @@
         cost_estimate=pl.CostEstimate(
             flops=2 * n_f * groups * LANES**3 * 6, bytes_accessed=4 * 2**20, transcendentals=0
         ),
-        compiler_params=pltpu.CompilerParams(vmem_limit_bytes=32 * 2**20),
+        compiler_params=pltpu.CompilerParams(vmem_limit_bytes=16 * 2**20),
     )(me, inv, idx, tokens, grad_out, moment)
 
 
@@ -217,7 +217,7 @@
         cost_estimate=pl.CostEstimate(
             flops=2 * groups * LANES**3 * 7, bytes_accessed=5 * rows * width * 4, transcendentals=0
         ),
-        compiler_params=pltpu.CompilerParams(vmem_limit_bytes=32 * 2**20),
+        compiler_params=pltpu.CompilerParams(vmem_limit_bytes=16 * 2**20),
     )(me, inv, idx, values, moment, *parts)
 
 
@@ -268,7 +268,7 @@
         cost_estimate=pl.CostEstimate(
             flops=2 * toks * width * out * 3, bytes_accessed=6 * toks * width * 2, transcendentals=0
         ),
-        compiler_params=pltpu.CompilerParams(vmem_limit_bytes=48 * 2**20),
+        compiler_params=pltpu.CompilerParams(vmem_limit_bytes=20 * 2**20),
     )(me, inv, next_tokens, weight, *pieces)
 
 
@@ -299,6 +299,7 @@
     idx_refs, val_refs = refs[:n_r], refs[n_r : n_r + n_r // 2]
     up_ref, out_ref, acc_ref, sort_ref, dense_ref = refs[n_r + n_r // 2 :]
     step = pl.program_id(0)
+    slot = jnp.minimum(step, 1)
     inv = inv_ref[...]
     fwd = fwd_ref[...]
 
@@ -342,25 +343,25 @@
         diagonal = lambda cross, i: jnp.where(low, cross[i : i + TILE, i : i + LANES], cross[i + TILE : i + LANES, i : i + LANES])
         denses = [jnp.concatenate([diagonal(cross, 0), diagonal(cross, LANES)], axis=0) for cross in crosses]
         for i, dense in zip(of, denses):
-            dense_ref[i * LANES : (i + 1) * LANES, :] = jnp.concatenate(split(dense), axis=1)
+            dense_ref[slot, i * LANES : (i + 1) * LANES, :] = jnp.concatenate(split(dense), axis=1)
 
     for g in range(0, groups, batch):
         some_groups(g)
 
-    both = dot(coef_ref[...], dense_ref[...])
+    both = dot(coef_ref[...], dense_ref[slot])
     acc_ref[...] += both[:, :LANES] + both[:, LANES:]
 
-    @pl.when(step == 0)
-    def _():
-        c_hi, c_lo = inv[:LANES], inv[LANES:]
-        f_hi, f_lo = fwd[:LANES], fwd[LANES:]
-        table = jnp.concatenate([c_hi, c_lo], axis=1)
-        last = jnp.concatenate([f_hi, f_lo, f_hi], axis=0)
-        parts = [dense_ref[g * LANES : (g + 1) * LANES, :] for g in range(groups)]
-        boths = [dot(table, jnp.concatenate([part, part], axis=0)) for part in parts]
-        halves = [split(both[:, :LANES] + both[:, LANES:]) for both in boths]
-        lines = jnp.concatenate([jnp.concatenate([hi, hi, lo], axis=1) for hi, lo in halves], axis=0)
-        up_ref[...] = dot(lines, last)
+    c_hi, c_lo = inv[:LANES], inv[LANES:]
+    f_hi, f_lo = fwd[:LANES], fwd[LANES:]
+    table = jnp.concatenate([c_hi, c_lo], axis=1)
+    last = jnp.concatenate([f_hi, f_lo, f_hi], axis=0)
+    count = up_ref.shape[0] // LANES
+    of = [pl.ds(pl.multiple_of((step * count + g) * LANES, LANES), LANES) for g in range(count)]
+    parts = [dense_ref[0, part, :] for part in of]
+    boths = [dot(table, jnp.concatenate([part, part], axis=0)) for part in parts]
+    halves = [split(both[:, :LANES] + both[:, LANES:]) for both in boths]
+    lines = jnp.concatenate([jnp.concatenate([hi, hi, lo], axis=1) for hi, lo in halves], axis=0)
+    up_ref[...] = dot(lines, last)
 
     @pl.when(step == pl.num_programs(0) - 1)
     def _():
@@ -389,13 +390,13 @@
             + [pl.BlockSpec((2 * groups, LANES), lambda s, me: (idx_block(s, unit), 0)) for _ in pieces]
             + [pl.BlockSpec((2, 1, groups, LANES), lambda s, me: (0, me[0] ^ s, 0, 0)) for _ in sent],
             out_specs=[
-                pl.BlockSpec((rows, width), lambda s, me: (0, 0)),
+                pl.BlockSpec((rows // n_f, width), lambda s, me: (s, 0)),
                 pl.BlockSpec((toks, width), lambda s, me: (0, 0)),
             ],
             scratch_shapes=[
                 pltpu.VMEM((toks, width), jnp.float32),
                 pltpu.VMEM((3, n_r // 4, 4, groups, LANES), jnp.float32),
-                pltpu.VMEM((rows, 2 * LANES), jnp.bfloat16),
+                pltpu.VMEM((2, rows, 2 * LANES), jnp.bfloat16),
             ],
         ),
         out_shape=[
@@ -405,7 +406,7 @@
         cost_estimate=pl.CostEstimate(
             flops=2 * n_f * groups * LANES**3 * (n_r + 2), bytes_accessed=4 * 2**20, transcendentals=0
         ),
-        compiler_params=pltpu.CompilerParams(vmem_limit_bytes=32 * 2**20),
+        compiler_params=pltpu.CompilerParams(vmem_limit_bytes=16 * 2**20),
     )(me, inv, fwd, coef, base, *pieces, *sent)
 
 

time: 65.6 us -> 65.4 us (level)
  Pallas kernels: 28.1 us -> 27.3 us
    pallas_call x1, Pallas kernels: 8.83 us -> 8.04 us  [totals(): pl.pallas_call(functools.partial(total_kernel, groups, n_r), grid_spec=pl...]
  transfers between devices with their start and end apart: 21 -> 21, of which waited for: 6 -> 7; matrix products, arithmetic and copies ran while one was open for 2% -> 2% of each run, Pallas kernels for 39% -> 38%
where the time goes in v4:
time: 65.4 us; the launch traced here: 64.9 us
  Pallas kernels  27.3 us (42%)
  starting transfers between devices  25.4 us (39%)
  waiting for transfers between devices  7.18 us (11%)
  local copies, waits for them, and re-layouts  2.64 us (4%)
  other arithmetic  1.56 us (2%)
  between operations  0.77 us (1%)
    ppermute x17, starting transfers between devices, swap(): return lax.ppermute(x, axis, [(i, i ^ mask) for i in range(size)])  18.9 us
    pallas_call x1, Pallas kernels, totals(): pl.pallas_call(functools.partial(total_kernel, groups, n_r), grid_spec=pl...  8.04 us
    ppermute x17, waiting for transfers between devices, swap(): return lax.ppermute(x, axis, [(i, i ^ mask) for i in range(size)])  6.58 us
    pallas_call x1, Pallas kernels, select_values(): pl.pallas_call(functools.partial(select_kernel, groups), grid_spec=pltpu....  6.2 us
    pallas_call x1, Pallas kernels, project(): pl.pallas_call(functools.partial(project_kernel, n_r, n_f, extra), grid_s...  4.48 us
    pallas_call x1, Pallas kernels, partial_chunks(): pl.pallas_call(partial_kernel, grid_spec=pltpu.PrefetchScalarGridSpec(num...  3.76 us
    ppermute x1, starting transfers between devices, line_fast(): far = lax.ppermute(second, 'fsdp', [(0, 1), (3, 2)])  3.59 us
    pallas_call x1, Pallas kernels, new_moment_of(): pl.pallas_call(functools.partial(moment_kernel, groups), grid_spec=pltpu....  2.84 us
  transfers between devices with their start and end apart: 21, of which 7 were waited for; matrix products, arithmetic and copies ran while one was open for 2% of the time, Pallas kernels for 38%

profile of v4, /device:TPU:0, one launch (start us, length us, event | category | flops | bytes accessed | tf_op | source)
XLA Modules:
  0.0 64.9 jit_solution(12358756746071800957)
XLA Ops:
  0.6 0.0 copy-start.5
  0.7 0.9 %reshape_squeeze.3 = s32[16,128]{1,0:T(8,128)S(1)} reshape(s32[1,32,2,32]{3,2,1,0:T(2,128)} %param.20) | data formatting | bytes 16384 | tf_op jit(solution)/shard_map/reshape;squeeze | solution.py:433
  1.5 0.8 %constant_dynamic-slice_fusion = bf16[256,128]{1,0:T(8,128)(2,1)S(1)} fusion(bf16[2048,128]{1,0:T(8,128)(2,1)} %param.18, s32[]{:T(128)S(6)} %select_n.46), kind=kLoop, calls=%fused_computation.35 | loop fusion | bytes 131076 | tf_op jit(solution)/shard_map/dynamic_slice | solution.py:439
  2.4 5.1 %collective-permute-start.16 = (bf16[288,128]{1,0:T(8,128)(2,1)S(1)}, bf16[288,128]{1,0:T(8,128)(2,1)S(1)}, u32[]{:S(2)}, u32[]{:S(2)}) collective-permute-start(bf16[288,128]{1,0:T(8,128)(2,1)S(1)} %pad_maximum_fusion.1), channel_id=1, source_target_pairs={{0,3},{1,2},{2,1},{3,0},{4,7},{5,6},{6,5},{7,4},{8,11},{9,10},{10,... | collective-permute-start | bytes 221192 | tf_op jit(solution)/shard_map/ppermute | solution.py:414
  7.5 0.6 collective-permute-start.14
  8.2 0.1 pad_add_fusion.me
  8.3 3.8 %shard_map.114 = (bf16[2048,128]{1,0:T(8,128)(2,1)S(1)}, bf16[2048,128]{1,0:T(8,128)(2,1)S(1)}, bf16[2048,128]{1,0:T(8,128)(2,1)S(1)}, bf16[2048,128]{1,0:T(8,128)(2,1)S(1)}) custom-call(s32[3]{0:T(128)S(1)} %pad_add_fusion.me, bf16[128,8192]{1,0:T(8,128)(2,1)} %tok.1, bf16[128,128]{1,0:T(8,128)(2,1)} %grad.1), custom_call_target="tpu_custom_call" | custom-call | flops 268435456 | bytes 4194304 | tf_op jit(solution)/shard_map/pallas_call | solution.py:73
  12.0 0.2 collective-permute-done.14
  12.3 1.5 %collective-permute-done.15 = bf16[288,128]{1,0:T(8,128)(2,1)S(1)} collective-permute-done((bf16[288,128]{1,0:T(8,128)(2,1)S(1)}, bf16[288,128]{1,0:T(8,128)(2,1)S(1)}, u32[]{:S(2)}, u32[]{:S(2)}) %collective-permute-start.15) | collective-permute-done | bytes 73760 | tf_op jit(solution)/shard_map/ppermute | solution.py:414
  13.8 0.0 collective-permute-done.16
  13.8 1.1 %collective-permute-start.17 = (bf16[2048,128]{1,0:T(8,128)(2,1)S(1)}, bf16[2048,128]{1,0:T(8,128)(2,1)S(1)}, u32[]{:S(2)}, u32[]{:S(2)}) collective-permute-start(bf16[2048,128]{1,0:T(8,128)(2,1)S(1)} %get-tuple-element.129), channel_id=1, source_target_pairs={{0,1},{1,0},{2,3},{3,2},{4,5},{5,4},{6,7},{7,6},{8,9},{9,8},{10,11... | collective-permute-start | bytes 1572872 | tf_op jit(solution)/shard_map/ppermute | solution.py:446
  14.9 0.7 %collective-permute-start.18 = (bf16[2048,128]{1,0:T(8,128)(2,1)S(1)}, bf16[2048,128]{1,0:T(8,128)(2,1)S(1)}, u32[]{:S(2)}, u32[]{:S(2)}) collective-permute-start(bf16[2048,128]{1,0:T(8,128)(2,1)S(1)} %get-tuple-element.154), channel_id=1, source_target_pairs={{1,2},{2,1},{5,6},{6,5},{9,10},{10,9},{13,14},{14,13},{17,18},{18,... | collective-permute-start | bytes 1572872 | tf_op jit(solution)/shard_map/ppermute | solution.py:447
  15.6 12.3 %conditional.3 = (f32[4,16,128]{2,1,0:T(8,128)S(1)}, bf16[896,128]{1,0:T(8,128)(2,1)}, bf16[896,128]{1,0:T(8,128)(2,1)}, bf16[896,128]{1,0:T(8,128)(2,1)}) conditional(s32[]{:T(128)} %convert_element_type.4, () %tuple.38, (s32[3]{0:T(128)S(1)}, (), bf16[896,128]{1,0:T(8,128)(2,1)S(1)}, bf16[128,8192]{1,0:T(8,128)(2,1)}, ...), branch_computations={%region_0.1_spmd, %region_1.2_spmd} | conditional | flops 1610612736 | bytes 7209140 | solution.py:420
  15.6 2.5 %collective-permute-start.2 = (bf16[896,128]{1,0:T(8,128)(2,1)S(1)}, bf16[896,128]{1,0:T(8,128)(2,1)}, u32[]{:S(2)}, u32[]{:S(2)}) collective-permute-start(bf16[896,128]{1,0:T(8,128)(2,1)S(1)} %get-tuple-element.54.idx_ref), channel_id=1, source_target_pairs={{0,24},{4,28},{8,16},{12,20},{16,8},{20,12},{24,0},{28,4},{1,25},{... | collective-permute-start | bytes 688136 | tf_op jit(solution)/shard_map/cond/branch_1_fun/ppermute | solution.py:414
  18.1 0.5 collective-permute-start.1
  18.6 0.5 collective-permute-start
  19.2 0.8 %copy-done.1 = bf16[256,128]{1,0:T(8,128)(2,1)S(1)} copy-done((bf16[256,128]{1,0:T(8,128)(2,1)S(1)}, bf16[256,128]{1,0:T(8,128)(2,1)}, u32[]{:S(2)}) %copy-start.1) | copy-done | bytes 65560 | tf_op jit(solution)/shard_map/cond
  20.0 6.2 %branch_1_fun.3 = f32[4,16,128]{2,1,0:T(8,128)S(1)} custom-call(s32[3]{0:T(128)S(1)} %get-tuple-element.52.me, bf16[256,128]{1,0:T(8,128)(2,1)S(1)} %copy-done.1, bf16[896,128]{1,0:T(8,128)(2,1)S(1)} %get-tuple-element.54.idx_ref, bf16[128,8192]{1,0:T(8,128)(2,1)} %get-tuple-element.55.tok_ref, bf16[128,128]{1,0:T(8,128)(2,1)S(1)} %get-tuple-element.56.grad_ref, ...), custom_call_target="tpu_custom_call" | custom-call | flops 1610612736 | bytes 4194304 | tf_op jit(solution)/shard_map/cond/branch_1_fun/pallas_call | solution.py:153
  26.2 1.6 %collective-permute-done.1 = bf16[896,128]{1,0:T(8,128)(2,1)} collective-permute-done((bf16[896,128]{1,0:T(8,128)(2,1)S(1)}, bf16[896,128]{1,0:T(8,128)(2,1)}, u32[]{:S(2)}, u32[]{:S(2)}) %collective-permute-start.1) | collective-permute-done | bytes 229408 | tf_op jit(solution)/shard_map/cond/branch_1_fun/ppermute | solution.py:414
  27.9 0.0 collective-permute-done.17.outer_ref
  27.9 9.4 %conditional.4 = (f32[4,16,128]{2,1,0:T(8,128)}, f32[4,16,128]{2,1,0:T(8,128)}, f32[4,16,128]{2,1,0:T(8,128)}, bf16[2048,128]{1,0:T(8,128)(2,1)}, bf16[896,128]{1,0:T(8,128)(2,1)}, /*index=5*/bf16[896,128]{1,0:T(8,128)(2,1)}) conditional(s32[]{:T(128)} %convert_element_type.4, () %tuple.41, (f32[4,16,128]{2,1,0:T(8,128)S(1)}, s32[3]{0:T(128)S(1)}, ...), branch_computations={%region_2.3_spmd, %region_3.4_spmd} | conditional | flops 262144 | bytes 3801336 | solution.py:420
  27.9 0.1 collective-permute-start.6
  28.0 0.5 collective-permute-start.7
  28.5 1.6 %collective-permute-start.5 = (f32[4,16,128]{2,1,0:T(8,128)S(1)}, f32[4,16,128]{2,1,0:T(8,128)}, u32[]{:S(2)}, u32[]{:S(2)}) collective-permute-start(f32[4,16,128]{2,1,0:T(8,128)S(1)} %get-tuple-element.58), channel_id=1, source_target_pairs={{0,3},{1,2},{2,1},{3,0},{4,7},{5,6},{6,5},{7,4},{8,11},{9,10},{10,... | collective-permute-start | bytes 98312 | tf_op jit(solution)/shard_map/cond/branch_1_fun/ppermute | solution.py:414
  30.1 3.2 %collective-permute-start.4 = (f32[4,16,128]{2,1,0:T(8,128)S(1)}, f32[4,16,128]{2,1,0:T(8,128)}, u32[]{:S(2)}, u32[]{:S(2)}) collective-permute-start(f32[4,16,128]{2,1,0:T(8,128)S(1)} %get-tuple-element.58), channel_id=1, source_target_pairs={{0,2},{1,3},{2,0},{3,1},{4,6},{5,7},{6,4},{7,5},{8,10},{9,11},{10,... | collective-permute-start | bytes 98312 | tf_op jit(solution)/shard_map/cond/branch_1_fun/ppermute | solution.py:414
  33.3 1.9 %branch_1_fun.4 = bf16[2048,128]{1,0:T(8,128)(2,1)} custom-call(s32[3]{0:T(128)S(1)} %get-tuple-element.59.me, bf16[2048,128]{1,0:T(8,128)(2,1)S(1)} %get-tuple-element.60.third_ref, bf16[2048,128]{1,0:T(8,128)(2,1)S(1)} %get-tuple-element.61.outer_ref), custom_call_target="tpu_custom_call" | custom-call | flops 262144 | bytes 1572864 | tf_op jit(solution)/shard_map/cond/branch_1_fun/pallas_call | solution.py:290
  35.2 0.5 collective-permute-done.4
  35.7 1.6 %collective-permute-done.3 = f32[4,16,128]{2,1,0:T(8,128)} collective-permute-done((f32[4,16,128]{2,1,0:T(8,128)S(1)}, f32[4,16,128]{2,1,0:T(8,128)}, u32[]{:S(2)}, u32[]{:S(2)}) %collective-permute-start.3) | collective-permute-done | bytes 32800 | tf_op jit(solution)/shard_map/cond/branch_1_fun/ppermute | solution.py:414
  37.3 1.1 %collective-permute-start.19 = (bf16[2048,128]{1,0:T(8,128)(2,1)}, bf16[2048,128]{1,0:T(8,128)(2,1)S(1)}, u32[]{:S(2)}, u32[]{:S(2)}) collective-permute-start(bf16[2048,128]{1,0:T(8,128)(2,1)} %get-tuple-element.153), channel_id=1, source_target_pairs={{0,2},{1,3},{2,0},{3,1},{4,6},{5,7},{6,4},{7,5},{8,10},{9,11},{10,... | collective-permute-start | bytes 1572872 | tf_op jit(solution)/shard_map/ppermute | solution.py:464
  38.4 3.6 %collective-permute-start.20 = (bf16[2048,128]{1,0:T(8,128)(2,1)S(1)}, bf16[2048,128]{1,0:T(8,128)(2,1)S(1)}, u32[]{:S(2)}, u32[]{:S(2)}) collective-permute-start(bf16[2048,128]{1,0:T(8,128)(2,1)S(1)} %get-tuple-element.154), channel_id=1, source_target_pairs={{0,1},{3,2},{4,5},{7,6},{8,9},{11,10},{12,13},{15,14},{16,17},{19,... | collective-permute-start | bytes 1572872 | tf_op jit(solution)/shard_map/ppermute | solution.py:465
  42.0 0.0 copy-start
  42.0 11.3 %conditional.5 = (f32[4,16,128]{2,1,0:T(8,128)S(1)}, bf16[2,4,16,128]{3,2,1,0:T(8,128)(2,1)}, bf16[2,4,16,128]{3,2,1,0:T(8,128)(2,1)}, bf16[2,4,16,128]{3,2,1,0:...) conditional(s32[]{:T(128)} %convert_element_type.4, () %tuple.37, ...), branch_computations={%region_4.5_spmd, %region_5.6_spmd} | conditional | flops 805355520 | bytes 15253844 | solution.py:420
  42.1 0.0 copy-start.4
  42.1 0.1 collective-permute-start.9
  42.1 0.5 collective-permute-start.10
  42.6 0.0 copy-done.4
  42.7 0.8 %convert_bitcast_fusion = (bf16[1,4,16,128]{3,2,1,0:T(8,128)(2,1)S(1)}, f32[4,16,128]{2,1,0:T(8,128)S(1)}) fusion(f32[4,16,128]{2,1,0:T(8,128)} %get-tuple-element.67, f32[4,16,128]{2,1,0:T(8,128)} %get-tuple-element.66, f32[4,16,128]{2,1,0:T(8,128)} %copy-done.4, f32[4,16,128]{2,1,0:T(8,128)} %get-tuple-element.65), kind=kLoop, calls=%fused_computation.2 | loop fusion | flops 32768 | bytes 180224 | tf_op jit(solution)/shard_map/cond/branch_1_fun/broadcast_in_dim | solution.py:469
  43.5 0.1 collective-permute-start.8
  43.6 1.1 %collective-permute-done.8 = bf16[1,4,16,128]{3,2,1,0:T(8,128)(2,1)S(1)} collective-permute-done((bf16[1,4,16,128]{3,2,1,0:T(8,128)(2,1)S(1)}, bf16[1,4,16,128]{3,2,1,0:T(8,128)(2,1)S(1)}, u32[]{:S(2)}, u32[]{:S(2)}) %collective-permute-start.8) | collective-permute-done | bytes 16416 | tf_op jit(solution)/shard_map/cond/branch_1_fun/ppermute | solution.py:414
  44.7 0.6 pad_maximum_fusion
  45.4 2.3 %collective-permute-start.13 = (bf16[2,4,16,128]{3,2,1,0:T(8,128)(2,1)}, bf16[2,4,16,128]{3,2,1,0:T(8,128)(2,1)}, u32[]{:S(2)}, u32[]{:S(2)}) collective-permute-start(bf16[2,4,16,128]{3,2,1,0:T(8,128)(2,1)} %pad_maximum_fusion), channel_id=1, source_target_pairs={{0,24},{4,28},{8,16},{12,20},{16,8},{20,12},{24,0},{28,4},{1,25},{... | collective-permute-start | bytes 98312 | tf_op jit(solution)/shard_map/cond/branch_1_fun/ppermute | solution.py:414
  47.7 0.5 collective-permute-start.12
  48.2 0.6 collective-permute-start.11
  48.9 4.5 %branch_1_fun.5 = (f32[128,128]{1,0:T(8,128)S(1)}, bf16[128,8192]{1,0:T(8,128)(2,1)S(1)}) custom-call(s32[3]{0:T(128)S(1)} %get-tuple-element.71.me, bf16[256,128]{1,0:T(8,128)(2,1)S(1)} %get-tuple-element.72.inv_ref, bf16[128,8192]{1,0:T(8,128)(2,1)} %get-tuple-element.165.nt_ref, bf16[2048,128]{1,0:T(8,128)(2,1)} %get-tuple-element.74.weight_ref, ...), custom_call_target="tpu_custom_call" | custom-call | flops 805306368 | bytes 12582912 | tf_op jit(solution)/shard_map/cond/branch_1_fun/pallas_call | solution.py:259
  53.4 0.0 copy-start.2
  53.4 8.0 %shard_map.115 = (f32[2048,128]{1,0:T(8,128)}, bf16[128,128]{1,0:T(8,128)(2,1)}) custom-call(s32[3]{0:T(128)S(1)} %pad_add_fusion.me, bf16[256,128]{1,0:T(8,128)(2,1)S(1)} %copy-done.3, bf16[256,128]{1,0:T(8,128)(2,1)S(1)} %copy-done, bf16[128,8192]{1,0:T(8,128)(2,1)S(1)} %get-tuple-element.144.coef_ref, f32[128,128]{1,0:T(8,128)S(1)} %get-tuple-element.145.base_ref, ...), custom_call_target="tpu_custom_call" | custom-call | flops 2684354560 | bytes 4194304 | tf_op jit(solution)/shard_map/pallas_call | solution.py:379
  61.4 0.6 collective-permute-done.19.two_ref
  62.0 2.8 %shard_map.116 = f32[2048,128]{1,0:T(8,128)} custom-call(s32[3]{0:T(128)S(1)} %pad_add_fusion.me, bf16[256,128]{1,0:T(8,128)(2,1)S(1)} %copy-done.3, bf16[896,128]{1,0:T(8,128)(2,1)S(1)} %constant_dynamic-update-slice_fusion.refs_0_.idx_ref, f32[4,16,128]{2,1,0:T(8,128)S(1)} %get-tuple-element.156.val_ref, f32[2048,128]{1,0:T(8,128)S(1)} %bitcast.7, ...), custom_call_target="tpu_custom_call" | custom-call | flops 469762048 | bytes 5242880 | tf_op jit(solution)/shard_map/pallas_call | solution.py:202
  (28 shorter events, 0.1 us)
Async XLA Ops:
  0.6 15.0 %copy-start.5 = (bf16[128,128]{1,0:T(8,128)(2,1)S(1)}, bf16[128,128]{1,0:T(8,128)(2,1)}, u32[]{:S(2)}) copy-start(bf16[128,128]{1,0:T(8,128)(2,1)} %grad.1) | copy-start | bytes 98308
  2.4 11.3 %collective-permute-start.16 = (bf16[288,128]{1,0:T(8,128)(2,1)S(1)}, bf16[288,128]{1,0:T(8,128)(2,1)S(1)}, u32[]{:S(2)}, u32[]{:S(2)}) collective-permute-start(bf16[288,128]{1,0:T(8,128)(2,1)S(1)} %pad_maximum_fusion.1), channel_id=1, source_target_pairs={{0,3},{1,2},{2,1},{3,0},{4,7},{5,6},{6,5},{7,4},{8,11},{9,10},{10,... | collective-permute-start | bytes 221192 | tf_op jit(solution)/shard_map/ppermute | solution.py:414
  7.5 6.2 %collective-permute-start.15 = (bf16[288,128]{1,0:T(8,128)(2,1)S(1)}, bf16[288,128]{1,0:T(8,128)(2,1)S(1)}, u32[]{:S(2)}, u32[]{:S(2)}) collective-permute-start(bf16[288,128]{1,0:T(8,128)(2,1)S(1)} %pad_maximum_fusion.1), channel_id=1, source_target_pairs={{0,2},{1,3},{2,0},{3,1},{4,6},{5,7},{6,4},{7,5},{8,10},{9,11},{10,... | collective-permute-start | bytes 221192 | tf_op jit(solution)/shard_map/ppermute | solution.py:414
  7.5 4.7 %collective-permute-start.14 = (bf16[288,128]{1,0:T(8,128)(2,1)S(1)}, bf16[288,128]{1,0:T(8,128)(2,1)S(1)}, u32[]{:S(2)}, u32[]{:S(2)}) collective-permute-start(bf16[288,128]{1,0:T(8,128)(2,1)S(1)} %pad_maximum_fusion.1), channel_id=1, source_target_pairs={{0,1},{1,0},{2,3},{3,2},{4,5},{5,4},{6,7},{7,6},{8,9},{9,8},{10,11... | collective-permute-start | bytes 221192 | tf_op jit(solution)/shard_map/ppermute | solution.py:414
  13.8 14.1 %collective-permute-start.17 = (bf16[2048,128]{1,0:T(8,128)(2,1)S(1)}, bf16[2048,128]{1,0:T(8,128)(2,1)S(1)}, u32[]{:S(2)}, u32[]{:S(2)}) collective-permute-start(bf16[2048,128]{1,0:T(8,128)(2,1)S(1)} %get-tuple-element.129), channel_id=1, source_target_pairs={{0,1},{1,0},{2,3},{3,2},{4,5},{5,4},{6,7},{7,6},{8,9},{9,8},{10,11... | collective-permute-start | bytes 1572872 | tf_op jit(solution)/shard_map/ppermute | solution.py:446
  14.9 13.0 %collective-permute-start.18 = (bf16[2048,128]{1,0:T(8,128)(2,1)S(1)}, bf16[2048,128]{1,0:T(8,128)(2,1)S(1)}, u32[]{:S(2)}, u32[]{:S(2)}) collective-permute-start(bf16[2048,128]{1,0:T(8,128)(2,1)S(1)} %get-tuple-element.154), channel_id=1, source_target_pairs={{1,2},{2,1},{5,6},{6,5},{9,10},{10,9},{13,14},{14,13},{17,18},{18,... | collective-permute-start | bytes 1572872 | tf_op jit(solution)/shard_map/ppermute | solution.py:447
  15.6 10.6 %collective-permute-start.2 = (bf16[896,128]{1,0:T(8,128)(2,1)S(1)}, bf16[896,128]{1,0:T(8,128)(2,1)}, u32[]{:S(2)}, u32[]{:S(2)}) collective-permute-start(bf16[896,128]{1,0:T(8,128)(2,1)S(1)} %get-tuple-element.54.idx_ref), channel_id=1, source_target_pairs={{0,24},{4,28},{8,16},{12,20},{16,8},{20,12},{24,0},{28,4},{1,25},{... | collective-permute-start | bytes 688136 | tf_op jit(solution)/shard_map/cond/branch_1_fun/ppermute | solution.py:414
  18.1 9.7 %collective-permute-start.1 = (bf16[896,128]{1,0:T(8,128)(2,1)S(1)}, bf16[896,128]{1,0:T(8,128)(2,1)}, u32[]{:S(2)}, u32[]{:S(2)}) collective-permute-start(bf16[896,128]{1,0:T(8,128)(2,1)S(1)} %get-tuple-element.54.idx_ref), channel_id=1, source_target_pairs={{0,8},{4,12},{8,0},{12,4},{16,24},{20,28},{24,16},{28,20},{1,9},{5... | collective-permute-start | bytes 688136 | tf_op jit(solution)/shard_map/cond/branch_1_fun/ppermute | solution.py:414
  18.6 9.2 %collective-permute-start = (bf16[896,128]{1,0:T(8,128)(2,1)S(1)}, bf16[896,128]{1,0:T(8,128)(2,1)}, u32[]{:S(2)}, u32[]{:S(2)}) collective-permute-start(bf16[896,128]{1,0:T(8,128)(2,1)S(1)} %get-tuple-element.54.idx_ref), channel_id=1, source_target_pairs={{0,16},{4,20},{8,24},{12,28},{16,0},{20,4},{24,8},{28,12},{1,17},{... | collective-permute-start | bytes 688136 | tf_op jit(solution)/shard_map/cond/branch_1_fun/ppermute | solution.py:414
  19.2 0.8 %copy-start.1 = (bf16[256,128]{1,0:T(8,128)(2,1)S(1)}, bf16[256,128]{1,0:T(8,128)(2,1)}, u32[]{:S(2)}) copy-start(bf16[256,128]{1,0:T(8,128)(2,1)} %constant.108.clone.1.pair_ref) | copy-start | bytes 196612 | tf_op jit(solution)/shard_map/cond
  27.9 14.2 %copy-start.3 = (bf16[256,128]{1,0:T(8,128)(2,1)S(1)}, bf16[256,128]{1,0:T(8,128)(2,1)}, u32[]{:S(2)}) copy-start(bf16[256,128]{1,0:T(8,128)(2,1)} %constant.106.clone.inv_ref) | copy-start | bytes 196612
  27.9 9.4 %collective-permute-start.6 = (bf16[896,128]{1,0:T(8,128)(2,1)S(1)}, bf16[896,128]{1,0:T(8,128)(2,1)}, u32[]{:S(2)}, u32[]{:S(2)}) collective-permute-start(bf16[896,128]{1,0:T(8,128)(2,1)S(1)} %get-tuple-element.62), channel_id=1, source_target_pairs={{0,4},{4,0},{8,12},{12,8},{16,20},{20,16},{24,28},{28,24},{1,5},{5... | collective-permute-start | bytes 688136 | tf_op jit(solution)/shard_map/cond/branch_1_fun/ppermute | solution.py:414
  28.0 9.4 %collective-permute-start.7 = (bf16[896,128]{1,0:T(8,128)(2,1)}, bf16[896,128]{1,0:T(8,128)(2,1)}, u32[]{:S(2)}, u32[]{:S(2)}) collective-permute-start(bf16[896,128]{1,0:T(8,128)(2,1)} %get-tuple-element.63), channel_id=1, source_target_pairs={{0,4},{4,0},{8,12},{12,8},{16,20},{20,16},{24,28},{28,24},{1,5},{5... | collective-permute-start | bytes 688136 | tf_op jit(solution)/shard_map/cond/branch_1_fun/ppermute | solution.py:414
  28.5 6.8 %collective-permute-start.5 = (f32[4,16,128]{2,1,0:T(8,128)S(1)}, f32[4,16,128]{2,1,0:T(8,128)}, u32[]{:S(2)}, u32[]{:S(2)}) collective-permute-start(f32[4,16,128]{2,1,0:T(8,128)S(1)} %get-tuple-element.58), channel_id=1, source_target_pairs={{0,3},{1,2},{2,1},{3,0},{4,7},{5,6},{6,5},{7,4},{8,11},{9,10},{10,... | collective-permute-start | bytes 98312 | tf_op jit(solution)/shard_map/cond/branch_1_fun/ppermute | solution.py:414
  30.1 5.6 %collective-permute-start.4 = (f32[4,16,128]{2,1,0:T(8,128)S(1)}, f32[4,16,128]{2,1,0:T(8,128)}, u32[]{:S(2)}, u32[]{:S(2)}) collective-permute-start(f32[4,16,128]{2,1,0:T(8,128)S(1)} %get-tuple-element.58), channel_id=1, source_target_pairs={{0,2},{1,3},{2,0},{3,1},{4,6},{5,7},{6,4},{7,5},{8,10},{9,11},{10,... | collective-permute-start | bytes 98312 | tf_op jit(solution)/shard_map/cond/branch_1_fun/ppermute | solution.py:414
  33.3 4.0 %collective-permute-start.3 = (f32[4,16,128]{2,1,0:T(8,128)S(1)}, f32[4,16,128]{2,1,0:T(8,128)}, u32[]{:S(2)}, u32[]{:S(2)}) collective-permute-start(f32[4,16,128]{2,1,0:T(8,128)S(1)} %get-tuple-element.58), channel_id=1, source_target_pairs={{0,1},{1,0},{2,3},{3,2},{4,5},{5,4},{6,7},{7,6},{8,9},{9,8},{10,11... | collective-permute-start | bytes 98312 | tf_op jit(solution)/shard_map/cond/branch_1_fun/ppermute | solution.py:414
  37.3 24.7 %collective-permute-start.19 = (bf16[2048,128]{1,0:T(8,128)(2,1)}, bf16[2048,128]{1,0:T(8,128)(2,1)S(1)}, u32[]{:S(2)}, u32[]{:S(2)}) collective-permute-start(bf16[2048,128]{1,0:T(8,128)(2,1)} %get-tuple-element.153), channel_id=1, source_target_pairs={{0,2},{1,3},{2,0},{3,1},{4,6},{5,7},{6,4},{7,5},{8,10},{9,11},{10,... | collective-permute-start | bytes 1572872 | tf_op jit(solution)/shard_map/ppermute | solution.py:464
  38.4 23.6 %collective-permute-start.20 = (bf16[2048,128]{1,0:T(8,128)(2,1)S(1)}, bf16[2048,128]{1,0:T(8,128)(2,1)S(1)}, u32[]{:S(2)}, u32[]{:S(2)}) collective-permute-start(bf16[2048,128]{1,0:T(8,128)(2,1)S(1)} %get-tuple-element.154), channel_id=1, source_target_pairs={{0,1},{3,2},{4,5},{7,6},{8,9},{11,10},{12,13},{15,14},{16,17},{19,... | collective-permute-start | bytes 1572872 | tf_op jit(solution)/shard_map/ppermute | solution.py:465
  42.0 11.3 %copy-start = (bf16[256,128]{1,0:T(8,128)(2,1)S(1)}, bf16[256,128]{1,0:T(8,128)(2,1)}, u32[]{:S(2)}) copy-start(bf16[256,128]{1,0:T(8,128)(2,1)} %constant.107.clone.fwd_ref) | copy-start | bytes 196612
  42.1 0.6 copy-start.4
  42.1 3.3 %collective-permute-start.9 = (bf16[896,128]{1,0:T(8,128)(2,1)}, bf16[896,128]{1,0:T(8,128)(2,1)}, u32[]{:S(2)}, u32[]{:S(2)}) collective-permute-start(bf16[896,128]{1,0:T(8,128)(2,1)} %get-tuple-element.68.refs_2_), channel_id=1, source_target_pairs={{0,4},{4,0},{8,12},{12,8},{16,20},{20,16},{24,28},{28,24},{1,5},{5... | collective-permute-start | bytes 688136 | tf_op jit(solution)/shard_map/cond/branch_1_fun/ppermute | solution.py:414
  42.1 3.2 %collective-permute-start.10 = (bf16[896,128]{1,0:T(8,128)(2,1)}, bf16[896,128]{1,0:T(8,128)(2,1)}, u32[]{:S(2)}, u32[]{:S(2)}) collective-permute-start(bf16[896,128]{1,0:T(8,128)(2,1)} %get-tuple-element.69.refs_3_), channel_id=1, source_target_pairs={{0,4},{4,0},{8,12},{12,8},{16,20},{20,16},{24,28},{28,24},{1,5},{5... | collective-permute-start | bytes 688136 | tf_op jit(solution)/shard_map/cond/branch_1_fun/ppermute | solution.py:414
  43.5 1.2 %collective-permute-start.8 = (bf16[1,4,16,128]{3,2,1,0:T(8,128)(2,1)S(1)}, bf16[1,4,16,128]{3,2,1,0:T(8,128)(2,1)S(1)}, u32[]{:S(2)}, u32[]{:S(2)}) collective-permute-start(bf16[1,4,16,128]{3,2,1,0:T(8,128)(2,1)S(1)} %get-tuple-element.166), channel_id=1, source_target_pairs={{0,4},{4,0},{8,12},{12,8},{16,20},{20,16},{24,28},{28,24},{1,5},{5... | collective-permute-start | bytes 49160 | tf_op jit(solution)/shard_map/cond/branch_1_fun/ppermute | solution.py:414
  45.4 8.0 %collective-permute-start.13 = (bf16[2,4,16,128]{3,2,1,0:T(8,128)(2,1)}, bf16[2,4,16,128]{3,2,1,0:T(8,128)(2,1)}, u32[]{:S(2)}, u32[]{:S(2)}) collective-permute-start(bf16[2,4,16,128]{3,2,1,0:T(8,128)(2,1)} %pad_maximum_fusion), channel_id=1, source_target_pairs={{0,24},{4,28},{8,16},{12,20},{16,8},{20,12},{24,0},{28,4},{1,25},{... | collective-permute-start | bytes 98312 | tf_op jit(solution)/shard_map/cond/branch_1_fun/ppermute | solution.py:414
  47.7 5.7 %collective-permute-start.12 = (bf16[2,4,16,128]{3,2,1,0:T(8,128)(2,1)}, bf16[2,4,16,128]{3,2,1,0:T(8,128)(2,1)}, u32[]{:S(2)}, u32[]{:S(2)}) collective-permute-start(bf16[2,4,16,128]{3,2,1,0:T(8,128)(2,1)} %pad_maximum_fusion), channel_id=1, source_target_pairs={{0,8},{4,12},{8,0},{12,4},{16,24},{20,28},{24,16},{28,20},{1,9},{5... | collective-permute-start | bytes 98312 | tf_op jit(solution)/shard_map/cond/branch_1_fun/ppermute | solution.py:414
  48.2 5.1 %collective-permute-start.11 = (bf16[2,4,16,128]{3,2,1,0:T(8,128)(2,1)}, bf16[2,4,16,128]{3,2,1,0:T(8,128)(2,1)}, u32[]{:S(2)}, u32[]{:S(2)}) collective-permute-start(bf16[2,4,16,128]{3,2,1,0:T(8,128)(2,1)} %pad_maximum_fusion), channel_id=1, source_target_pairs={{0,16},{4,20},{8,24},{12,28},{16,0},{20,4},{24,8},{28,12},{1,17},{... | collective-permute-start | bytes 98312 | tf_op jit(solution)/shard_map/cond/branch_1_fun/ppermute | solution.py:414
  53.4 8.6 %copy-start.2 = (f32[1,2048,128]{2,1,0:T(8,128)S(1)}, f32[1,2048,128]{2,1,0:T(8,128)}, u32[]{:S(2)}) copy-start(f32[1,2048,128]{2,1,0:T(8,128)} %param.17) | copy-start | bytes 3145732
